TPU v7x, 256 devices: a whole 4x4x8 slice. The times are simulated.
256 devices in a mesh: pair: 32 (over x, z), tile: 8 (over y, core).
Axes of the slice: x: 4, y: 4, z: 8, core: 2. Of those that a mesh axis runs over, the one named last changes fastest.
Arguments:
- valence_waves: bfloat16 [32, 96, 9216], P('pair', 'tile'), may hold values from -6 to 6
- cond_waves: bfloat16 [64, 96, 9216], P('pair', 'tile'), may hold values from -6 to 6
- valence_energy: float32 [128], replicated, may hold values from -16 to -1
- conduction_energy: float32 [256], replicated, may hold values from 0.5 to 12
- valence_pick: int32 [32], replicated, may hold values from 0 to 127, as said below
- cond_pick: int32 [64], replicated, may hold values from 0 to 255, as said below
- cond_slot: int32 [64], replicated, may hold values from 0 to 63, each once
- g_index: int32 [12000], replicated, may hold values from 0 to 52021, as said below
Outputs:
- chi0: float32 [12000, 12000], P('pair', 'tile')
Inputs may be any that keep to these rules, and one draw needn't show every extreme that they name: `valence_pick`: distinct levels. `cond_pick`: distinct levels. `cond_slot`: each slot once. `g_index`: distinct positions in the flattened spectrum of 2 x (37) x (37) x (19) entries.
All inputs are finite; a program needn't handle non-finite values.
Results may differ from a plain program's by a relative error of at most 0.019.
Values may be sent and summed in bfloat16 or wider, within the bound.
No kernel may reach another device: no remote copies, remote signals or barrier semaphores. Data moves between devices by JAX's collectives and lax.ppermute only.
A program may use at most 192 MiB of HBM per device.

v0:
```python
import functools
import math

import jax
import jax.numpy as jnp
import ml_dtypes
import numpy as np
from jax import lax
from jax.experimental import pallas as pl
from jax.experimental.pallas import tpu as pltpu
from jax.sharding import Mesh, PartitionSpec as P

NV = 32
NC = 64
GRID = 96
KM = 18
NG = 12000
KEPT = 2 * KM + 1
HALF = KM + 1
NX, NZ, NY, NCORE = 4, 8, 4, 2
NT = NY * NCORE
SLAB = GRID // NT
VB = 8
SB = 8
VC = 4
QC = 4
SLOTS = ((0, 1, 7, 2), (6, 3, 5, 4))
ROWS = SLAB * VC * SB
ZOUT = HALF * 16
YSTEP = 768
NSTEP = GRID * GRID // YSTEP
BTILE = 128
NBT = 5
KWIN = 5
YL = 1408
AEI = 2 * KEPT
RB = 384
GP = 32 * RB
GCH = 768
CODES = 256
NGRP = 3
BF = jnp.bfloat16
F32 = jnp.float32


def tables():
    pos = np.arange(GRID)
    scale = 1.0 / math.sqrt(GRID)

    def angles(freqs):
        turns = (np.mod(freqs, GRID)[None, :] * pos[:, None]) % GRID
        return turns.astype(np.float64) * (2.0 * math.pi / GRID)

    ad = angles(np.arange(HALF))
    depth = np.stack([np.cos(ad), -np.sin(ad)], axis=1) * scale
    ap = angles(np.arange(KEPT) - KM)
    c, s = np.cos(ap), np.sin(ap)
    plane = np.stack([np.stack([c, s]), np.stack([-s, c])], axis=2) * scale
    return depth, plane


def depth_block():
    depth, _ = tables()
    out = np.zeros((2, 4, GRID, HALF, 2, 2, 4), np.float64)
    for h in range(2):
        for y in range(4):
            out[h, y, :, :, h, :, y] = depth.transpose(0, 2, 1)
    return out.reshape(YSTEP, ZOUT).astype(ml_dtypes.bfloat16)


def window(n):
    return min((BTILE * n) // KEPT, HALF - KWIN)


def plane_block():
    _, plane = tables()
    perk = plane.reshape(2, GRID // 4, 4, 2, KEPT).transpose(3, 4, 1, 0, 2).reshape(2, KEPT, 2 * GRID)
    out = np.zeros((YL, KWIN, 2 * GRID), np.float64)
    for d in range(2):
        for b in range(KEPT * HALF):
            k, j = divmod(b, KEPT)
            n, r = divmod(b, BTILE)
            row = n * 2 * BTILE + d * (BTILE if n < NBT else 64) + r
            out[row, k - window(n)] = perk[d, j]
    return out.reshape(YL, KWIN * 2 * GRID).astype(ml_dtypes.bfloat16)


def kron_block():
    _, plane = tables()
    out = np.zeros((2, 2, AEI, SB, NT, QC, SLAB), np.float64)
    for c in range(2):
        for q in range(QC):
            out[c, :, :, c * QC + q, :, q, :] = plane.reshape(2, NT, SLAB, AEI).transpose(0, 3, 1, 2)
    return out.reshape(2, 2, AEI * SB, GRID * QC).astype(ml_dtypes.bfloat16)


def copy_in(refs, spaces, sems):
    copies = [pltpu.make_async_copy(ref, space, sems.at[i]) for i, (ref, space) in enumerate(zip(refs, spaces))]
    for copy in copies:
        copy.start()
    return copies


def spectra_kernel(*refs):
    n = VC + NX + 3
    o_ref, wide, dens, zs, sems = refs[n], *refs[2 * n + 1 :]
    spaces = refs[n + 1 : 2 * n + 1]
    copies = copy_in(refs[:n], spaces, sems)
    v_refs, c_refs, (t_ref, w_ref) = spaces[:VC], spaces[VC : n - 2], spaces[n - 2 :]
    for copy in copies[:-1]:
        copy.wait()

    def body(step, _):
        lanes = pl.ds(pl.multiple_of(step * YSTEP, YSTEP), YSTEP)

        def stack(slot, pieces):
            for i, (ref, b) in enumerate(pieces):
                wide[slot, i * SLAB : (i + 1) * SLAB, :] = ref[b, :, lanes].astype(F32)
            return wide[slot].astype(BF)

        bands = [(c_refs[m], b) for m in range(3) for b in range(2)] + [(c_refs[3], 0), (c_refs[4], 0)]
        cond = [stack(h, bands[QC * h : QC * (h + 1)]) for h in range(2)]
        for v in range(VC):
            val = stack(2 + v, [(v_refs[v], 0)] * QC)
            for h in range(2):
                r0 = (v * 2 + h) * SLAB * QC
                dens[r0 : r0 + SLAB * QC, :] = val * cond[h]
        z = jnp.dot(dens[...], t_ref[...], preferred_element_type=F32).astype(BF)
        zs[:, pl.ds(pl.multiple_of(step * 16, 16), 16), :] = z.T.reshape(HALF, 16, ROWS)
        return 0

    lax.fori_loop(0, NSTEP, body, 0)
    copies[-1].wait()
    for n in range(NBT + 1):
        r0 = n * 2 * BTILE
        rows = 2 * BTILE if n < NBT else BTILE
        k0 = window(n)
        zk = zs[k0 : k0 + KWIN].reshape(KWIN * 2 * GRID, ROWS)
        y = jnp.dot(w_ref[r0 : r0 + rows, :], zk, preferred_element_type=F32)
        yt = y.astype(BF).T.reshape(NT, SLAB * QC, rows)
        if n < NBT - 1:
            l0 = n // 2 * 512 + n % 2 * BTILE
            o_ref[:, :, l0 : l0 + BTILE] = yt[:, :, :BTILE]
            o_ref[:, :, l0 + 256 : l0 + 256 + BTILE] = yt[:, :, BTILE:]
        else:
            o_ref[:, :, r0 : r0 + rows] = yt


def spectra(vs, cs, t, w):
    operands = [*vs, *cs, t, w]
    return pl.pallas_call(
        spectra_kernel,
        in_specs=[pl.BlockSpec(memory_space=pl.ANY)] * len(operands),
        out_specs=pl.BlockSpec(memory_space=pltpu.VMEM),
        out_shape=jax.ShapeDtypeStruct((NT, SLAB * QC, YL), BF),
        scratch_shapes=[pltpu.VMEM(x.shape, BF) for x in operands]
        + [
            pltpu.VMEM((2 + VC, QC * SLAB, YSTEP), F32),
            pltpu.VMEM((ROWS, YSTEP), BF),
            pltpu.VMEM((HALF, 2 * GRID, ROWS), BF),
            pltpu.SemaphoreType.DMA((len(operands),)),
        ],
        compiler_params=pltpu.CompilerParams(vmem_limit_bytes=40 * 2**20),
        name="spectra",
    )(*operands)


def lines_kernel(y0_ref, y1_ref, m_ref, s_ref):
    rows = AEI * SB

    def line(d, lanes):
        parts = [
            jnp.dot(m_ref[c, d], ref[:, lanes], preferred_element_type=F32) for c, ref in ((0, y0_ref), (1, y1_ref))
        ]
        return parts[0] + parts[1]

    for g in range(2):
        s = line(0, pl.ds(512 * g, 256)) + line(1, pl.ds(512 * g + 256, 256))
        s_ref[g * rows : (g + 1) * rows, :] = s.astype(BF)
    s = line(0, pl.ds(1024, BTILE)) + line(1, pl.ds(1024 + BTILE, BTILE))
    s_ref[2 * rows :, :BTILE] = s.astype(BF)
    last = pl.ds(1024 + 2 * BTILE, BTILE)
    s = line(0, last) + pltpu.roll(line(1, last), 64, 1)
    s_ref[2 * rows :, BTILE:] = s.astype(BF)


def lines(y0, y1, m):
    return pl.pallas_call(
        lines_kernel,
        out_shape=jax.ShapeDtypeStruct((NGRP * AEI * SB, CODES), BF),
        compiler_params=pltpu.CompilerParams(vmem_limit_bytes=40 * 2**20),
        name="lines",
    )(y0, y1, m)


def pick_kernel(s_ref, a_ref, b_ref, oc_ref, or_ref):
    codes = lax.broadcasted_iota(jnp.int32, (CODES, CODES), 0)
    outs = []
    for g in range(GCH // CODES):
        lanes = pl.ds(g * CODES, CODES)
        chosen = (codes == b_ref[:, lanes]).astype(F32).astype(BF)
        r = jnp.dot(s_ref[...], chosen, preferred_element_type=F32)
        code = jnp.broadcast_to(a_ref[:, lanes], (SB, CODES))
        acc = jnp.zeros((SB, CODES), F32)
        for a in range(NGRP * AEI):
            acc = jnp.where(code == a, r[a * SB : (a + 1) * SB], acc)
        outs.append(acc.astype(BF))
    out = jnp.concatenate(outs, axis=1)
    oc_ref[0] = out
    for h in range(GCH // RB):
        or_ref[h] = out[:, h * RB : (h + 1) * RB]


def pick(s, a, b):
    per = 4 * RB // GCH
    return pl.pallas_call(
        pick_kernel,
        grid=(GP // GCH,),
        in_specs=[
            pl.BlockSpec((NGRP * AEI * SB, CODES), lambda i: (0, 0)),
            pl.BlockSpec((1, GCH), lambda i: (0, i)),
            pl.BlockSpec((1, GCH), lambda i: (0, i)),
        ],
        out_specs=[
            pl.BlockSpec((1, SB, GCH), lambda i: (i // per, 0, i % per)),
            pl.BlockSpec((GCH // RB, SB, RB), lambda i: (i, 0, 0)),
        ],
        out_shape=[
            jax.ShapeDtypeStruct((NT, SB, 4 * RB), BF),
            jax.ShapeDtypeStruct((32, SB, RB), BF),
        ],
        compiler_params=pltpu.CompilerParams(vmem_limit_bytes=40 * 2**20),
        name="pick",
    )(s, a, b)


KP = NT * SB
LA = 512
XORDER = (0, 1, 3, 2)
ZORDER = (0, 1, 2, 3, 7, 6, 5, 4)


def a_pieces():
    whole = [[(x, z) for x in XORDER] for z in ZORDER[:-1]]
    return whole + [[(x, 4) for x in XORDER[:2]], [(x, 4) for x in XORDER[2:]]]


def b_pieces():
    whole = [[(x, z) for z in range(NZ)] for x in XORDER[:-1]]
    return whole + [[(2, z) for z in range(NZ // 2)], [(2, z) for z in range(NZ // 2, NZ)]]


def product_kernel(xz_ref, w_ref, *refs):
    na, nb = len(a_pieces()), len(b_pieces())
    n = 1 + na + nb
    o_ref, spaces, (wr, acc_ref, sems) = refs[n], refs[n + 1 : 2 * n + 1], refs[2 * n + 1 :]
    copies = copy_in(refs[:n], spaces, sems)
    r_ref, a_refs, b_refs = spaces[0], spaces[1 : 1 + na], spaces[1 + na :]
    copies[0].wait()
    for p in range(32):
        rows = jnp.concatenate([r_ref[t, p].astype(F32) for t in range(NT)], axis=0)
        wr[p] = (rows * w_ref[KP * p : KP * (p + 1), :]).astype(BF)
    for copy in copies[1:]:
        copy.wait()

    def part(pieces, ref, z_of):
        lhs = [wr[lax.rem(xz_ref[0] + (NX - dx), NX) * NZ + z_of(dz)] for dx, dz in pieces]
        return lax.dot_general(
            jnp.concatenate(lhs, axis=0), ref[...], (((0,), (0,)), ((), ())), preferred_element_type=F32
        )

    def total(pieces, operands, z_of):
        acc = part(pieces[0], operands[0], z_of)
        for piece, ref in zip(pieces[1:], operands[1:]):
            acc += part(piece, ref, z_of)
        return acc

    acc_ref[:, :LA] = total(a_pieces(), a_refs, lambda dz: lax.rem(xz_ref[1] + (NZ - dz), NZ))
    acc_ref[:, LA:] = total(b_pieces(), b_refs, lambda z: z)
    for q in range(4):
        o_ref[:, 375 * q : 375 * (q + 1)] = acc_ref[:375, RB * q : RB * q + 375]


def product(place, rows, weight, a_cols, b_cols):
    operands = [rows, *a_cols, *b_cols]
    vmem = pl.BlockSpec(memory_space=pltpu.VMEM)
    return pl.pallas_call(
        product_kernel,
        in_specs=[pl.BlockSpec(memory_space=pltpu.SMEM), vmem] + [pl.BlockSpec(memory_space=pl.ANY)] * len(operands),
        out_specs=vmem,
        out_shape=jax.ShapeDtypeStruct((375, 1500), F32),
        scratch_shapes=[pltpu.VMEM(x.shape, BF) for x in operands]
        + [
            pltpu.VMEM((32, KP, RB), BF),
            pltpu.VMEM((RB, 4 * RB), F32),
            pltpu.SemaphoreType.DMA((len(operands),)),
        ],
        compiler_params=pltpu.CompilerParams(vmem_limit_bytes=48 * 2**20),
        name="product",
    )(place, weight, *operands)


def ring(value, axis, size):
    out_up, out_down = [value], [value]
    for _ in range(size // 2 - 1):
        out_up.append(shift(out_up[-1], axis, size, 1))
        out_down.append(shift(out_down[-1], axis, size, -1))
    half = value.shape[0] // 2
    far = [shift(out_up[-1][:half], axis, size, 1), shift(out_down[-1][half:], axis, size, -1)]
    return out_up + out_down[1:], far


def pick_levels(picks, table):
    codes = jnp.arange(table.shape[0], dtype=jnp.int32)
    return jnp.sum(jnp.where(picks[:, None] == codes[None, :], table[None, :], 0.0), axis=1)


def spread(levels, places):
    codes = jnp.arange(levels.shape[0], dtype=jnp.int32)[None, :]
    return jnp.sum(jnp.where(codes == places.astype(np.int32), levels[None, :], 0.0), axis=1, keepdims=True)


def shift(value, axis, size, step):
    return lax.ppermute(value, axis, [(i, (i + step) % size) for i in range(size)])


def per_device(
    valence_waves,
    cond_waves,
    valence_energy,
    conduction_energy,
    valence_pick,
    cond_pick,
    cond_slot,
    g_index,
):
    cs, far = ring(cond_waves, "x", NX)
    cs += far
    depth, plane, kron = jnp.asarray(depth_block()), jnp.asarray(plane_block()), jnp.asarray(kron_block())
    tile = ("y", "core")
    vs = [valence_waves] + [None] * (VB - 1)
    specs = []
    for m in range(1, VB // 2 + 1):
        if m == VB // 2:
            specs.append(spectra([vs[k] for k in SLOTS[0]], cs, depth, plane))
        vs[m] = shift(vs[m - 1], "z", NZ, 1)
        if m < VB // 2:
            vs[VB - m] = shift(vs[(VB - m + 1) % VB], "z", NZ, -1)
    specs.append(spectra([vs[k] for k in SLOTS[1]], cs, depth, plane))
    slabs = [lax.all_to_all(spec, tile, split_axis=0, concat_axis=0, tiled=True) for spec in specs]

    valence_level = pick_levels(valence_pick, valence_energy)
    band_level = pick_levels(cond_pick, conduction_energy)
    slot_codes = jnp.arange(NC, dtype=jnp.int32)
    slot_level = jnp.sum(
        jnp.where(cond_slot[:, None] == slot_codes[None, :], band_level[:, None], 0.0), axis=0
    )
    factor = 4.0 / math.sqrt(NV * NC)
    xs, zs, ts, c, ms, bs = np.ix_(*(np.arange(n) for n in (NX, NZ, NT, 2, 2, 2)))
    v_of = VB * xs + (zs - np.array(SLOTS)[c, ts // 2]) % NZ
    s_of = 2 * NZ * ((xs - np.array(XORDER)[2 * (ts % 2) + ms]) % NX) + 2 * zs + bs
    v_of, s_of = (np.broadcast_to(m, (NX, NZ, NT, 2, 2, 2)).reshape(NV * NC, 1) for m in (v_of, s_of))
    weight = factor / (spread(valence_level, v_of) - spread(slot_level, s_of))

    index = jnp.pad(g_index.reshape(32, 375), ((0, 0), (0, RB - 375))).reshape(1, GP)
    a_code = index // (KEPT * HALF)
    rest = index % (KEPT * HALF)
    b_code = (rest % HALF) * KEPT + rest // HALF
    a_code = a_code + AEI * (b_code // CODES)
    b_code = b_code % CODES

    combined = lines(slabs[0].reshape(GRID * QC, YL), slabs[1].reshape(GRID * QC, YL), kron)
    cols, for_rows = pick(combined, a_code, b_code)
    cols = lax.all_to_all(cols, tile, split_axis=0, concat_axis=0, tiled=True).reshape(KP, 4 * RB)
    b_bundle = lax.all_gather(cols[:, LA:], "z", axis=0, tiled=True)
    near, far = ring(cols[:, :LA], "x", NX)
    for_rows, near[1] = lax.optimization_barrier((for_rows, near[1]))
    a_cols, a_far = ring(jnp.concatenate(near + far, axis=0), "z", NZ)
    b_cols, b_far = ring(b_bundle, "x", NX)
    rows = lax.all_to_all(for_rows, ("x", "z"), split_axis=0, concat_axis=0, tiled=True)
    rows = lax.all_gather(rows, ("y", "core"), axis=0, tiled=False)
    place = jnp.stack([lax.axis_index("x"), lax.axis_index("z")]).astype(jnp.int32)
    return product(place, rows, weight, a_cols + a_far, b_cols + b_far)


def solution(mesh):
    fine = Mesh(mesh.devices.reshape(NX, NZ, NY, NCORE), ("x", "z", "y", "core"))
    waves = P(("x", "z"), ("y", "core"), None)
    return jax.shard_map(
        per_device,
        mesh=fine,
        in_specs=(waves, waves, P(), P(), P(), P(), P(), P()),
        out_specs=P(("x", "z"), ("y", "core")),
        check_vma=False,
    )
```

profile of v0, /device:TPU:6, one launch (start us, length us, event | category | flops | bytes accessed | tf_op | source)
XLA Modules:
  0.0 229.2 jit_solution(17943121519041192189)
XLA Ops:
  10.5 3.9 %collective-permute-start.1 = (bf16[1,12,9216]{2,1,0:T(8,128)(2,1)}, bf16[1,12,9216]{2,1,0:T(8,128)(2,1)}, u32[]{:S(2)}, u32[]{:S(2)}) collective-permute-start(bf16[1,12,9216]{2,1,0:T(8,128)(2,1)} %refs_0_.1), channel_id=1, source_target_pairs={{0,56},{8,0},{16,8},{24,16},{32,24},{40,32},{48,40},{56,48},{1,57}... | collective-permute-start | bytes 663560 | tf_op jit(solution)/shard_map/ppermute | solution.py:324
  14.4 6.7 %collective-permute-done.refs_1_ = bf16[1,12,9216]{2,1,0:T(8,128)(2,1)S(1)} collective-permute-done((bf16[1,12,9216]{2,1,0:T(8,128)(2,1)}, bf16[1,12,9216]{2,1,0:T(8,128)(2,1)S(1)}, u32[]{:S(2)}, u32[]{:S(2)}) %collective-permute-start) | collective-permute-done | bytes 221216 | tf_op jit(solution)/shard_map/ppermute | solution.py:324
  21.1 3.2 %collective-permute-start.7 = (bf16[1,12,9216]{2,1,0:T(8,128)(2,1)}, bf16[1,12,9216]{2,1,0:T(8,128)(2,1)}, u32[]{:S(2)}, u32[]{:S(2)}) collective-permute-start(bf16[1,12,9216]{2,1,0:T(8,128)(2,1)} %collective-permute-done.1.refs_2_), channel_id=1, source_target_pairs={{0,56},{8,0},{16,8},{24,16},{32,24},{40,32},{48,40},{56,48},{1,57}... | collective-permute-start | bytes 663560 | tf_op jit(solution)/shard_map/ppermute | solution.py:324
  33.1 3.2 %collective-permute-start.9 = (bf16[1,12,9216]{2,1,0:T(8,128)(2,1)}, bf16[1,12,9216]{2,1,0:T(8,128)(2,1)}, u32[]{:S(2)}, u32[]{:S(2)}) collective-permute-start(bf16[1,12,9216]{2,1,0:T(8,128)(2,1)} %collective-permute-done.7.refs_0_), channel_id=1, source_target_pairs={{0,56},{8,0},{16,8},{24,16},{32,24},{40,32},{48,40},{56,48},{1,57}... | collective-permute-start | bytes 663560 | tf_op jit(solution)/shard_map/ppermute | solution.py:324
  41.9 9.9 %spectra.2 = bf16[8,48,1408]{2,1,0:T(8,128)(2,1)S(1)} custom-call(bf16[1,12,9216]{2,1,0:T(8,128)(2,1)S(1)} %copy-done.12, bf16[1,12,9216]{2,1,0:T(8,128)(2,1)S(1)} %copy-done.14, bf16[1,12,9216]{2,1,0:T(8,128)(2,1)} %collective-permute-done.1.refs_2_, bf16[1,12,9216]{2,1,0:T(8,128)(2,1)} %collective-permute-done.2.refs_3_, ...), custom_call_target="tpu_custom_call" | custom-call | tf_op jit(solution)/shard_map/spectra/pallas_call | solution.py:151
  52.7 4.5 %all-to-all-start = ((bf16[8,48,1408]{2,1,0:T(8,128)(2,1)}), bf16[8,48,1408]{2,1,0:T(8,128)(2,1)}, u32[]{:S(2)}, u32[]{:S(2)}) async-start(bf16[8,48,1408]{2,1,0:T(8,128)(2,1)} %copy-done.6), calls=%async_computation | async-start | bytes 2162688 | tf_op jit(solution)/shard_map/all_to_all | solution.py:350
  62.5 5.6 %collective-permute-done.10.refs_3_ = bf16[1,12,9216]{2,1,0:T(8,128)(2,1)S(1)} collective-permute-done((bf16[1,12,9216]{2,1,0:T(8,128)(2,1)}, bf16[1,12,9216]{2,1,0:T(8,128)(2,1)S(1)}, u32[]{:S(2)}, u32[]{:S(2)}) %collective-permute-start.10) | collective-permute-done | bytes 221216 | tf_op jit(solution)/shard_map/ppermute | solution.py:324
  71.3 9.9 %spectra.3 = bf16[8,48,1408]{2,1,0:T(8,128)(2,1)S(1)} custom-call(bf16[1,12,9216]{2,1,0:T(8,128)(2,1)} %collective-permute-done.7.refs_0_, bf16[1,12,9216]{2,1,0:T(8,128)(2,1)} %collective-permute-done.8.refs_1_, bf16[1,12,9216]{2,1,0:T(8,128)(2,1)} %collective-permute-done.9.refs_2_, bf16[1,12,9216]{2,1,0:T(8,128)(2,1)S(1)} %collective-permute-done.10.refs_3_, ...), custom_call_target="tpu_custom_call" | custom-call | tf_op jit(solution)/shard_map/spectra/pallas_call | solution.py:151
  82.2 4.6 %all-to-all-start.1 = ((bf16[8,48,1408]{2,1,0:T(8,128)(2,1)}), bf16[8,48,1408]{2,1,0:T(8,128)(2,1)S(1)}, u32[]{:S(2)}, u32[]{:S(2)}) async-start(bf16[8,48,1408]{2,1,0:T(8,128)(2,1)} %copy-done.7), calls=%async_computation.1 | async-start | bytes 2162688 | tf_op jit(solution)/shard_map/all_to_all | solution.py:350
  87.2 15.9 %all-to-all-done.1 = bf16[8,48,1408]{2,1,0:T(8,128)(2,1)S(1)} async-done(((bf16[8,48,1408]{2,1,0:T(8,128)(2,1)}), bf16[8,48,1408]{2,1,0:T(8,128)(2,1)S(1)}, u32[]{:S(2)}, u32[]{:S(2)}) %all-to-all-start.1) | async-done | bytes 1081376 | tf_op jit(solution)/shard_map/all_to_all | solution.py:350
  103.1 4.0 %lines.1.s_ref = bf16[1776,256]{1,0:T(8,128)(2,1)S(1)} custom-call(bf16[384,1408]{1,0:T(8,128)(2,1)} %bitcast.3.y0_ref, bf16[384,1408]{1,0:T(8,128)(2,1)S(1)} %bitcast.19, bf16[2,2,592,384]{3,2,1,0:T(8,128)(2,1)S(1)} %copy-done.10), custom_call_target="tpu_custom_call" | custom-call | tf_op jit(solution)/shard_map/lines/pallas_call | solution.py:188
  107.1 14.4 %pick.1 = (bf16[8,8,1536]{2,1,0:T(8,128)(2,1)S(1)}, bf16[32,8,384]{2,1,0:T(8,128)(2,1)S(1)}) custom-call(bf16[1776,256]{1,0:T(8,128)(2,1)S(1)} %lines.1.s_ref, s32[1,12288]{1,0:T(1,128)S(1)} %multiply_add_fusion.a_ref, s32[1,12288]{1,0:T(1,128)S(1)} %get-tuple-element.13.b_ref), custom_call_target="tpu_custom_call" | custom-call | tf_op jit(solution)/shard_map/pick/pallas_call | solution.py:216
  121.6 9.2 %all_to_all.20 = bf16[8,8,1536]{2,1,0:T(8,128)(2,1)S(1)} all-to-all(bf16[8,8,1536]{2,1,0:T(8,128)(2,1)S(1)} %get-tuple-element.10), channel_id=1, replica_groups=mesh['x'=4,'z'=8,'y'=4,'core'=2] {'y','core'}, dimensions={0} | all-to-all | bytes 393216 | tf_op jit(solution)/shard_map/all_to_all | solution.py:374
  135.9 18.5 %all_to_all.21 = bf16[32,8,384]{2,1,0:T(8,128)(2,1)} all-to-all(bf16[32,8,384]{2,1,0:T(8,128)(2,1)S(1)} %get-tuple-element.11), channel_id=1, replica_groups=mesh['x'=4,'z'=8,'y'=4,'core'=2] {'x','z'}, dimensions={0} | all-to-all | bytes 393216 | tf_op jit(solution)/shard_map/all_to_all | solution.py:380
  155.5 4.4 %collective-permute-done.12 = bf16[64,512]{1,0:T(8,128)(2,1)S(1)} collective-permute-done((bf16[64,512]{1,0:T(8,128)(2,1)S(1)}, bf16[64,512]{1,0:T(8,128)(2,1)S(1)}, u32[]{:S(2)}, u32[]{:S(2)}) %collective-permute-start.12) | collective-permute-done | bytes 65568 | tf_op jit(solution)/shard_map/ppermute | solution.py:324
  163.2 5.1 %all-gather.4.cloned.1.call-done.refs_10_ = bf16[512,1024]{1,0:T(8,128)(2,1)} async-done(((bf16[64,1024]{1,0:T(8,128)(2,1)}), bf16[512,1024]{1,0:T(8,128)(2,1)}) %all-gather.4.cloned.1.call-update) | async-done | bytes 1048592 | tf_op jit(solution)/shard_map/all_gather | solution.py:375
  174.5 6.0 %collective-permute-done.18.refs_5_ = bf16[256,512]{1,0:T(8,128)(2,1)S(1)} collective-permute-done((bf16[256,512]{1,0:T(8,128)(2,1)S(1)}, bf16[256,512]{1,0:T(8,128)(2,1)S(1)}, u32[]{:S(2)}, u32[]{:S(2)}) %collective-permute-start.18) | collective-permute-done | bytes 262176 | tf_op jit(solution)/shard_map/ppermute | solution.py:324
  180.5 3.7 %collective-permute-start.19 = (bf16[256,512]{1,0:T(8,128)(2,1)S(1)}, bf16[256,512]{1,0:T(8,128)(2,1)S(1)}, u32[]{:S(2)}, u32[]{:S(2)}) collective-permute-start(bf16[256,512]{1,0:T(8,128)(2,1)S(1)} %collective-permute-done.18.refs_5_), channel_id=1, source_target_pairs={{0,56},{8,0},{16,8},{24,16},{32,24},{40,32},{48,40},{56,48},{1,57}... | collective-permute-start | bytes 786440 | tf_op jit(solution)/shard_map/ppermute | solution.py:324
  186.0 4.7 %collective-permute-done.19.refs_6_ = bf16[256,512]{1,0:T(8,128)(2,1)S(1)} collective-permute-done((bf16[256,512]{1,0:T(8,128)(2,1)S(1)}, bf16[256,512]{1,0:T(8,128)(2,1)S(1)}, u32[]{:S(2)}, u32[]{:S(2)}) %collective-permute-start.19) | collective-permute-done | bytes 262176 | tf_op jit(solution)/shard_map/ppermute | solution.py:324
  190.7 3.7 %collective-permute-start.20 = (bf16[256,512]{1,0:T(8,128)(2,1)S(1)}, bf16[256,512]{1,0:T(8,128)(2,1)S(1)}, u32[]{:S(2)}, u32[]{:S(2)}) collective-permute-start(bf16[256,512]{1,0:T(8,128)(2,1)S(1)} %collective-permute-done.19.refs_6_), channel_id=1, source_target_pairs={{0,56},{8,0},{16,8},{24,16},{32,24},{40,32},{48,40},{56,48},{1,57}... | collective-permute-start | bytes 786440 | tf_op jit(solution)/shard_map/ppermute | solution.py:324
  196.4 3.3 %collective-permute-start.25 = (bf16[256,1024]{1,0:T(8,128)(2,1)}, bf16[256,1024]{1,0:T(8,128)(2,1)}, u32[]{:S(2)}, u32[]{:S(2)}) collective-permute-start(bf16[256,1024]{1,0:T(8,128)(2,1)} %slice.48), channel_id=1, source_target_pairs={{0,64},{64,128},{128,192},{192,0},{1,65},{65,129},{129,193},{193,1... | collective-permute-start | bytes 1572872 | tf_op jit(solution)/shard_map/ppermute | solution.py:324
  200.6 3.4 %collective-permute-start.22 = (bf16[128,512]{1,0:T(8,128)(2,1)}, bf16[128,512]{1,0:T(8,128)(2,1)S(1)}, u32[]{:S(2)}, u32[]{:S(2)}) collective-permute-start(bf16[128,512]{1,0:T(8,128)(2,1)} %slice.46), channel_id=1, source_target_pairs={{0,56},{8,0},{16,8},{24,16},{32,24},{40,32},{48,40},{56,48},{1,57}... | collective-permute-start | bytes 393224 | tf_op jit(solution)/shard_map/ppermute | solution.py:324
  206.8 4.3 %collective-permute-done.21.refs_8_ = bf16[128,512]{1,0:T(8,128)(2,1)} collective-permute-done((bf16[128,512]{1,0:T(8,128)(2,1)}, bf16[128,512]{1,0:T(8,128)(2,1)}, u32[]{:S(2)}, u32[]{:S(2)}) %collective-permute-start.21) | collective-permute-done | bytes 131104 | tf_op jit(solution)/shard_map/ppermute | solution.py:324
  215.0 7.4 %product.1 = f32[375,1500]{1,0:T(8,128)} custom-call(s32[2]{0:T(128)S(1)} %pad_add_fusion.xz_ref, f32[2048,1]{1,0:T(8,128)S(1)} %copy.40.w_ref, bf16[8,32,8,384]{3,2,1,0:T(8,128)(2,1)} %bitcast.20, bf16[256,512]{1,0:T(8,128)(2,1)S(1)} %constant_dynamic-update-slice_fusion.refs_1_, bf16[256,512]{1,0:T(8,128)(2,1)S(1)} %copy-done.18, ...), custom_call_target="tpu_custom_call" | custom-call | tf_op jit(solution)/shard_map/product/pallas_call | solution.py:287
  (156 shorter events, 55.9 us)
Async XLA Ops:
  6.5 17.8 %collective-permute-start.3 = (bf16[2,12,9216]{2,0,1:T(2,128)(2,1)}, bf16[2,12,9216]{2,0,1:T(2,128)(2,1)S(1)}, u32[]{:S(2)}, u32[]{:S(2)}) collective-permute-start(bf16[2,12,9216]{2,0,1:T(2,128)(2,1)} %param.14), channel_id=1, source_target_pairs={{0,64},{64,128},{128,192},{192,0},{1,65},{65,129},{129,193},{193,1... | collective-permute-start | bytes 1327112 | tf_op jit(solution)/shard_map/ppermute | solution.py:324
  8.8 18.1 %collective-permute-start.4 = (bf16[2,12,9216]{2,0,1:T(2,128)(2,1)}, bf16[2,12,9216]{2,0,1:T(2,128)(2,1)S(1)}, u32[]{:S(2)}, u32[]{:S(2)}) collective-permute-start(bf16[2,12,9216]{2,0,1:T(2,128)(2,1)} %param.14), channel_id=1, source_target_pairs={{0,192},{64,0},{128,64},{192,128},{1,193},{65,1},{129,65},{193,129... | collective-permute-start | bytes 1327112 | tf_op jit(solution)/shard_map/ppermute | solution.py:324
  8.8 12.3 %collective-permute-start = (bf16[1,12,9216]{2,1,0:T(8,128)(2,1)}, bf16[1,12,9216]{2,1,0:T(8,128)(2,1)S(1)}, u32[]{:S(2)}, u32[]{:S(2)}) collective-permute-start(bf16[1,12,9216]{2,1,0:T(8,128)(2,1)} %refs_0_.1), channel_id=1, source_target_pairs={{0,8},{8,16},{16,24},{24,32},{32,40},{40,48},{48,56},{56,0},{1,9},... | collective-permute-start | bytes 663560 | tf_op jit(solution)/shard_map/ppermute | solution.py:324
  10.5 10.6 %collective-permute-start.1 = (bf16[1,12,9216]{2,1,0:T(8,128)(2,1)}, bf16[1,12,9216]{2,1,0:T(8,128)(2,1)}, u32[]{:S(2)}, u32[]{:S(2)}) collective-permute-start(bf16[1,12,9216]{2,1,0:T(8,128)(2,1)} %refs_0_.1), channel_id=1, source_target_pairs={{0,56},{8,0},{16,8},{24,16},{32,24},{40,32},{48,40},{56,48},{1,57}... | collective-permute-start | bytes 663560 | tf_op jit(solution)/shard_map/ppermute | solution.py:324
  21.1 12.0 %collective-permute-start.7 = (bf16[1,12,9216]{2,1,0:T(8,128)(2,1)}, bf16[1,12,9216]{2,1,0:T(8,128)(2,1)}, u32[]{:S(2)}, u32[]{:S(2)}) collective-permute-start(bf16[1,12,9216]{2,1,0:T(8,128)(2,1)} %collective-permute-done.1.refs_2_), channel_id=1, source_target_pairs={{0,56},{8,0},{16,8},{24,16},{32,24},{40,32},{48,40},{56,48},{1,57}... | collective-permute-start | bytes 663560 | tf_op jit(solution)/shard_map/ppermute | solution.py:324
  25.2 11.2 %collective-permute-start.5 = (bf16[1,12,9216]{2,1,0:T(8,128)(2,1)}, bf16[1,12,9216]{2,1,0:T(8,128)(2,1)}, u32[]{:S(2)}, u32[]{:S(2)}) collective-permute-start(bf16[1,12,9216]{2,1,0:T(8,128)(2,1)} %slice.40), channel_id=1, source_target_pairs={{0,64},{64,128},{128,192},{192,0},{1,65},{65,129},{129,193},{193,1... | collective-permute-start | bytes 663560 | tf_op jit(solution)/shard_map/ppermute | solution.py:324
  30.0 27.3 %collective-permute-start.8 = (bf16[1,12,9216]{2,1,0:T(8,128)(2,1)}, bf16[1,12,9216]{2,1,0:T(8,128)(2,1)}, u32[]{:S(2)}, u32[]{:S(2)}) collective-permute-start(bf16[1,12,9216]{2,1,0:T(8,128)(2,1)} %collective-permute-done.2.refs_3_), channel_id=1, source_target_pairs={{0,8},{8,16},{16,24},{24,32},{32,40},{40,48},{48,56},{56,0},{1,9},... | collective-permute-start | bytes 663560 | tf_op jit(solution)/shard_map/ppermute | solution.py:324
  33.1 29.4 %collective-permute-start.9 = (bf16[1,12,9216]{2,1,0:T(8,128)(2,1)}, bf16[1,12,9216]{2,1,0:T(8,128)(2,1)}, u32[]{:S(2)}, u32[]{:S(2)}) collective-permute-start(bf16[1,12,9216]{2,1,0:T(8,128)(2,1)} %collective-permute-done.7.refs_0_), channel_id=1, source_target_pairs={{0,56},{8,0},{16,8},{24,16},{32,24},{40,32},{48,40},{56,48},{1,57}... | collective-permute-start | bytes 663560 | tf_op jit(solution)/shard_map/ppermute | solution.py:324
  52.7 29.4 %all-to-all-start = ((bf16[8,48,1408]{2,1,0:T(8,128)(2,1)}), bf16[8,48,1408]{2,1,0:T(8,128)(2,1)}, u32[]{:S(2)}, u32[]{:S(2)}) async-start(bf16[8,48,1408]{2,1,0:T(8,128)(2,1)} %copy-done.6), calls=%async_computation | async-start | bytes 2162688 | tf_op jit(solution)/shard_map/all_to_all | solution.py:350
  57.2 10.8 %collective-permute-start.10 = (bf16[1,12,9216]{2,1,0:T(8,128)(2,1)}, bf16[1,12,9216]{2,1,0:T(8,128)(2,1)S(1)}, u32[]{:S(2)}, u32[]{:S(2)}) collective-permute-start(bf16[1,12,9216]{2,1,0:T(8,128)(2,1)} %collective-permute-done.8.refs_1_), channel_id=1, source_target_pairs={{0,8},{8,16},{16,24},{24,32},{32,40},{40,48},{48,56},{56,0},{1,9},... | collective-permute-start | bytes 663560 | tf_op jit(solution)/shard_map/ppermute | solution.py:324
  82.2 20.9 %all-to-all-start.1 = ((bf16[8,48,1408]{2,1,0:T(8,128)(2,1)}), bf16[8,48,1408]{2,1,0:T(8,128)(2,1)S(1)}, u32[]{:S(2)}, u32[]{:S(2)}) async-start(bf16[8,48,1408]{2,1,0:T(8,128)(2,1)} %copy-done.7), calls=%async_computation.1 | async-start | bytes 2162688 | tf_op jit(solution)/shard_map/all_to_all | solution.py:350
  86.8 81.5 %all-gather.4.cloned.1.call-start = ((), (), s32[]{:S(2)}) async-start(), calls=%async_computation.4 | async-start | bytes 1179648 | tf_op jit(solution)/shard_map/all_gather | solution.py:375
  131.5 79.7 %all-gather.6.cloned.1.call-start = ((), (), s32[]{:S(2)}) async-start(), calls=%async_computation.5 | async-start | bytes 1769472 | tf_op jit(solution)/shard_map/all_gather | solution.py:381
  159.9 11.6 %collective-permute-start.14 = (bf16[32,512]{1,0:T(8,128)(2,1)S(1)}, bf16[32,512]{1,0:T(8,128)(2,1)S(1)}, u32[]{:S(2)}, u32[]{:S(2)}) collective-permute-start(bf16[32,512]{1,0:T(8,128)(2,1)S(1)} %slice.44), channel_id=1, source_target_pairs={{0,192},{64,0},{128,64},{192,128},{1,193},{65,1},{129,65},{193,129... | collective-permute-start | bytes 98312 | tf_op jit(solution)/shard_map/ppermute | solution.py:324
  160.1 11.4 %collective-permute-start.13 = (bf16[32,512]{1,0:T(8,128)(2,1)S(1)}, bf16[32,512]{1,0:T(8,128)(2,1)S(1)}, u32[]{:S(2)}, u32[]{:S(2)}) collective-permute-start(bf16[32,512]{1,0:T(8,128)(2,1)S(1)} %slice.43), channel_id=1, source_target_pairs={{0,64},{64,128},{128,192},{192,0},{1,65},{65,129},{129,193},{193,1... | collective-permute-start | bytes 98312 | tf_op jit(solution)/shard_map/ppermute | solution.py:324
  168.2 26.4 %collective-permute-start.24 = (bf16[512,1024]{1,0:T(8,128)(2,1)}, bf16[512,1024]{1,0:T(8,128)(2,1)S(1)}, u32[]{:S(2)}, u32[]{:S(2)}) collective-permute-start(bf16[512,1024]{1,0:T(8,128)(2,1)} %all-gather.4.cloned.1.call-done.refs_10_), channel_id=1, source_target_pairs={{0,192},{64,0},{128,64},{192,128},{1,193},{65,1},{129,65},{193,129... | collective-permute-start | bytes 3145736 | tf_op jit(solution)/shard_map/ppermute | solution.py:324
  169.1 26.4 %collective-permute-start.23 = (bf16[512,1024]{1,0:T(8,128)(2,1)}, bf16[512,1024]{1,0:T(8,128)(2,1)S(1)}, u32[]{:S(2)}, u32[]{:S(2)}) collective-permute-start(bf16[512,1024]{1,0:T(8,128)(2,1)} %all-gather.4.cloned.1.call-done.refs_10_), channel_id=1, source_target_pairs={{0,64},{64,128},{128,192},{192,0},{1,65},{65,129},{129,193},{193,1... | collective-permute-start | bytes 3145736 | tf_op jit(solution)/shard_map/ppermute | solution.py:324
  174.5 10.4 %collective-permute-start.15 = (bf16[256,512]{1,0:T(8,128)(2,1)S(1)}, bf16[256,512]{1,0:T(8,128)(2,1)S(1)}, u32[]{:S(2)}, u32[]{:S(2)}) collective-permute-start(bf16[256,512]{1,0:T(8,128)(2,1)S(1)} %constant_dynamic-update-slice_fusion.refs_1_), channel_id=1, source_target_pairs={{0,8},{8,16},{16,24},{24,32},{32,40},{40,48},{48,56},{56,0},{1,9},... | collective-permute-start | bytes 786440 | tf_op jit(solution)/shard_map/ppermute | solution.py:324
  180.5 10.2 %collective-permute-start.19 = (bf16[256,512]{1,0:T(8,128)(2,1)S(1)}, bf16[256,512]{1,0:T(8,128)(2,1)S(1)}, u32[]{:S(2)}, u32[]{:S(2)}) collective-permute-start(bf16[256,512]{1,0:T(8,128)(2,1)S(1)} %collective-permute-done.18.refs_5_), channel_id=1, source_target_pairs={{0,56},{8,0},{16,8},{24,16},{32,24},{40,32},{48,40},{56,48},{1,57}... | collective-permute-start | bytes 786440 | tf_op jit(solution)/shard_map/ppermute | solution.py:324
  184.9 9.5 %collective-permute-start.16 = (bf16[256,512]{1,0:T(8,128)(2,1)S(1)}, bf16[256,512]{1,0:T(8,128)(2,1)S(1)}, u32[]{:S(2)}, u32[]{:S(2)}) collective-permute-start(bf16[256,512]{1,0:T(8,128)(2,1)S(1)} %collective-permute-done.15.refs_2_), channel_id=1, source_target_pairs={{0,8},{8,16},{16,24},{24,32},{32,40},{40,48},{48,56},{56,0},{1,9},... | collective-permute-start | bytes 786440 | tf_op jit(solution)/shard_map/ppermute | solution.py:324
  190.7 9.2 %collective-permute-start.20 = (bf16[256,512]{1,0:T(8,128)(2,1)S(1)}, bf16[256,512]{1,0:T(8,128)(2,1)S(1)}, u32[]{:S(2)}, u32[]{:S(2)}) collective-permute-start(bf16[256,512]{1,0:T(8,128)(2,1)S(1)} %collective-permute-done.19.refs_6_), channel_id=1, source_target_pairs={{0,56},{8,0},{16,8},{24,16},{32,24},{40,32},{48,40},{56,48},{1,57}... | collective-permute-start | bytes 786440 | tf_op jit(solution)/shard_map/ppermute | solution.py:324
  194.4 9.6 %collective-permute-start.17 = (bf16[256,512]{1,0:T(8,128)(2,1)S(1)}, bf16[256,512]{1,0:T(8,128)(2,1)S(1)}, u32[]{:S(2)}, u32[]{:S(2)}) collective-permute-start(bf16[256,512]{1,0:T(8,128)(2,1)S(1)} %collective-permute-done.16.refs_3_), channel_id=1, source_target_pairs={{0,8},{8,16},{16,24},{24,32},{32,40},{40,48},{48,56},{56,0},{1,9},... | collective-permute-start | bytes 786440 | tf_op jit(solution)/shard_map/ppermute | solution.py:324
  195.5 15.7 %collective-permute-start.26 = (bf16[256,1024]{1,0:T(8,128)(2,1)}, bf16[256,1024]{1,0:T(8,128)(2,1)S(1)}, u32[]{:S(2)}, u32[]{:S(2)}) collective-permute-start(bf16[256,1024]{1,0:T(8,128)(2,1)} %slice.49), channel_id=1, source_target_pairs={{0,192},{64,0},{128,64},{192,128},{1,193},{65,1},{129,65},{193,129... | collective-permute-start | bytes 1572872 | tf_op jit(solution)/shard_map/ppermute | solution.py:324
  196.4 14.8 %collective-permute-start.25 = (bf16[256,1024]{1,0:T(8,128)(2,1)}, bf16[256,1024]{1,0:T(8,128)(2,1)}, u32[]{:S(2)}, u32[]{:S(2)}) collective-permute-start(bf16[256,1024]{1,0:T(8,128)(2,1)} %slice.48), channel_id=1, source_target_pairs={{0,64},{64,128},{128,192},{192,0},{1,65},{65,129},{129,193},{193,1... | collective-permute-start | bytes 1572872 | tf_op jit(solution)/shard_map/ppermute | solution.py:324
  (45 other events, 763.0 us)
Sparse Core Ops, SparseCore 0:
  131.6 36.5 all-gather.3
  170.1 26.8 all-gather.5
where the time goes:
time: 230 us; the launch traced here: 229 us
  waiting for transfers between devices  58.9 us (26%)
  starting transfers between devices  51.8 us (23%)
  Pallas kernels  45.5 us (20%)
  blocking collectives  27.7 us (12%)
  local copies, waits for them, and re-layouts  26.8 us (12%)
  between operations  13.8 us (6%)
  other arithmetic  4.66 us (2%)
    ppermute x27, starting transfers between devices, shift(): lax.ppermute(value, axis, [(i, (i + step) % size) for i in range(size)])  42.7 us
    ppermute x27, waiting for transfers between devices, shift(): lax.ppermute(value, axis, [(i, (i + step) % size) for i in range(size)])  37.9 us
    unnamed x84, local copies, waits for them, and re-layouts  20.1 us
    pallas_call x2, Pallas kernels, spectra(): pl.pallas_call(spectra_kernel, in_specs=[pl.BlockSpec(memory_space=pl.ANY...  19.8 us
    all_to_all x1, blocking collectives, per_device(): lax.all_to_all(for_rows, ('x', 'z'), split_axis=0, concat_axis=0, tiled=T...  18.5 us
    all_to_all x2, waiting for transfers between devices, per_device(): lax.all_to_all(spec, tile, split_axis=0, concat_axis=0, tiled=True)  15.9 us
    pallas_call x1, Pallas kernels, pick(): pl.pallas_call(pick_kernel, grid=(GP // GCH,), in_specs=[pl.BlockSpec((NG...  14.4 us
    all_to_all x1, blocking collectives, per_device(): lax.all_to_all(cols, tile, split_axis=0, concat_axis=0, tiled=True)  9.23 us
  transfers between devices with their start and end apart: 31, of which 12 were waited for; matrix products, arithmetic and copies ran while one was open for 6% of the time, Pallas kernels for 9%

commit v1 on v0

--- a/solution.py
+++ b/solution.py
@@ -87,11 +87,10 @@
 
 def kron_block():
     _, plane = tables()
-    out = np.zeros((2, 2, AEI, SB, NT, QC, SLAB), np.float64)
-    for c in range(2):
-        for q in range(QC):
-            out[c, :, :, c * QC + q, :, q, :] = plane.reshape(2, NT, SLAB, AEI).transpose(0, 3, 1, 2)
-    return out.reshape(2, 2, AEI * SB, GRID * QC).astype(ml_dtypes.bfloat16)
+    out = np.zeros((2, AEI, QC, NT, QC, SLAB), np.float64)
+    for q in range(QC):
+        out[:, :, q, :, q, :] = plane.reshape(2, NT, SLAB, AEI).transpose(0, 3, 1, 2)
+    return out.reshape(2, AEI * QC, GRID * QC).astype(ml_dtypes.bfloat16)
 
 
 def copy_in(refs, spaces, sems):
@@ -160,19 +159,16 @@
             pltpu.VMEM((HALF, 2 * GRID, ROWS), BF),
             pltpu.SemaphoreType.DMA((len(operands),)),
         ],
-        compiler_params=pltpu.CompilerParams(vmem_limit_bytes=40 * 2**20),
+        compiler_params=pltpu.CompilerParams(vmem_limit_bytes=58 * 2**20),
         name="spectra",
     )(*operands)
 
 
-def lines_kernel(y0_ref, y1_ref, m_ref, s_ref):
-    rows = AEI * SB
+def lines_kernel(y_ref, m_ref, s_ref):
+    rows = AEI * QC
 
     def line(d, lanes):
-        parts = [
-            jnp.dot(m_ref[c, d], ref[:, lanes], preferred_element_type=F32) for c, ref in ((0, y0_ref), (1, y1_ref))
-        ]
-        return parts[0] + parts[1]
+        return jnp.dot(m_ref[d], y_ref[:, lanes], preferred_element_type=F32)
 
     for g in range(2):
         s = line(0, pl.ds(512 * g, 256)) + line(1, pl.ds(512 * g + 256, 256))
@@ -184,43 +180,69 @@
     s_ref[2 * rows :, BTILE:] = s.astype(BF)
 
 
-def lines(y0, y1, m):
+def lines(y, m):
     return pl.pallas_call(
         lines_kernel,
-        out_shape=jax.ShapeDtypeStruct((NGRP * AEI * SB, CODES), BF),
+        out_shape=jax.ShapeDtypeStruct((NGRP * AEI * QC, CODES), BF),
         compiler_params=pltpu.CompilerParams(vmem_limit_bytes=40 * 2**20),
         name="lines",
-    )(y0, y1, m)
-
-
-def pick_kernel(s_ref, a_ref, b_ref, oc_ref, or_ref):
+    )(y, m)
+
+
+def picked(s_ref, a_ref, b_ref, chunk):
     codes = lax.broadcasted_iota(jnp.int32, (CODES, CODES), 0)
+    row = lax.broadcasted_iota(jnp.int32, (SB, CODES), 0)
     outs = []
     for g in range(GCH // CODES):
         lanes = pl.ds(g * CODES, CODES)
         chosen = (codes == b_ref[:, lanes]).astype(F32).astype(BF)
         r = jnp.dot(s_ref[...], chosen, preferred_element_type=F32)
-        code = jnp.broadcast_to(a_ref[:, lanes], (SB, CODES))
+        code = a_ref[:, lanes] - row // QC
         acc = jnp.zeros((SB, CODES), F32)
-        for a in range(NGRP * AEI):
-            acc = jnp.where(code == a, r[a * SB : (a + 1) * SB], acc)
-        outs.append(acc.astype(BF))
-    out = jnp.concatenate(outs, axis=1)
+        for a in range(0, NGRP * AEI, 2):
+            acc = jnp.where(code == a, r[a * QC : (a + 2) * QC], acc)
+        both = acc + pltpu.roll(acc, QC, 0)
+        outs.append(jnp.where(row // QC == chunk, both, 0.0))
+    return jnp.concatenate(outs, axis=1)
+
+
+def first_kernel(s_ref, a_ref, b_ref, o_ref):
+    o_ref[...] = picked(s_ref, a_ref, b_ref, 0)
+
+
+def second_kernel(s_ref, a_ref, b_ref, first_ref, oc_ref, or_ref):
+    out = (first_ref[...] + picked(s_ref, a_ref, b_ref, 1)).astype(BF)
     oc_ref[0] = out
     for h in range(GCH // RB):
         or_ref[h] = out[:, h * RB : (h + 1) * RB]
 
 
-def pick(s, a, b):
+def pick_specs():
+    return [
+        pl.BlockSpec((NGRP * AEI * QC, CODES), lambda i: (0, 0)),
+        pl.BlockSpec((1, GCH), lambda i: (0, i)),
+        pl.BlockSpec((1, GCH), lambda i: (0, i)),
+    ]
+
+
+def pick_first(s, a, b):
+    return pl.pallas_call(
+        first_kernel,
+        grid=(GP // GCH,),
+        in_specs=pick_specs(),
+        out_specs=pl.BlockSpec((SB, GCH), lambda i: (0, i)),
+        out_shape=jax.ShapeDtypeStruct((SB, GP), F32),
+        compiler_params=pltpu.CompilerParams(vmem_limit_bytes=40 * 2**20),
+        name="pick_first",
+    )(s, a, b)
+
+
+def pick_second(s, a, b, first):
     per = 4 * RB // GCH
     return pl.pallas_call(
-        pick_kernel,
+        second_kernel,
         grid=(GP // GCH,),
-        in_specs=[
-            pl.BlockSpec((NGRP * AEI * SB, CODES), lambda i: (0, 0)),
-            pl.BlockSpec((1, GCH), lambda i: (0, i)),
-            pl.BlockSpec((1, GCH), lambda i: (0, i)),
-        ],
+        in_specs=pick_specs() + [pl.BlockSpec((SB, GCH), lambda i: (0, i))],
         out_specs=[
             pl.BlockSpec((1, SB, GCH), lambda i: (i // per, 0, i % per)),
             pl.BlockSpec((GCH // RB, SB, RB), lambda i: (i, 0, 0)),
@@ -230,8 +252,8 @@
             jax.ShapeDtypeStruct((32, SB, RB), BF),
         ],
         compiler_params=pltpu.CompilerParams(vmem_limit_bytes=40 * 2**20),
-        name="pick",
-    )(s, a, b)
+        name="pick_second",
+    )(s, a, b, first)
 
 
 KP = NT * SB
@@ -295,7 +317,7 @@
             pltpu.VMEM((RB, 4 * RB), F32),
             pltpu.SemaphoreType.DMA((len(operands),)),
         ],
-        compiler_params=pltpu.CompilerParams(vmem_limit_bytes=48 * 2**20),
+        compiler_params=pltpu.CompilerParams(vmem_limit_bytes=58 * 2**20),
         name="product",
     )(place, weight, *operands)
 
@@ -347,7 +369,9 @@
         if m < VB // 2:
             vs[VB - m] = shift(vs[(VB - m + 1) % VB], "z", NZ, -1)
     specs.append(spectra([vs[k] for k in SLOTS[1]], cs, depth, plane))
-    slabs = [lax.all_to_all(spec, tile, split_axis=0, concat_axis=0, tiled=True) for spec in specs]
+    slabs = [lax.all_to_all(specs[0], tile, split_axis=0, concat_axis=0, tiled=True)]
+    slabs[0], specs[1] = lax.optimization_barrier((slabs[0], specs[1]))
+    slabs.append(lax.all_to_all(specs[1], tile, split_axis=0, concat_axis=0, tiled=True))
 
     valence_level = pick_levels(valence_pick, valence_energy)
     band_level = pick_levels(cond_pick, conduction_energy)
@@ -369,12 +393,12 @@
     a_code = a_code + AEI * (b_code // CODES)
     b_code = b_code % CODES
 
-    combined = lines(slabs[0].reshape(GRID * QC, YL), slabs[1].reshape(GRID * QC, YL), kron)
-    cols, for_rows = pick(combined, a_code, b_code)
+    first = pick_first(lines(slabs[0].reshape(GRID * QC, YL), kron), a_code, b_code)
+    cols, for_rows = pick_second(lines(slabs[1].reshape(GRID * QC, YL), kron), a_code, b_code, first)
     cols = lax.all_to_all(cols, tile, split_axis=0, concat_axis=0, tiled=True).reshape(KP, 4 * RB)
     b_bundle = lax.all_gather(cols[:, LA:], "z", axis=0, tiled=True)
     near, far = ring(cols[:, :LA], "x", NX)
-    for_rows, near[1] = lax.optimization_barrier((for_rows, near[1]))
+    for_rows, near[1], near[2] = lax.optimization_barrier((for_rows, near[1], near[2]))
     a_cols, a_far = ring(jnp.concatenate(near + far, axis=0), "z", NZ)
     b_cols, b_far = ring(b_bundle, "x", NX)
     rows = lax.all_to_all(for_rows, ("x", "z"), split_axis=0, concat_axis=0, tiled=True)

time: 230 us -> 211 us (0.917)
  local copies, waits for them, and re-layouts: 26.8 us -> 8.28 us
  Pallas kernels: 45.5 us -> 51.6 us
  waiting for transfers between devices: 58.9 us -> 54.6 us
    unnamed x84 -> x76, local copies, waits for them, and re-layouts: 20.1 us -> 4.27 us
    all_to_all x2, waiting for transfers between devices: 15.9 us -> 6.13 us  [the longest x1 6.13 us: per_device(): lax.all_to_all(specs[1], tile, split_axis=0, concat_axis=0, tiled=True)]
    all_gather x1, waiting for transfers between devices: 5.06 us -> 9.43 us  [per_device(): b_bundle = lax.all_gather(cols[:, LA:], 'z', axis=0, tiled=True)]
    pallas_call x1 -> x2, Pallas kernels: 14.4 us -> 18 us  [the longest x1 8.99 us: pick_second(): pl.pallas_call(second_kernel, grid=(GP // GCH,), in_specs=pick_specs() +...]
    pallas_call x2, Pallas kernels: 19.8 us -> 22.9 us  [spectra(): pl.pallas_call(spectra_kernel, in_specs=[pl.BlockSpec(memory_space=pl.ANY...]
    pallas_call x1 -> x2, Pallas kernels: 3.97 us -> 1.61 us  [lines(): pl.pallas_call(lines_kernel, out_shape=jax.ShapeDtypeStruct((NGRP * AEI *...]
  transfers between devices with their start and end apart: 31 -> 31, of which waited for: 12 -> 13; matrix products, arithmetic and copies ran while one was open for 6% -> 3% of each run, Pallas kernels for 9% -> 16%
where the time goes in v1:
time: 211 us; the launch traced here: 209 us
  waiting for transfers between devices  54.6 us (26%)
  Pallas kernels  51.6 us (24%)
  starting transfers between devices  49.9 us (24%)
  blocking collectives  28.4 us (13%)
  between operations  14 us (7%)
  local copies, waits for them, and re-layouts  8.28 us (4%)
  other arithmetic  2.42 us (1%)
    ppermute x27, starting transfers between devices, shift(): lax.ppermute(value, axis, [(i, (i + step) % size) for i in range(size)])  40.8 us
    ppermute x27, waiting for transfers between devices, shift(): lax.ppermute(value, axis, [(i, (i + step) % size) for i in range(size)])  39 us
    pallas_call x2, Pallas kernels, spectra(): pl.pallas_call(spectra_kernel, in_specs=[pl.BlockSpec(memory_space=pl.ANY...  22.9 us
    all_to_all x1, blocking collectives, per_device(): lax.all_to_all(for_rows, ('x', 'z'), split_axis=0, concat_axis=0, tiled=T...  19 us
    all_gather x1, waiting for transfers between devices, per_device(): b_bundle = lax.all_gather(cols[:, LA:], 'z', axis=0, tiled=True)  9.43 us
    all_to_all x1, blocking collectives, per_device(): lax.all_to_all(cols, tile, split_axis=0, concat_axis=0, tiled=True)  9.36 us
    pallas_call x1, Pallas kernels, product(): pl.pallas_call(product_kernel, in_specs=[pl.BlockSpec(memory_space=pltpu....  9.06 us
    pallas_call x1, Pallas kernels, pick_second(): pl.pallas_call(second_kernel, grid=(GP // GCH,), in_specs=pick_specs() +...  8.99 us
  transfers between devices with their start and end apart: 31, of which 13 were waited for; matrix products, arithmetic and copies ran while one was open for 3% of the time, Pallas kernels for 16%

profile of v1, /device:TPU:6, one launch (start us, length us, event | category | flops | bytes accessed | tf_op | source)
XLA Modules:
  0.0 209.2 jit_solution(13590504170756728802)
XLA Ops:
  10.5 3.9 %collective-permute-start.1 = (bf16[1,12,9216]{2,1,0:T(8,128)(2,1)}, bf16[1,12,9216]{2,1,0:T(8,128)(2,1)S(1)}, u32[]{:S(2)}, u32[]{:S(2)}) collective-permute-start(bf16[1,12,9216]{2,1,0:T(8,128)(2,1)} %refs_0_.1), channel_id=1, source_target_pairs={{0,56},{8,0},{16,8},{24,16},{32,24},{40,32},{48,40},{56,48},{1,57}... | collective-permute-start | bytes 663560 | tf_op jit(solution)/shard_map/ppermute | solution.py:346
  14.4 6.7 %collective-permute-done.refs_1_ = bf16[1,12,9216]{2,1,0:T(8,128)(2,1)S(1)} collective-permute-done((bf16[1,12,9216]{2,1,0:T(8,128)(2,1)}, bf16[1,12,9216]{2,1,0:T(8,128)(2,1)S(1)}, u32[]{:S(2)}, u32[]{:S(2)}) %collective-permute-start) | collective-permute-done | bytes 221216 | tf_op jit(solution)/shard_map/ppermute | solution.py:346
  21.1 3.2 %collective-permute-start.7 = (bf16[1,12,9216]{2,1,0:T(8,128)(2,1)S(1)}, bf16[1,12,9216]{2,1,0:T(8,128)(2,1)S(1)}, u32[]{:S(2)}, u32[]{:S(2)}) collective-permute-start(bf16[1,12,9216]{2,1,0:T(8,128)(2,1)S(1)} %collective-permute-done.1.refs_2_), channel_id=1, source_target_pairs={{0,56},{8,0},{16,8},{24,16},{32,24},{40,32},{48,40},{56,48},{1,57}... | collective-permute-start | bytes 663560 | tf_op jit(solution)/shard_map/ppermute | solution.py:346
  26.8 3.0 %collective-permute-done.2.refs_3_ = bf16[1,12,9216]{2,1,0:T(8,128)(2,1)S(1)} collective-permute-done((bf16[1,12,9216]{2,1,0:T(8,128)(2,1)S(1)}, bf16[1,12,9216]{2,1,0:T(8,128)(2,1)S(1)}, u32[]{:S(2)}, u32[]{:S(2)}) %collective-permute-start.2) | collective-permute-done | bytes 221216 | tf_op jit(solution)/shard_map/ppermute | solution.py:346
  31.0 3.3 %collective-permute-start.9 = (bf16[1,12,9216]{2,1,0:T(8,128)(2,1)S(1)}, bf16[1,12,9216]{2,1,0:T(8,128)(2,1)S(1)}, u32[]{:S(2)}, u32[]{:S(2)}) collective-permute-start(bf16[1,12,9216]{2,1,0:T(8,128)(2,1)S(1)} %collective-permute-done.7.refs_0_), channel_id=1, source_target_pairs={{0,56},{8,0},{16,8},{24,16},{32,24},{40,32},{48,40},{56,48},{1,57}... | collective-permute-start | bytes 663560 | tf_op jit(solution)/shard_map/ppermute | solution.py:346
  35.7 11.5 %spectra.2 = bf16[8,48,1408]{2,1,0:T(8,128)(2,1)} custom-call(bf16[1,12,9216]{2,1,0:T(8,128)(2,1)} %refs_0_.1, bf16[1,12,9216]{2,1,0:T(8,128)(2,1)} %copy-done.14, bf16[1,12,9216]{2,1,0:T(8,128)(2,1)} %copy-done.15, bf16[1,12,9216]{2,1,0:T(8,128)(2,1)} %copy-done.16, bf16[2,12,9216]{2,1,0:T(8,128)(2,1)} %copy.34.refs_4_, bf16[2,12,9216]{2,1,0:T(8,128)(2,1)} %copy-done.1, ...), custom_call_target="tpu_custom_call" | custom-call | tf_op jit(solution)/shard_map/spectra/pallas_call | solution.py:150
  47.3 4.5 %all-to-all-start = ((bf16[8,48,1408]{2,1,0:T(8,128)(2,1)}), bf16[8,48,1408]{2,1,0:T(8,128)(2,1)S(1)}, u32[]{:S(2)}, u32[]{:S(2)}) async-start(bf16[8,48,1408]{2,1,0:T(8,128)(2,1)} %spectra.2), calls=%async_computation | async-start | bytes 2162688 | tf_op jit(solution)/shard_map/all_to_all | solution.py:372
  52.9 9.8 %collective-permute-done.10.refs_3_ = bf16[1,12,9216]{2,1,0:T(8,128)(2,1)S(1)} collective-permute-done((bf16[1,12,9216]{2,1,0:T(8,128)(2,1)S(1)}, bf16[1,12,9216]{2,1,0:T(8,128)(2,1)S(1)}, u32[]{:S(2)}, u32[]{:S(2)}) %collective-permute-start.10) | collective-permute-done | bytes 221216 | tf_op jit(solution)/shard_map/ppermute | solution.py:346
  63.4 11.4 %spectra.3 = bf16[8,48,1408]{2,1,0:T(8,128)(2,1)} custom-call(bf16[1,12,9216]{2,1,0:T(8,128)(2,1)} %copy-done.13, bf16[1,12,9216]{2,1,0:T(8,128)(2,1)} %copy-done.17, bf16[1,12,9216]{2,1,0:T(8,128)(2,1)} %copy-done.18, bf16[1,12,9216]{2,1,0:T(8,128)(2,1)} %copy-done.19, bf16[2,12,9216]{2,1,0:T(8,128)(2,1)} %copy.34.refs_4_, bf16[2,12,9216]{2,1,0:T(8,128)(2,1)} %copy-done.1, ...), custom_call_target="tpu_custom_call" | custom-call | tf_op jit(solution)/shard_map/spectra/pallas_call | solution.py:150
  74.8 4.6 %all-to-all-start.1 = ((bf16[8,48,1408]{2,1,0:T(8,128)(2,1)}), bf16[8,48,1408]{2,1,0:T(8,128)(2,1)S(1)}, u32[]{:S(2)}, u32[]{:S(2)}) async-start(bf16[8,48,1408]{2,1,0:T(8,128)(2,1)} %spectra.3), calls=%async_computation.1 | async-start | bytes 2162688 | tf_op jit(solution)/shard_map/all_to_all | solution.py:374
  80.6 9.0 %pick_first.1.first_ref = f32[8,12288]{1,0:T(8,128)S(1)} custom-call(bf16[888,256]{1,0:T(8,128)(2,1)S(1)} %lines.3.s_ref, s32[1,12288]{1,0:T(1,128)S(1)} %multiply_add_fusion.a_ref, s32[1,12288]{1,0:T(1,128)S(1)} %get-tuple-element.19.b_ref), custom_call_target="tpu_custom_call" | custom-call | tf_op jit(solution)/shard_map/pick_first/pallas_call | solution.py:229
  89.6 6.1 %all-to-all-done.1 = bf16[8,48,1408]{2,1,0:T(8,128)(2,1)S(1)} async-done(((bf16[8,48,1408]{2,1,0:T(8,128)(2,1)}), bf16[8,48,1408]{2,1,0:T(8,128)(2,1)S(1)}, u32[]{:S(2)}, u32[]{:S(2)}) %all-to-all-start.1) | async-done | bytes 1081376 | tf_op jit(solution)/shard_map/all_to_all | solution.py:374
  96.6 9.0 %pick_second.1 = (bf16[8,8,1536]{2,1,0:T(8,128)(2,1)S(1)}, bf16[32,8,384]{2,1,0:T(8,128)(2,1)S(1)}) custom-call(bf16[888,256]{1,0:T(8,128)(2,1)S(1)} %lines.2.s_ref, s32[1,12288]{1,0:T(1,128)S(1)} %multiply_add_fusion.a_ref, s32[1,12288]{1,0:T(1,128)S(1)} %get-tuple-element.19.b_ref, f32[8,12288]{1,0:T(8,128)S(1)} %pick_first.1.first_ref), custom_call_target="tpu_custom_call" | custom-call | tf_op jit(solution)/shard_map/pick_second/pallas_call | solution.py:242
  105.6 9.4 %all_to_all.20 = bf16[8,8,1536]{2,1,0:T(8,128)(2,1)S(1)} all-to-all(bf16[8,8,1536]{2,1,0:T(8,128)(2,1)S(1)} %get-tuple-element.15), channel_id=1, replica_groups=mesh['x'=4,'z'=8,'y'=4,'core'=2] {'y','core'}, dimensions={0} | all-to-all | bytes 393216 | tf_op jit(solution)/shard_map/all_to_all | solution.py:398
  121.3 19.0 %all_to_all.21 = bf16[32,8,384]{2,1,0:T(8,128)(2,1)} all-to-all(bf16[32,8,384]{2,1,0:T(8,128)(2,1)S(1)} %get-tuple-element.16), channel_id=1, replica_groups=mesh['x'=4,'z'=8,'y'=4,'core'=2] {'x','z'}, dimensions={0} | all-to-all | bytes 393216 | tf_op jit(solution)/shard_map/all_to_all | solution.py:404
  140.9 2.7 %collective-permute-start.13 = (bf16[32,512]{1,0:T(8,128)(2,1)S(1)}, bf16[32,512]{1,0:T(8,128)(2,1)S(1)}, u32[]{:S(2)}, u32[]{:S(2)}) collective-permute-start(bf16[32,512]{1,0:T(8,128)(2,1)S(1)} %slice.43), channel_id=1, source_target_pairs={{0,64},{64,128},{128,192},{192,0},{1,65},{65,129},{129,193},{193,1... | collective-permute-start | bytes 98312 | tf_op jit(solution)/shard_map/ppermute | solution.py:346
  143.7 9.4 %all-gather.4.cloned.1.call-done.refs_10_ = bf16[512,1024]{1,0:T(8,128)(2,1)} async-done(((bf16[64,1024]{1,0:T(8,128)(2,1)}), bf16[512,1024]{1,0:T(8,128)(2,1)}) %all-gather.4.cloned.1.call-update) | async-done | bytes 1048592 | tf_op jit(solution)/shard_map/all_gather | solution.py:399
  158.5 6.6 %collective-permute-done.18.refs_5_ = bf16[256,512]{1,0:T(8,128)(2,1)S(1)} collective-permute-done((bf16[256,512]{1,0:T(8,128)(2,1)S(1)}, bf16[256,512]{1,0:T(8,128)(2,1)S(1)}, u32[]{:S(2)}, u32[]{:S(2)}) %collective-permute-start.18) | collective-permute-done | bytes 262176 | tf_op jit(solution)/shard_map/ppermute | solution.py:346
  167.5 5.5 %collective-permute-done.19.refs_6_ = bf16[256,512]{1,0:T(8,128)(2,1)S(1)} collective-permute-done((bf16[256,512]{1,0:T(8,128)(2,1)S(1)}, bf16[256,512]{1,0:T(8,128)(2,1)S(1)}, u32[]{:S(2)}, u32[]{:S(2)}) %collective-permute-start.19) | collective-permute-done | bytes 262176 | tf_op jit(solution)/shard_map/ppermute | solution.py:346
  173.0 3.1 %collective-permute-start.20 = (bf16[256,512]{1,0:T(8,128)(2,1)S(1)}, bf16[256,512]{1,0:T(8,128)(2,1)S(1)}, u32[]{:S(2)}, u32[]{:S(2)}) collective-permute-start(bf16[256,512]{1,0:T(8,128)(2,1)S(1)} %collective-permute-done.19.refs_6_), channel_id=1, source_target_pairs={{0,56},{8,0},{16,8},{24,16},{32,24},{40,32},{48,40},{56,48},{1,57}... | collective-permute-start | bytes 786440 | tf_op jit(solution)/shard_map/ppermute | solution.py:346
  178.5 2.7 %collective-permute-start.25 = (bf16[256,1024]{1,0:T(8,128)(2,1)}, bf16[256,1024]{1,0:T(8,128)(2,1)S(1)}, u32[]{:S(2)}, u32[]{:S(2)}) collective-permute-start(bf16[256,1024]{1,0:T(8,128)(2,1)} %slice.48), channel_id=1, source_target_pairs={{0,64},{64,128},{128,192},{192,0},{1,65},{65,129},{129,193},{193,1... | collective-permute-start | bytes 1572872 | tf_op jit(solution)/shard_map/ppermute | solution.py:346
  182.2 3.7 %collective-permute-start.22 = (bf16[128,512]{1,0:T(8,128)(2,1)}, bf16[128,512]{1,0:T(8,128)(2,1)S(1)}, u32[]{:S(2)}, u32[]{:S(2)}) collective-permute-start(bf16[128,512]{1,0:T(8,128)(2,1)} %slice.46), channel_id=1, source_target_pairs={{0,56},{8,0},{16,8},{24,16},{32,24},{40,32},{48,40},{56,48},{1,57}... | collective-permute-start | bytes 393224 | tf_op jit(solution)/shard_map/ppermute | solution.py:346
  188.8 3.4 %collective-permute-done.21.refs_8_ = bf16[128,512]{1,0:T(8,128)(2,1)S(1)} collective-permute-done((bf16[128,512]{1,0:T(8,128)(2,1)S(1)}, bf16[128,512]{1,0:T(8,128)(2,1)S(1)}, u32[]{:S(2)}, u32[]{:S(2)}) %collective-permute-start.21) | collective-permute-done | bytes 131104 | tf_op jit(solution)/shard_map/ppermute | solution.py:346
  193.3 9.1 %product.1 = f32[375,1500]{1,0:T(8,128)} custom-call(s32[2]{0:T(128)} %pad_add_fusion.xz_ref, f32[2048,1]{1,0:T(8,128)} %copy.40.w_ref, bf16[8,32,8,384]{3,2,1,0:T(8,128)(2,1)} %bitcast.21, bf16[256,512]{1,0:T(8,128)(2,1)} %copy-done.12, bf16[256,512]{1,0:T(8,128)(2,1)} %copy-done.21, bf16[256,512]{1,0:T(8,128)(2,1)} %copy-done.23, ...), custom_call_target="tpu_custom_call" | custom-call | tf_op jit(solution)/shard_map/product/pallas_call | solution.py:309
  (150 shorter events, 34.4 us)
Async XLA Ops:
  6.5 17.8 %collective-permute-start.3 = (bf16[2,12,9216]{2,0,1:T(2,128)(2,1)}, bf16[2,12,9216]{2,0,1:T(2,128)(2,1)S(1)}, u32[]{:S(2)}, u32[]{:S(2)}) collective-permute-start(bf16[2,12,9216]{2,0,1:T(2,128)(2,1)} %param.14), channel_id=1, source_target_pairs={{0,64},{64,128},{128,192},{192,0},{1,65},{65,129},{129,193},{193,1... | collective-permute-start | bytes 1327112 | tf_op jit(solution)/shard_map/ppermute | solution.py:346
  8.7 17.5 %collective-permute-start.4 = (bf16[2,12,9216]{2,0,1:T(2,128)(2,1)}, bf16[2,12,9216]{2,0,1:T(2,128)(2,1)S(1)}, u32[]{:S(2)}, u32[]{:S(2)}) collective-permute-start(bf16[2,12,9216]{2,0,1:T(2,128)(2,1)} %param.14), channel_id=1, source_target_pairs={{0,192},{64,0},{128,64},{192,128},{1,193},{65,1},{129,65},{193,129... | collective-permute-start | bytes 1327112 | tf_op jit(solution)/shard_map/ppermute | solution.py:346
  8.8 12.3 %collective-permute-start = (bf16[1,12,9216]{2,1,0:T(8,128)(2,1)}, bf16[1,12,9216]{2,1,0:T(8,128)(2,1)S(1)}, u32[]{:S(2)}, u32[]{:S(2)}) collective-permute-start(bf16[1,12,9216]{2,1,0:T(8,128)(2,1)} %refs_0_.1), channel_id=1, source_target_pairs={{0,8},{8,16},{16,24},{24,32},{32,40},{40,48},{48,56},{56,0},{1,9},... | collective-permute-start | bytes 663560 | tf_op jit(solution)/shard_map/ppermute | solution.py:346
  10.5 10.6 %collective-permute-start.1 = (bf16[1,12,9216]{2,1,0:T(8,128)(2,1)}, bf16[1,12,9216]{2,1,0:T(8,128)(2,1)S(1)}, u32[]{:S(2)}, u32[]{:S(2)}) collective-permute-start(bf16[1,12,9216]{2,1,0:T(8,128)(2,1)} %refs_0_.1), channel_id=1, source_target_pairs={{0,56},{8,0},{16,8},{24,16},{32,24},{40,32},{48,40},{56,48},{1,57}... | collective-permute-start | bytes 663560 | tf_op jit(solution)/shard_map/ppermute | solution.py:346
  21.1 8.8 %collective-permute-start.2 = (bf16[1,12,9216]{2,1,0:T(8,128)(2,1)S(1)}, bf16[1,12,9216]{2,1,0:T(8,128)(2,1)S(1)}, u32[]{:S(2)}, u32[]{:S(2)}) collective-permute-start(bf16[1,12,9216]{2,1,0:T(8,128)(2,1)S(1)} %collective-permute-done.refs_1_), channel_id=1, source_target_pairs={{0,8},{8,16},{16,24},{24,32},{32,40},{40,48},{48,56},{56,0},{1,9},... | collective-permute-start | bytes 663560 | tf_op jit(solution)/shard_map/ppermute | solution.py:346
  21.1 9.9 %collective-permute-start.7 = (bf16[1,12,9216]{2,1,0:T(8,128)(2,1)S(1)}, bf16[1,12,9216]{2,1,0:T(8,128)(2,1)S(1)}, u32[]{:S(2)}, u32[]{:S(2)}) collective-permute-start(bf16[1,12,9216]{2,1,0:T(8,128)(2,1)S(1)} %collective-permute-done.1.refs_2_), channel_id=1, source_target_pairs={{0,56},{8,0},{16,8},{24,16},{32,24},{40,32},{48,40},{56,48},{1,57}... | collective-permute-start | bytes 663560 | tf_op jit(solution)/shard_map/ppermute | solution.py:346
  24.5 9.9 %collective-permute-start.5 = (bf16[1,12,9216]{2,1,0:T(8,128)(2,1)S(1)}, bf16[1,12,9216]{2,1,0:T(8,128)(2,1)S(1)}, u32[]{:S(2)}, u32[]{:S(2)}) collective-permute-start(bf16[1,12,9216]{2,1,0:T(8,128)(2,1)S(1)} %slice.40), channel_id=1, source_target_pairs={{0,64},{64,128},{128,192},{192,0},{1,65},{65,129},{129,193},{193,1... | collective-permute-start | bytes 663560 | tf_op jit(solution)/shard_map/ppermute | solution.py:346
  29.8 21.9 %collective-permute-start.8 = (bf16[1,12,9216]{2,1,0:T(8,128)(2,1)S(1)}, bf16[1,12,9216]{2,1,0:T(8,128)(2,1)S(1)}, u32[]{:S(2)}, u32[]{:S(2)}) collective-permute-start(bf16[1,12,9216]{2,1,0:T(8,128)(2,1)S(1)} %collective-permute-done.2.refs_3_), channel_id=1, source_target_pairs={{0,8},{8,16},{16,24},{24,32},{32,40},{40,48},{48,56},{56,0},{1,9},... | collective-permute-start | bytes 663560 | tf_op jit(solution)/shard_map/ppermute | solution.py:346
  31.0 21.8 %collective-permute-start.9 = (bf16[1,12,9216]{2,1,0:T(8,128)(2,1)S(1)}, bf16[1,12,9216]{2,1,0:T(8,128)(2,1)S(1)}, u32[]{:S(2)}, u32[]{:S(2)}) collective-permute-start(bf16[1,12,9216]{2,1,0:T(8,128)(2,1)S(1)} %collective-permute-done.7.refs_0_), channel_id=1, source_target_pairs={{0,56},{8,0},{16,8},{24,16},{32,24},{40,32},{48,40},{56,48},{1,57}... | collective-permute-start | bytes 663560 | tf_op jit(solution)/shard_map/ppermute | solution.py:346
  47.3 27.6 %all-to-all-start = ((bf16[8,48,1408]{2,1,0:T(8,128)(2,1)}), bf16[8,48,1408]{2,1,0:T(8,128)(2,1)S(1)}, u32[]{:S(2)}, u32[]{:S(2)}) async-start(bf16[8,48,1408]{2,1,0:T(8,128)(2,1)} %spectra.2), calls=%async_computation | async-start | bytes 2162688 | tf_op jit(solution)/shard_map/all_to_all | solution.py:372
  51.8 10.9 %collective-permute-start.10 = (bf16[1,12,9216]{2,1,0:T(8,128)(2,1)S(1)}, bf16[1,12,9216]{2,1,0:T(8,128)(2,1)S(1)}, u32[]{:S(2)}, u32[]{:S(2)}) collective-permute-start(bf16[1,12,9216]{2,1,0:T(8,128)(2,1)S(1)} %collective-permute-done.8.refs_1_), channel_id=1, source_target_pairs={{0,8},{8,16},{16,24},{24,32},{32,40},{40,48},{48,56},{56,0},{1,9},... | collective-permute-start | bytes 663560 | tf_op jit(solution)/shard_map/ppermute | solution.py:346
  74.8 20.9 %all-to-all-start.1 = ((bf16[8,48,1408]{2,1,0:T(8,128)(2,1)}), bf16[8,48,1408]{2,1,0:T(8,128)(2,1)S(1)}, u32[]{:S(2)}, u32[]{:S(2)}) async-start(bf16[8,48,1408]{2,1,0:T(8,128)(2,1)} %spectra.3), calls=%async_computation.1 | async-start | bytes 2162688 | tf_op jit(solution)/shard_map/all_to_all | solution.py:374
  79.4 73.7 %all-gather.4.cloned.1.call-start = ((), (), s32[]{:S(2)}) async-start(), calls=%async_computation.4 | async-start | bytes 1179648 | tf_op jit(solution)/shard_map/all_gather | solution.py:399
  115.7 76.5 %all-gather.6.cloned.1.call-start = ((), (), s32[]{:S(2)}) async-start(), calls=%async_computation.5 | async-start | bytes 1769472 | tf_op jit(solution)/shard_map/all_gather | solution.py:405
  140.4 16.1 %collective-permute-start.14 = (bf16[32,512]{1,0:T(8,128)(2,1)S(1)}, bf16[32,512]{1,0:T(8,128)(2,1)S(1)}, u32[]{:S(2)}, u32[]{:S(2)}) collective-permute-start(bf16[32,512]{1,0:T(8,128)(2,1)S(1)} %slice.44), channel_id=1, source_target_pairs={{0,192},{64,0},{128,64},{192,128},{1,193},{65,1},{129,65},{193,129... | collective-permute-start | bytes 98312 | tf_op jit(solution)/shard_map/ppermute | solution.py:346
  140.9 15.4 %collective-permute-start.13 = (bf16[32,512]{1,0:T(8,128)(2,1)S(1)}, bf16[32,512]{1,0:T(8,128)(2,1)S(1)}, u32[]{:S(2)}, u32[]{:S(2)}) collective-permute-start(bf16[32,512]{1,0:T(8,128)(2,1)S(1)} %slice.43), channel_id=1, source_target_pairs={{0,64},{64,128},{128,192},{192,0},{1,65},{65,129},{129,193},{193,1... | collective-permute-start | bytes 98312 | tf_op jit(solution)/shard_map/ppermute | solution.py:346
  153.1 23.8 %collective-permute-start.24 = (bf16[512,1024]{1,0:T(8,128)(2,1)}, bf16[512,1024]{1,0:T(8,128)(2,1)S(1)}, u32[]{:S(2)}, u32[]{:S(2)}) collective-permute-start(bf16[512,1024]{1,0:T(8,128)(2,1)} %all-gather.4.cloned.1.call-done.refs_10_), channel_id=1, source_target_pairs={{0,192},{64,0},{128,64},{192,128},{1,193},{65,1},{129,65},{193,129... | collective-permute-start | bytes 3145736 | tf_op jit(solution)/shard_map/ppermute | solution.py:346
  153.7 24.0 %collective-permute-start.23 = (bf16[512,1024]{1,0:T(8,128)(2,1)}, bf16[512,1024]{1,0:T(8,128)(2,1)S(1)}, u32[]{:S(2)}, u32[]{:S(2)}) collective-permute-start(bf16[512,1024]{1,0:T(8,128)(2,1)} %all-gather.4.cloned.1.call-done.refs_10_), channel_id=1, source_target_pairs={{0,64},{64,128},{128,192},{192,0},{1,65},{65,129},{129,193},{193,1... | collective-permute-start | bytes 3145736 | tf_op jit(solution)/shard_map/ppermute | solution.py:346
  156.4 8.7 %collective-permute-start.18 = (bf16[256,512]{1,0:T(8,128)(2,1)S(1)}, bf16[256,512]{1,0:T(8,128)(2,1)S(1)}, u32[]{:S(2)}, u32[]{:S(2)}) collective-permute-start(bf16[256,512]{1,0:T(8,128)(2,1)S(1)} %constant_dynamic-update-slice_fusion.refs_1_), channel_id=1, source_target_pairs={{0,56},{8,0},{16,8},{24,16},{32,24},{40,32},{48,40},{56,48},{1,57}... | collective-permute-start | bytes 786440 | tf_op jit(solution)/shard_map/ppermute | solution.py:346
  158.0 8.9 %collective-permute-start.15 = (bf16[256,512]{1,0:T(8,128)(2,1)S(1)}, bf16[256,512]{1,0:T(8,128)(2,1)S(1)}, u32[]{:S(2)}, u32[]{:S(2)}) collective-permute-start(bf16[256,512]{1,0:T(8,128)(2,1)S(1)} %constant_dynamic-update-slice_fusion.refs_1_), channel_id=1, source_target_pairs={{0,8},{8,16},{16,24},{24,32},{32,40},{40,48},{48,56},{56,0},{1,9},... | collective-permute-start | bytes 786440 | tf_op jit(solution)/shard_map/ppermute | solution.py:346
  166.9 9.8 %collective-permute-start.16 = (bf16[256,512]{1,0:T(8,128)(2,1)S(1)}, bf16[256,512]{1,0:T(8,128)(2,1)S(1)}, u32[]{:S(2)}, u32[]{:S(2)}) collective-permute-start(bf16[256,512]{1,0:T(8,128)(2,1)S(1)} %collective-permute-done.15.refs_2_), channel_id=1, source_target_pairs={{0,8},{8,16},{16,24},{24,32},{32,40},{40,48},{48,56},{56,0},{1,9},... | collective-permute-start | bytes 786440 | tf_op jit(solution)/shard_map/ppermute | solution.py:346
  176.7 9.2 %collective-permute-start.17 = (bf16[256,512]{1,0:T(8,128)(2,1)S(1)}, bf16[256,512]{1,0:T(8,128)(2,1)S(1)}, u32[]{:S(2)}, u32[]{:S(2)}) collective-permute-start(bf16[256,512]{1,0:T(8,128)(2,1)S(1)} %collective-permute-done.16.refs_3_), channel_id=1, source_target_pairs={{0,8},{8,16},{16,24},{24,32},{32,40},{40,48},{48,56},{56,0},{1,9},... | collective-permute-start | bytes 786440 | tf_op jit(solution)/shard_map/ppermute | solution.py:346
  177.0 15.2 %collective-permute-start.26 = (bf16[256,1024]{1,0:T(8,128)(2,1)S(1)}, bf16[256,1024]{1,0:T(8,128)(2,1)S(1)}, u32[]{:S(2)}, u32[]{:S(2)}) collective-permute-start(bf16[256,1024]{1,0:T(8,128)(2,1)S(1)} %slice.49), channel_id=1, source_target_pairs={{0,192},{64,0},{128,64},{192,128},{1,193},{65,1},{129,65},{193,129... | collective-permute-start | bytes 1572872 | tf_op jit(solution)/shard_map/ppermute | solution.py:346
  178.5 13.7 %collective-permute-start.25 = (bf16[256,1024]{1,0:T(8,128)(2,1)}, bf16[256,1024]{1,0:T(8,128)(2,1)S(1)}, u32[]{:S(2)}, u32[]{:S(2)}) collective-permute-start(bf16[256,1024]{1,0:T(8,128)(2,1)} %slice.48), channel_id=1, source_target_pairs={{0,64},{64,128},{128,192},{192,0},{1,65},{65,129},{129,193},{193,1... | collective-permute-start | bytes 1572872 | tf_op jit(solution)/shard_map/ppermute | solution.py:346
  (41 other events, 605.8 us)
Sparse Core Ops, SparseCore 0:
  115.8 37.2 all-gather.3
  154.9 25.8 all-gather.5

commit v2 on v1

--- a/solution.py
+++ b/solution.py
@@ -87,9 +87,11 @@
 
 def kron_block():
     _, plane = tables()
-    out = np.zeros((2, AEI, QC, NT, QC, SLAB), np.float64)
+    out = np.zeros((2, AEI, QC, NT, QC * SLAB), np.float64)
+    slabs = plane.reshape(2, NT, SLAB, AEI).transpose(0, 3, 1, 2)
     for q in range(QC):
-        out[:, :, q, :, q, :] = plane.reshape(2, NT, SLAB, AEI).transpose(0, 3, 1, 2)
+        out[:, :, q, :, 8 * q : 8 * q + 8] = slabs[..., :8]
+        out[:, :, q, :, 8 * QC + 4 * q : 8 * QC + 4 * q + 4] = slabs[..., 8:]
     return out.reshape(2, AEI * QC, GRID * QC).astype(ml_dtypes.bfloat16)
 
 
@@ -102,7 +104,7 @@
 
 def spectra_kernel(*refs):
     n = VC + NX + 3
-    o_ref, wide, dens, zs, sems = refs[n], *refs[2 * n + 1 :]
+    o_ref, dens, zs, sems = refs[n], *refs[2 * n + 1 :]
     spaces = refs[n + 1 : 2 * n + 1]
     copies = copy_in(refs[:n], spaces, sems)
     v_refs, c_refs, (t_ref, w_ref) = spaces[:VC], spaces[VC : n - 2], spaces[n - 2 :]
@@ -112,15 +114,19 @@
     def body(step, _):
         lanes = pl.ds(pl.multiple_of(step * YSTEP, YSTEP), YSTEP)
 
-        def stack(slot, pieces):
-            for i, (ref, b) in enumerate(pieces):
-                wide[slot, i * SLAB : (i + 1) * SLAB, :] = ref[b, :, lanes].astype(F32)
-            return wide[slot].astype(BF)
+        def parts(ref, b):
+            wave = ref[b, :, lanes].astype(F32)
+            return wave[:8], wave[8:]
+
+        def tile(pieces):
+            heads = [head for head, _ in pieces]
+            tails = [jnp.concatenate([pieces[i][1], pieces[i + 1][1]], axis=0) for i in range(0, QC, 2)]
+            return jnp.concatenate(heads + tails, axis=0).astype(BF)
 
         bands = [(c_refs[m], b) for m in range(3) for b in range(2)] + [(c_refs[3], 0), (c_refs[4], 0)]
-        cond = [stack(h, bands[QC * h : QC * (h + 1)]) for h in range(2)]
+        cond = [tile([parts(ref, b) for ref, b in bands[QC * h : QC * (h + 1)]]) for h in range(2)]
         for v in range(VC):
-            val = stack(2 + v, [(v_refs[v], 0)] * QC)
+            val = tile([parts(v_refs[v], 0)] * QC)
             for h in range(2):
                 r0 = (v * 2 + h) * SLAB * QC
                 dens[r0 : r0 + SLAB * QC, :] = val * cond[h]
@@ -154,7 +160,6 @@
         out_shape=jax.ShapeDtypeStruct((NT, SLAB * QC, YL), BF),
         scratch_shapes=[pltpu.VMEM(x.shape, BF) for x in operands]
         + [
-            pltpu.VMEM((2 + VC, QC * SLAB, YSTEP), F32),
             pltpu.VMEM((ROWS, YSTEP), BF),
             pltpu.VMEM((HALF, 2 * GRID, ROWS), BF),
             pltpu.SemaphoreType.DMA((len(operands),)),
@@ -323,13 +328,17 @@
 
 
 def ring(value, axis, size):
-    out_up, out_down = [value], [value]
-    for _ in range(size // 2 - 1):
-        out_up.append(shift(out_up[-1], axis, size, 1))
-        out_down.append(shift(out_down[-1], axis, size, -1))
+    return ring_on(value, shift(value, axis, size, 1), shift(value, axis, size, -1), axis, size)
+
+
+def ring_on(value, up, down, axis, size):
+    ups, downs = [up], [down]
+    for _ in range(size // 2 - 2):
+        ups.append(shift(ups[-1], axis, size, 1))
+        downs.append(shift(downs[-1], axis, size, -1))
     half = value.shape[0] // 2
-    far = [shift(out_up[-1][:half], axis, size, 1), shift(out_down[-1][half:], axis, size, -1)]
-    return out_up + out_down[1:], far
+    far = [shift(ups[-1][:half], axis, size, 1), shift(downs[-1][half:], axis, size, -1)]
+    return [value] + ups + downs, far
 
 
 def pick_levels(picks, table):
@@ -361,14 +370,11 @@
     depth, plane, kron = jnp.asarray(depth_block()), jnp.asarray(plane_block()), jnp.asarray(kron_block())
     tile = ("y", "core")
     vs = [valence_waves] + [None] * (VB - 1)
-    specs = []
-    for m in range(1, VB // 2 + 1):
-        if m == VB // 2:
-            specs.append(spectra([vs[k] for k in SLOTS[0]], cs, depth, plane))
+    for m in range(1, VB // 2):
         vs[m] = shift(vs[m - 1], "z", NZ, 1)
-        if m < VB // 2:
-            vs[VB - m] = shift(vs[(VB - m + 1) % VB], "z", NZ, -1)
-    specs.append(spectra([vs[k] for k in SLOTS[1]], cs, depth, plane))
+        vs[VB - m] = shift(vs[(VB - m + 1) % VB], "z", NZ, -1)
+    vs[VB // 2] = shift(vs[2], "z", NZ, 2)
+    specs = [spectra([vs[k] for k in slots], cs, depth, plane) for slots in SLOTS]
     slabs = [lax.all_to_all(specs[0], tile, split_axis=0, concat_axis=0, tiled=True)]
     slabs[0], specs[1] = lax.optimization_barrier((slabs[0], specs[1]))
     slabs.append(lax.all_to_all(specs[1], tile, split_axis=0, concat_axis=0, tiled=True))
@@ -398,8 +404,10 @@
     cols = lax.all_to_all(cols, tile, split_axis=0, concat_axis=0, tiled=True).reshape(KP, 4 * RB)
     b_bundle = lax.all_gather(cols[:, LA:], "z", axis=0, tiled=True)
     near, far = ring(cols[:, :LA], "x", NX)
-    for_rows, near[1], near[2] = lax.optimization_barrier((for_rows, near[1], near[2]))
-    a_cols, a_far = ring(jnp.concatenate(near + far, axis=0), "z", NZ)
+    a_bundle = jnp.concatenate(near + far, axis=0)
+    a_up, a_down = shift(a_bundle, "z", NZ, 1), shift(a_bundle, "z", NZ, -1)
+    for_rows, a_up, a_down = lax.optimization_barrier((for_rows, a_up, a_down))
+    a_cols, a_far = ring_on(a_bundle, a_up, a_down, "z", NZ)
     b_cols, b_far = ring(b_bundle, "x", NX)
     rows = lax.all_to_all(for_rows, ("x", "z"), split_axis=0, concat_axis=0, tiled=True)
     rows = lax.all_gather(rows, ("y", "core"), axis=0, tiled=False)

time: 211 us -> 201 us (0.953)
  waiting for transfers between devices: 54.6 us -> 47.2 us
  blocking collectives: 28.4 us -> 26.1 us
    all_gather x1, waiting for transfers between devices: 9.43 us -> 0.02 us  [per_device(): b_bundle = lax.all_gather(cols[:, LA:], 'z', axis=0, tiled=True)]
    all_to_all x1, waiting for transfers between devices: 0.01 us -> 2.57 us  [per_device(): lax.all_to_all(specs[0], tile, split_axis=0, concat_axis=0, tiled=True)]
    all_to_all x1, blocking collectives: 19 us -> 16.7 us  [per_device(): lax.all_to_all(for_rows, ('x', 'z'), split_axis=0, concat_axis=0, tiled=T...]
    unnamed x76 -> x75, local copies, waits for them, and re-layouts: 4.27 us -> 4.39 us
  transfers between devices with their start and end apart: 31 -> 31, of which waited for: 13 -> 14; matrix products, arithmetic and copies ran while one was open for 3% -> 3% of each run, Pallas kernels for 16% -> 16%
where the time goes in v2:
time: 201 us; the launch traced here: 199 us
  Pallas kernels  51.4 us (26%)
  starting transfers between devices  49.6 us (25%)
  waiting for transfers between devices  47.2 us (23%)
  blocking collectives  26.1 us (13%)
  between operations  14 us (7%)
  local copies, waits for them, and re-layouts  8.5 us (4%)
  other arithmetic  2.35 us (1%)
    ppermute x27, starting transfers between devices, shift(): lax.ppermute(value, axis, [(i, (i + step) % size) for i in range(size)])  41.4 us
    ppermute x27, waiting for transfers between devices, shift(): lax.ppermute(value, axis, [(i, (i + step) % size) for i in range(size)])  38.5 us
    pallas_call x2, Pallas kernels, spectra(): pl.pallas_call(spectra_kernel, in_specs=[pl.BlockSpec(memory_space=pl.ANY...  22.8 us
    all_to_all x1, blocking collectives, per_device(): lax.all_to_all(for_rows, ('x', 'z'), split_axis=0, concat_axis=0, tiled=T...  16.7 us
    all_to_all x1, blocking collectives, per_device(): lax.all_to_all(cols, tile, split_axis=0, concat_axis=0, tiled=True)  9.36 us
    pallas_call x1, Pallas kernels, product(): pl.pallas_call(product_kernel, in_specs=[pl.BlockSpec(memory_space=pltpu....  9.04 us
    pallas_call x1, Pallas kernels, pick_second(): pl.pallas_call(second_kernel, grid=(GP // GCH,), in_specs=pick_specs() +...  8.99 us
    pallas_call x1, Pallas kernels, pick_first(): pl.pallas_call(first_kernel, grid=(GP // GCH,), in_specs=pick_specs(), ou...  8.96 us
  transfers between devices with their start and end apart: 31, of which 14 were waited for; matrix products, arithmetic and copies ran while one was open for 3% of the time, Pallas kernels for 16%

profile of v2, /device:TPU:6, one launch (start us, length us, event | category | flops | bytes accessed | tf_op | source)
XLA Modules:
  0.0 199.1 jit_solution(12856885368245273152)
XLA Ops:
  10.5 3.9 %collective-permute-start.1 = (bf16[1,12,9216]{2,1,0:T(8,128)(2,1)}, bf16[1,12,9216]{2,1,0:T(8,128)(2,1)S(1)}, u32[]{:S(2)}, u32[]{:S(2)}) collective-permute-start(bf16[1,12,9216]{2,1,0:T(8,128)(2,1)} %refs_0_.1), channel_id=1, source_target_pairs={{0,56},{8,0},{16,8},{24,16},{32,24},{40,32},{48,40},{56,48},{1,57}... | collective-permute-start | bytes 663560 | tf_op jit(solution)/shard_map/ppermute | solution.py:355
  14.4 6.7 %collective-permute-done.refs_1_ = bf16[1,12,9216]{2,1,0:T(8,128)(2,1)S(1)} collective-permute-done((bf16[1,12,9216]{2,1,0:T(8,128)(2,1)}, bf16[1,12,9216]{2,1,0:T(8,128)(2,1)S(1)}, u32[]{:S(2)}, u32[]{:S(2)}) %collective-permute-start) | collective-permute-done | bytes 221216 | tf_op jit(solution)/shard_map/ppermute | solution.py:355
  21.1 3.2 %collective-permute-start.7 = (bf16[1,12,9216]{2,1,0:T(8,128)(2,1)S(1)}, bf16[1,12,9216]{2,1,0:T(8,128)(2,1)S(1)}, u32[]{:S(2)}, u32[]{:S(2)}) collective-permute-start(bf16[1,12,9216]{2,1,0:T(8,128)(2,1)S(1)} %collective-permute-done.1.refs_2_), channel_id=1, source_target_pairs={{0,56},{8,0},{16,8},{24,16},{32,24},{40,32},{48,40},{56,48},{1,57}... | collective-permute-start | bytes 663560 | tf_op jit(solution)/shard_map/ppermute | solution.py:355
  35.1 11.4 %spectra.2 = bf16[8,48,1408]{2,1,0:T(8,128)(2,1)} custom-call(bf16[1,12,9216]{2,1,0:T(8,128)(2,1)} %refs_0_.1, bf16[1,12,9216]{2,1,0:T(8,128)(2,1)} %copy-done.15, bf16[1,12,9216]{2,1,0:T(8,128)(2,1)} %copy-done.16, bf16[1,12,9216]{2,1,0:T(8,128)(2,1)} %copy-done.14, bf16[2,12,9216]{2,1,0:T(8,128)(2,1)} %copy.34.refs_4_, bf16[2,12,9216]{2,1,0:T(8,128)(2,1)} %copy-done.1, ...), custom_call_target="tpu_custom_call" | custom-call | tf_op jit(solution)/shard_map/spectra/pallas_call | solution.py:156
  46.6 4.5 %all-to-all-start = ((bf16[8,48,1408]{2,1,0:T(8,128)(2,1)}), bf16[8,48,1408]{2,1,0:T(8,128)(2,1)S(1)}, u32[]{:S(2)}, u32[]{:S(2)}) async-start(bf16[8,48,1408]{2,1,0:T(8,128)(2,1)} %spectra.2), calls=%async_computation | async-start | bytes 2162688 | tf_op jit(solution)/shard_map/all_to_all | solution.py:378
  53.4 11.4 %spectra.3 = bf16[8,48,1408]{2,1,0:T(8,128)(2,1)} custom-call(bf16[1,12,9216]{2,1,0:T(8,128)(2,1)} %copy-done.13, bf16[1,12,9216]{2,1,0:T(8,128)(2,1)} %copy-done.18, bf16[1,12,9216]{2,1,0:T(8,128)(2,1)} %copy-done.19, bf16[1,12,9216]{2,1,0:T(8,128)(2,1)} %copy-done.17, bf16[2,12,9216]{2,1,0:T(8,128)(2,1)} %copy.34.refs_4_, bf16[2,12,9216]{2,1,0:T(8,128)(2,1)} %copy-done.1, ...), custom_call_target="tpu_custom_call" | custom-call | tf_op jit(solution)/shard_map/spectra/pallas_call | solution.py:156
  64.8 2.6 %all-to-all-done = bf16[8,48,1408]{2,1,0:T(8,128)(2,1)S(1)} async-done(((bf16[8,48,1408]{2,1,0:T(8,128)(2,1)}), bf16[8,48,1408]{2,1,0:T(8,128)(2,1)S(1)}, u32[]{:S(2)}, u32[]{:S(2)}) %all-to-all-start) | async-done | bytes 1081376 | tf_op jit(solution)/shard_map/all_to_all | solution.py:378
  67.4 3.6 %all-to-all-start.1 = ((bf16[8,48,1408]{2,1,0:T(8,128)(2,1)}), bf16[8,48,1408]{2,1,0:T(8,128)(2,1)S(1)}, u32[]{:S(2)}, u32[]{:S(2)}) async-start(bf16[8,48,1408]{2,1,0:T(8,128)(2,1)} %spectra.3), calls=%async_computation.1 | async-start | bytes 2162688 | tf_op jit(solution)/shard_map/all_to_all | solution.py:380
  72.2 9.0 %pick_first.1.first_ref = f32[8,12288]{1,0:T(8,128)S(1)} custom-call(bf16[888,256]{1,0:T(8,128)(2,1)S(1)} %lines.3.s_ref, s32[1,12288]{1,0:T(1,128)S(1)} %multiply_add_fusion.a_ref, s32[1,12288]{1,0:T(1,128)S(1)} %get-tuple-element.19.b_ref), custom_call_target="tpu_custom_call" | custom-call | tf_op jit(solution)/shard_map/pick_first/pallas_call | solution.py:234
  81.1 6.1 %all-to-all-done.1 = bf16[8,48,1408]{2,1,0:T(8,128)(2,1)S(1)} async-done(((bf16[8,48,1408]{2,1,0:T(8,128)(2,1)}), bf16[8,48,1408]{2,1,0:T(8,128)(2,1)S(1)}, u32[]{:S(2)}, u32[]{:S(2)}) %all-to-all-start.1) | async-done | bytes 1081376 | tf_op jit(solution)/shard_map/all_to_all | solution.py:380
  88.0 9.0 %pick_second.1 = (bf16[8,8,1536]{2,1,0:T(8,128)(2,1)S(1)}, bf16[32,8,384]{2,1,0:T(8,128)(2,1)S(1)}) custom-call(bf16[888,256]{1,0:T(8,128)(2,1)S(1)} %lines.2.s_ref, s32[1,12288]{1,0:T(1,128)S(1)} %multiply_add_fusion.a_ref, s32[1,12288]{1,0:T(1,128)S(1)} %get-tuple-element.19.b_ref, f32[8,12288]{1,0:T(8,128)S(1)} %pick_first.1.first_ref), custom_call_target="tpu_custom_call" | custom-call | tf_op jit(solution)/shard_map/pick_second/pallas_call | solution.py:247
  97.1 9.4 %all_to_all.20 = bf16[8,8,1536]{2,1,0:T(8,128)(2,1)S(1)} all-to-all(bf16[8,8,1536]{2,1,0:T(8,128)(2,1)S(1)} %get-tuple-element.15), channel_id=1, replica_groups=mesh['x'=4,'z'=8,'y'=4,'core'=2] {'y','core'}, dimensions={0} | all-to-all | bytes 393216 | tf_op jit(solution)/shard_map/all_to_all | solution.py:404
  107.5 3.0 %collective-permute-start.11 = (bf16[64,512]{1,0:T(8,128)(2,1)S(1)}, bf16[64,512]{1,0:T(8,128)(2,1)S(1)}, u32[]{:S(2)}, u32[]{:S(2)}) collective-permute-start(bf16[64,512]{1,0:T(8,128)(2,1)S(1)} %get-tuple-element.21), channel_id=1, source_target_pairs={{0,64},{64,128},{128,192},{192,0},{1,65},{65,129},{129,193},{193,1... | collective-permute-start | bytes 196616 | tf_op jit(solution)/shard_map/ppermute | solution.py:355
  110.5 2.2 %collective-permute-done.12 = bf16[64,512]{1,0:T(8,128)(2,1)S(1)} collective-permute-done((bf16[64,512]{1,0:T(8,128)(2,1)S(1)}, bf16[64,512]{1,0:T(8,128)(2,1)S(1)}, u32[]{:S(2)}, u32[]{:S(2)}) %collective-permute-start.12) | collective-permute-done | bytes 65568 | tf_op jit(solution)/shard_map/ppermute | solution.py:355
  112.8 3.2 %collective-permute-start.13 = (bf16[32,512]{1,0:T(8,128)(2,1)S(1)}, bf16[32,512]{1,0:T(8,128)(2,1)S(1)}, u32[]{:S(2)}, u32[]{:S(2)}) collective-permute-start(bf16[32,512]{1,0:T(8,128)(2,1)S(1)} %slice.43), channel_id=1, source_target_pairs={{0,64},{64,128},{128,192},{192,0},{1,65},{65,129},{129,193},{193,1... | collective-permute-start | bytes 98312 | tf_op jit(solution)/shard_map/ppermute | solution.py:355
  119.9 6.6 %collective-permute-done.16.refs_5_ = bf16[256,512]{1,0:T(8,128)(2,1)S(1)} collective-permute-done((bf16[256,512]{1,0:T(8,128)(2,1)S(1)}, bf16[256,512]{1,0:T(8,128)(2,1)S(1)}, u32[]{:S(2)}, u32[]{:S(2)}) %collective-permute-start.16) | collective-permute-done | bytes 262176 | tf_op jit(solution)/shard_map/ppermute | solution.py:355
  126.5 3.2 %collective-permute-done.15.refs_2_ = bf16[256,512]{1,0:T(8,128)(2,1)S(1)} collective-permute-done((bf16[256,512]{1,0:T(8,128)(2,1)S(1)}, bf16[256,512]{1,0:T(8,128)(2,1)S(1)}, u32[]{:S(2)}, u32[]{:S(2)}) %collective-permute-start.15) | collective-permute-done | bytes 262176 | tf_op jit(solution)/shard_map/ppermute | solution.py:355
  129.7 16.7 %all_to_all.21 = bf16[32,8,384]{2,1,0:T(8,128)(2,1)} all-to-all(bf16[32,8,384]{2,1,0:T(8,128)(2,1)S(1)} %get-tuple-element.16), channel_id=1, replica_groups=mesh['x'=4,'z'=8,'y'=4,'core'=2] {'x','z'}, dimensions={0} | all-to-all | bytes 393216 | tf_op jit(solution)/shard_map/all_to_all | solution.py:412
  147.2 2.6 %collective-permute-start.23 = (bf16[512,1024]{1,0:T(8,128)(2,1)}, bf16[512,1024]{1,0:T(8,128)(2,1)S(1)}, u32[]{:S(2)}, u32[]{:S(2)}) collective-permute-start(bf16[512,1024]{1,0:T(8,128)(2,1)} %all-gather.4.cloned.1.call-done.refs_10_), channel_id=1, source_target_pairs={{0,64},{64,128},{128,192},{192,0},{1,65},{65,129},{129,193},{193,1... | collective-permute-start | bytes 3145736 | tf_op jit(solution)/shard_map/ppermute | solution.py:355
  153.4 6.5 %collective-permute-done.17.refs_3_ = bf16[256,512]{1,0:T(8,128)(2,1)S(1)} collective-permute-done((bf16[256,512]{1,0:T(8,128)(2,1)S(1)}, bf16[256,512]{1,0:T(8,128)(2,1)S(1)}, u32[]{:S(2)}, u32[]{:S(2)}) %collective-permute-start.17) | collective-permute-done | bytes 262176 | tf_op jit(solution)/shard_map/ppermute | solution.py:355
  159.9 3.3 %collective-permute-start.20 = (bf16[256,512]{1,0:T(8,128)(2,1)S(1)}, bf16[256,512]{1,0:T(8,128)(2,1)S(1)}, u32[]{:S(2)}, u32[]{:S(2)}) collective-permute-start(bf16[256,512]{1,0:T(8,128)(2,1)S(1)} %collective-permute-done.19.refs_6_), channel_id=1, source_target_pairs={{0,56},{8,0},{16,8},{24,16},{32,24},{40,32},{48,40},{56,48},{1,57}... | collective-permute-start | bytes 786440 | tf_op jit(solution)/shard_map/ppermute | solution.py:355
  163.4 6.6 %collective-permute-done.24.refs_12_ = bf16[512,1024]{1,0:T(8,128)(2,1)S(1)} collective-permute-done((bf16[512,1024]{1,0:T(8,128)(2,1)}, bf16[512,1024]{1,0:T(8,128)(2,1)S(1)}, u32[]{:S(2)}, u32[]{:S(2)}) %collective-permute-start.24) | collective-permute-done | bytes 1048608 | tf_op jit(solution)/shard_map/ppermute | solution.py:355
  171.1 3.1 %collective-permute-start.25 = (bf16[256,1024]{1,0:T(8,128)(2,1)}, bf16[256,1024]{1,0:T(8,128)(2,1)S(1)}, u32[]{:S(2)}, u32[]{:S(2)}) collective-permute-start(bf16[256,1024]{1,0:T(8,128)(2,1)} %slice.48), channel_id=1, source_target_pairs={{0,64},{64,128},{128,192},{192,0},{1,65},{65,129},{129,193},{193,1... | collective-permute-start | bytes 1572872 | tf_op jit(solution)/shard_map/ppermute | solution.py:355
  183.2 9.0 %product.1 = f32[375,1500]{1,0:T(8,128)} custom-call(s32[2]{0:T(128)} %pad_add_fusion.xz_ref, f32[2048,1]{1,0:T(8,128)} %copy.40.w_ref, bf16[8,32,8,384]{3,2,1,0:T(8,128)(2,1)} %bitcast.21, bf16[256,512]{1,0:T(8,128)(2,1)} %copy-done.12, bf16[256,512]{1,0:T(8,128)(2,1)} %copy-done.21, bf16[256,512]{1,0:T(8,128)(2,1)} %copy-done.22, ...), custom_call_target="tpu_custom_call" | custom-call | tf_op jit(solution)/shard_map/product/pallas_call | solution.py:314
  (150 shorter events, 38.4 us)
Async XLA Ops:
  6.5 17.8 %collective-permute-start.3 = (bf16[2,12,9216]{2,0,1:T(2,128)(2,1)}, bf16[2,12,9216]{2,0,1:T(2,128)(2,1)S(1)}, u32[]{:S(2)}, u32[]{:S(2)}) collective-permute-start(bf16[2,12,9216]{2,0,1:T(2,128)(2,1)} %param.14), channel_id=1, source_target_pairs={{0,64},{64,128},{128,192},{192,0},{1,65},{65,129},{129,193},{193,1... | collective-permute-start | bytes 1327112 | tf_op jit(solution)/shard_map/ppermute | solution.py:355
  8.7 17.5 %collective-permute-start.4 = (bf16[2,12,9216]{2,0,1:T(2,128)(2,1)}, bf16[2,12,9216]{2,0,1:T(2,128)(2,1)S(1)}, u32[]{:S(2)}, u32[]{:S(2)}) collective-permute-start(bf16[2,12,9216]{2,0,1:T(2,128)(2,1)} %param.14), channel_id=1, source_target_pairs={{0,192},{64,0},{128,64},{192,128},{1,193},{65,1},{129,65},{193,129... | collective-permute-start | bytes 1327112 | tf_op jit(solution)/shard_map/ppermute | solution.py:355
  8.8 12.3 %collective-permute-start = (bf16[1,12,9216]{2,1,0:T(8,128)(2,1)}, bf16[1,12,9216]{2,1,0:T(8,128)(2,1)S(1)}, u32[]{:S(2)}, u32[]{:S(2)}) collective-permute-start(bf16[1,12,9216]{2,1,0:T(8,128)(2,1)} %refs_0_.1), channel_id=1, source_target_pairs={{0,8},{8,16},{16,24},{24,32},{32,40},{40,48},{48,56},{56,0},{1,9},... | collective-permute-start | bytes 663560 | tf_op jit(solution)/shard_map/ppermute | solution.py:355
  10.5 10.6 %collective-permute-start.1 = (bf16[1,12,9216]{2,1,0:T(8,128)(2,1)}, bf16[1,12,9216]{2,1,0:T(8,128)(2,1)S(1)}, u32[]{:S(2)}, u32[]{:S(2)}) collective-permute-start(bf16[1,12,9216]{2,1,0:T(8,128)(2,1)} %refs_0_.1), channel_id=1, source_target_pairs={{0,56},{8,0},{16,8},{24,16},{32,24},{40,32},{48,40},{56,48},{1,57}... | collective-permute-start | bytes 663560 | tf_op jit(solution)/shard_map/ppermute | solution.py:355
  21.1 8.8 %collective-permute-start.2 = (bf16[1,12,9216]{2,1,0:T(8,128)(2,1)S(1)}, bf16[1,12,9216]{2,1,0:T(8,128)(2,1)S(1)}, u32[]{:S(2)}, u32[]{:S(2)}) collective-permute-start(bf16[1,12,9216]{2,1,0:T(8,128)(2,1)S(1)} %collective-permute-done.refs_1_), channel_id=1, source_target_pairs={{0,8},{8,16},{16,24},{24,32},{32,40},{40,48},{48,56},{56,0},{1,9},... | collective-permute-start | bytes 663560 | tf_op jit(solution)/shard_map/ppermute | solution.py:355
  21.1 10.2 %collective-permute-start.7 = (bf16[1,12,9216]{2,1,0:T(8,128)(2,1)S(1)}, bf16[1,12,9216]{2,1,0:T(8,128)(2,1)S(1)}, u32[]{:S(2)}, u32[]{:S(2)}) collective-permute-start(bf16[1,12,9216]{2,1,0:T(8,128)(2,1)S(1)} %collective-permute-done.1.refs_2_), channel_id=1, source_target_pairs={{0,56},{8,0},{16,8},{24,16},{32,24},{40,32},{48,40},{56,48},{1,57}... | collective-permute-start | bytes 663560 | tf_op jit(solution)/shard_map/ppermute | solution.py:355
  24.5 8.6 %collective-permute-start.5 = (bf16[1,12,9216]{2,1,0:T(8,128)(2,1)S(1)}, bf16[1,12,9216]{2,1,0:T(8,128)(2,1)S(1)}, u32[]{:S(2)}, u32[]{:S(2)}) collective-permute-start(bf16[1,12,9216]{2,1,0:T(8,128)(2,1)S(1)} %slice.40), channel_id=1, source_target_pairs={{0,64},{64,128},{128,192},{192,0},{1,65},{65,129},{129,193},{193,1... | collective-permute-start | bytes 663560 | tf_op jit(solution)/shard_map/ppermute | solution.py:355
  29.8 22.0 %collective-permute-start.10 = (bf16[1,12,9216]{2,1,0:T(8,128)(2,1)S(1)}, bf16[1,12,9216]{2,1,0:T(8,128)(2,1)S(1)}, u32[]{:S(2)}, u32[]{:S(2)}) collective-permute-start(bf16[1,12,9216]{2,1,0:T(8,128)(2,1)S(1)} %collective-permute-done.2.refs_3_), channel_id=1, source_target_pairs={{0,16},{8,24},{16,32},{24,40},{32,48},{40,56},{48,0},{56,8},{1,17}... | collective-permute-start | bytes 663560 | tf_op jit(solution)/shard_map/ppermute | solution.py:355
  29.9 22.0 %collective-permute-start.8 = (bf16[1,12,9216]{2,1,0:T(8,128)(2,1)S(1)}, bf16[1,12,9216]{2,1,0:T(8,128)(2,1)S(1)}, u32[]{:S(2)}, u32[]{:S(2)}) collective-permute-start(bf16[1,12,9216]{2,1,0:T(8,128)(2,1)S(1)} %collective-permute-done.2.refs_3_), channel_id=1, source_target_pairs={{0,8},{8,16},{16,24},{24,32},{32,40},{40,48},{48,56},{56,0},{1,9},... | collective-permute-start | bytes 663560 | tf_op jit(solution)/shard_map/ppermute | solution.py:355
  31.3 20.6 %collective-permute-start.9 = (bf16[1,12,9216]{2,1,0:T(8,128)(2,1)S(1)}, bf16[1,12,9216]{2,1,0:T(8,128)(2,1)S(1)}, u32[]{:S(2)}, u32[]{:S(2)}) collective-permute-start(bf16[1,12,9216]{2,1,0:T(8,128)(2,1)S(1)} %collective-permute-done.7.refs_0_), channel_id=1, source_target_pairs={{0,56},{8,0},{16,8},{24,16},{32,24},{40,32},{48,40},{56,48},{1,57}... | collective-permute-start | bytes 663560 | tf_op jit(solution)/shard_map/ppermute | solution.py:355
  46.6 20.8 %all-to-all-start = ((bf16[8,48,1408]{2,1,0:T(8,128)(2,1)}), bf16[8,48,1408]{2,1,0:T(8,128)(2,1)S(1)}, u32[]{:S(2)}, u32[]{:S(2)}) async-start(bf16[8,48,1408]{2,1,0:T(8,128)(2,1)} %spectra.2), calls=%async_computation | async-start | bytes 2162688 | tf_op jit(solution)/shard_map/all_to_all | solution.py:378
  67.4 19.8 %all-to-all-start.1 = ((bf16[8,48,1408]{2,1,0:T(8,128)(2,1)}), bf16[8,48,1408]{2,1,0:T(8,128)(2,1)S(1)}, u32[]{:S(2)}, u32[]{:S(2)}) async-start(bf16[8,48,1408]{2,1,0:T(8,128)(2,1)} %spectra.3), calls=%async_computation.1 | async-start | bytes 2162688 | tf_op jit(solution)/shard_map/all_to_all | solution.py:380
  70.9 75.6 %all-gather.4.cloned.1.call-start = ((), (), s32[]{:S(2)}) async-start(), calls=%async_computation.4 | async-start | bytes 1179648 | tf_op jit(solution)/shard_map/all_gather | solution.py:405
  107.1 75.1 %all-gather.6.cloned.1.call-start = ((), (), s32[]{:S(2)}) async-start(), calls=%async_computation.5 | async-start | bytes 1769472 | tf_op jit(solution)/shard_map/all_gather | solution.py:413
  117.9 8.6 %collective-permute-start.16 = (bf16[256,512]{1,0:T(8,128)(2,1)S(1)}, bf16[256,512]{1,0:T(8,128)(2,1)S(1)}, u32[]{:S(2)}, u32[]{:S(2)}) collective-permute-start(bf16[256,512]{1,0:T(8,128)(2,1)S(1)} %constant_dynamic-update-slice_fusion.refs_1_), channel_id=1, source_target_pairs={{0,56},{8,0},{16,8},{24,16},{32,24},{40,32},{48,40},{56,48},{1,57}... | collective-permute-start | bytes 786440 | tf_op jit(solution)/shard_map/ppermute | solution.py:355
  118.9 10.8 %collective-permute-start.15 = (bf16[256,512]{1,0:T(8,128)(2,1)S(1)}, bf16[256,512]{1,0:T(8,128)(2,1)S(1)}, u32[]{:S(2)}, u32[]{:S(2)}) collective-permute-start(bf16[256,512]{1,0:T(8,128)(2,1)S(1)} %constant_dynamic-update-slice_fusion.refs_1_), channel_id=1, source_target_pairs={{0,8},{8,16},{16,24},{24,32},{32,40},{40,48},{48,56},{56,0},{1,9},... | collective-permute-start | bytes 786440 | tf_op jit(solution)/shard_map/ppermute | solution.py:355
  146.5 23.5 %collective-permute-start.24 = (bf16[512,1024]{1,0:T(8,128)(2,1)}, bf16[512,1024]{1,0:T(8,128)(2,1)S(1)}, u32[]{:S(2)}, u32[]{:S(2)}) collective-permute-start(bf16[512,1024]{1,0:T(8,128)(2,1)} %all-gather.4.cloned.1.call-done.refs_10_), channel_id=1, source_target_pairs={{0,192},{64,0},{128,64},{192,128},{1,193},{65,1},{129,65},{193,129... | collective-permute-start | bytes 3145736 | tf_op jit(solution)/shard_map/ppermute | solution.py:355
  147.2 22.9 %collective-permute-start.23 = (bf16[512,1024]{1,0:T(8,128)(2,1)}, bf16[512,1024]{1,0:T(8,128)(2,1)S(1)}, u32[]{:S(2)}, u32[]{:S(2)}) collective-permute-start(bf16[512,1024]{1,0:T(8,128)(2,1)} %all-gather.4.cloned.1.call-done.refs_10_), channel_id=1, source_target_pairs={{0,64},{64,128},{128,192},{192,0},{1,65},{65,129},{129,193},{193,1... | collective-permute-start | bytes 3145736 | tf_op jit(solution)/shard_map/ppermute | solution.py:355
  149.8 10.0 %collective-permute-start.17 = (bf16[256,512]{1,0:T(8,128)(2,1)S(1)}, bf16[256,512]{1,0:T(8,128)(2,1)S(1)}, u32[]{:S(2)}, u32[]{:S(2)}) collective-permute-start(bf16[256,512]{1,0:T(8,128)(2,1)S(1)} %collective-permute-done.15.refs_2_), channel_id=1, source_target_pairs={{0,8},{8,16},{16,24},{24,32},{32,40},{40,48},{48,56},{56,0},{1,9},... | collective-permute-start | bytes 786440 | tf_op jit(solution)/shard_map/ppermute | solution.py:355
  151.5 8.3 %collective-permute-start.19 = (bf16[256,512]{1,0:T(8,128)(2,1)S(1)}, bf16[256,512]{1,0:T(8,128)(2,1)S(1)}, u32[]{:S(2)}, u32[]{:S(2)}) collective-permute-start(bf16[256,512]{1,0:T(8,128)(2,1)S(1)} %collective-permute-done.16.refs_5_), channel_id=1, source_target_pairs={{0,56},{8,0},{16,8},{24,16},{32,24},{40,32},{48,40},{56,48},{1,57}... | collective-permute-start | bytes 786440 | tf_op jit(solution)/shard_map/ppermute | solution.py:355
  159.9 14.6 %collective-permute-start.18 = (bf16[256,512]{1,0:T(8,128)(2,1)S(1)}, bf16[256,512]{1,0:T(8,128)(2,1)S(1)}, u32[]{:S(2)}, u32[]{:S(2)}) collective-permute-start(bf16[256,512]{1,0:T(8,128)(2,1)S(1)} %collective-permute-done.17.refs_3_), channel_id=1, source_target_pairs={{0,8},{8,16},{16,24},{24,32},{32,40},{40,48},{48,56},{56,0},{1,9},... | collective-permute-start | bytes 786440 | tf_op jit(solution)/shard_map/ppermute | solution.py:355
  159.9 16.4 %collective-permute-start.20 = (bf16[256,512]{1,0:T(8,128)(2,1)S(1)}, bf16[256,512]{1,0:T(8,128)(2,1)S(1)}, u32[]{:S(2)}, u32[]{:S(2)}) collective-permute-start(bf16[256,512]{1,0:T(8,128)(2,1)S(1)} %collective-permute-done.19.refs_6_), channel_id=1, source_target_pairs={{0,56},{8,0},{16,8},{24,16},{32,24},{40,32},{48,40},{56,48},{1,57}... | collective-permute-start | bytes 786440 | tf_op jit(solution)/shard_map/ppermute | solution.py:355
  170.0 12.1 %collective-permute-start.26 = (bf16[256,1024]{1,0:T(8,128)(2,1)S(1)}, bf16[256,1024]{1,0:T(8,128)(2,1)S(1)}, u32[]{:S(2)}, u32[]{:S(2)}) collective-permute-start(bf16[256,1024]{1,0:T(8,128)(2,1)S(1)} %slice.49), channel_id=1, source_target_pairs={{0,192},{64,0},{128,64},{192,128},{1,193},{65,1},{129,65},{193,129... | collective-permute-start | bytes 1572872 | tf_op jit(solution)/shard_map/ppermute | solution.py:355
  171.1 11.1 %collective-permute-start.25 = (bf16[256,1024]{1,0:T(8,128)(2,1)}, bf16[256,1024]{1,0:T(8,128)(2,1)S(1)}, u32[]{:S(2)}, u32[]{:S(2)}) collective-permute-start(bf16[256,1024]{1,0:T(8,128)(2,1)} %slice.48), channel_id=1, source_target_pairs={{0,64},{64,128},{128,192},{192,0},{1,65},{65,129},{129,193},{193,1... | collective-permute-start | bytes 1572872 | tf_op jit(solution)/shard_map/ppermute | solution.py:355
  (41 other events, 625.0 us)
Sparse Core Ops, SparseCore 0:
  107.2 37.3 all-gather.3
  146.6 25.4 all-gather.5

commit v3 on v2

--- a/solution.py
+++ b/solution.py
@@ -26,9 +26,11 @@
 QC = 4
 SLOTS = ((0, 1, 7, 2), (6, 3, 5, 4))
 ROWS = SLAB * VC * SB
-ZOUT = HALF * 16
+ZGRP = 384
+ZOUT = HALF * 8
 YSTEP = 768
 NSTEP = GRID * GRID // YSTEP
+NCUT = 4
 BTILE = 128
 NBT = 5
 KWIN = 5
@@ -61,15 +63,15 @@
 
 def depth_block():
     depth, _ = tables()
-    out = np.zeros((2, 4, GRID, HALF, 2, 2, 4), np.float64)
-    for h in range(2):
-        for y in range(4):
-            out[h, y, :, :, h, :, y] = depth.transpose(0, 2, 1)
-    return out.reshape(YSTEP, ZOUT).astype(ml_dtypes.bfloat16)
+    out = np.zeros((4, GRID, HALF, 2, 4), np.float64)
+    for y in range(4):
+        out[y, :, :, :, y] = depth.transpose(0, 2, 1)
+    return out.reshape(ZGRP, ZOUT).astype(ml_dtypes.bfloat16)
 
 
 def window(n):
-    return min((BTILE * n) // KEPT, HALF - KWIN)
+    first = BTILE * n // KEPT
+    return first, min((BTILE * n + BTILE - 1) // KEPT, HALF - 1) + 1 - first
 
 
 def plane_block():
@@ -81,7 +83,7 @@
             k, j = divmod(b, KEPT)
             n, r = divmod(b, BTILE)
             row = n * 2 * BTILE + d * (BTILE if n < NBT else 64) + r
-            out[row, k - window(n)] = perk[d, j]
+            out[row, k - window(n)[0]] = perk[d, j]
     return out.reshape(YL, KWIN * 2 * GRID).astype(ml_dtypes.bfloat16)
 
 
@@ -106,10 +108,13 @@
     n = VC + NX + 3
     o_ref, dens, zs, sems = refs[n], *refs[2 * n + 1 :]
     spaces = refs[n + 1 : 2 * n + 1]
-    copies = copy_in(refs[:n], spaces, sems)
     v_refs, c_refs, (t_ref, w_ref) = spaces[:VC], spaces[VC : n - 2], spaces[n - 2 :]
-    for copy in copies[:-1]:
-        copy.wait()
+    tables = copy_in(refs[n - 2 : n], spaces[n - 2 :], sems.at[NCUT])
+    cuts = []
+    for cut in range(NCUT):
+        lanes = pl.ds(cut * (GRID * GRID // NCUT), GRID * GRID // NCUT)
+        cuts.append(copy_in([r.at[:, :, lanes] for r in refs[: n - 2]], [r.at[:, :, lanes] for r in spaces[: n - 2]], sems.at[cut]))
+    tables[0].wait()
 
     def body(step, _):
         lanes = pl.ds(pl.multiple_of(step * YSTEP, YSTEP), YSTEP)
@@ -130,19 +135,25 @@
             for h in range(2):
                 r0 = (v * 2 + h) * SLAB * QC
                 dens[r0 : r0 + SLAB * QC, :] = val * cond[h]
-        z = jnp.dot(dens[...], t_ref[...], preferred_element_type=F32).astype(BF)
-        zs[:, pl.ds(pl.multiple_of(step * 16, 16), 16), :] = z.T.reshape(HALF, 16, ROWS)
+        groups = []
+        for sub in range(YSTEP // ZGRP):
+            z = jnp.dot(dens[:, sub * ZGRP : (sub + 1) * ZGRP], t_ref[...], preferred_element_type=F32)
+            groups.append(z.T.reshape(HALF, 8, ROWS))
+        zs[:, pl.ds(pl.multiple_of(step * 16, 16), 16), :] = jnp.concatenate(groups, axis=1).astype(BF)
         return 0
 
-    lax.fori_loop(0, NSTEP, body, 0)
-    copies[-1].wait()
+    for cut in range(NCUT):
+        for copy in cuts[cut]:
+            copy.wait()
+        lax.fori_loop(cut * (NSTEP // NCUT), (cut + 1) * (NSTEP // NCUT), body, 0)
+    tables[1].wait()
     for n in range(NBT + 1):
         r0 = n * 2 * BTILE
         rows = 2 * BTILE if n < NBT else BTILE
-        k0 = window(n)
-        zk = zs[k0 : k0 + KWIN].reshape(KWIN * 2 * GRID, ROWS)
-        y = jnp.dot(w_ref[r0 : r0 + rows, :], zk, preferred_element_type=F32)
-        yt = y.astype(BF).T.reshape(NT, SLAB * QC, rows)
+        k0, width = window(n)
+        zk = zs[k0 : k0 + width].reshape(width * 2 * GRID, ROWS)
+        y = jnp.dot(w_ref[r0 : r0 + rows, : width * 2 * GRID], zk, preferred_element_type=F32)
+        yt = y.T.astype(BF).reshape(NT, SLAB * QC, rows)
         if n < NBT - 1:
             l0 = n // 2 * 512 + n % 2 * BTILE
             o_ref[:, :, l0 : l0 + BTILE] = yt[:, :, :BTILE]
@@ -162,7 +173,7 @@
         + [
             pltpu.VMEM((ROWS, YSTEP), BF),
             pltpu.VMEM((HALF, 2 * GRID, ROWS), BF),
-            pltpu.SemaphoreType.DMA((len(operands),)),
+            pltpu.SemaphoreType.DMA((NCUT + 1, len(operands) - 2)),
         ],
         compiler_params=pltpu.CompilerParams(vmem_limit_bytes=58 * 2**20),
         name="spectra",
@@ -287,8 +298,6 @@
     for p in range(32):
         rows = jnp.concatenate([r_ref[t, p].astype(F32) for t in range(NT)], axis=0)
         wr[p] = (rows * w_ref[KP * p : KP * (p + 1), :]).astype(BF)
-    for copy in copies[1:]:
-        copy.wait()
 
     def part(pieces, ref, z_of):
         lhs = [wr[lax.rem(xz_ref[0] + (NX - dx), NX) * NZ + z_of(dz)] for dx, dz in pieces]
@@ -296,14 +305,16 @@
             jnp.concatenate(lhs, axis=0), ref[...], (((0,), (0,)), ((), ())), preferred_element_type=F32
         )
 
-    def total(pieces, operands, z_of):
-        acc = part(pieces[0], operands[0], z_of)
-        for piece, ref in zip(pieces[1:], operands[1:]):
-            acc += part(piece, ref, z_of)
+    def total(pieces, operands, waits, z_of):
+        acc = None
+        for piece, ref, copy in zip(pieces, operands, waits):
+            copy.wait()
+            more = part(piece, ref, z_of)
+            acc = more if acc is None else acc + more
         return acc
 
-    acc_ref[:, :LA] = total(a_pieces(), a_refs, lambda dz: lax.rem(xz_ref[1] + (NZ - dz), NZ))
-    acc_ref[:, LA:] = total(b_pieces(), b_refs, lambda z: z)
+    acc_ref[:, :LA] = total(a_pieces(), a_refs, copies[1 : 1 + na], lambda dz: lax.rem(xz_ref[1] + (NZ - dz), NZ))
+    acc_ref[:, LA:] = total(b_pieces(), b_refs, copies[1 + na :], lambda z: z)
     for q in range(4):
         o_ref[:, 375 * q : 375 * (q + 1)] = acc_ref[:375, RB * q : RB * q + 375]
 

time: 201 us -> 200 us (level)
  no operation moved by 1% of the time
where the time goes in v3:
time: 200 us; the launch traced here: 198 us
  Pallas kernels  49.9 us (25%)
  starting transfers between devices  49.8 us (25%)
  waiting for transfers between devices  47.9 us (24%)
  blocking collectives  26 us (13%)
  between operations  14 us (7%)
  local copies, waits for them, and re-layouts  8.5 us (4%)
  other arithmetic  2.35 us (1%)
    ppermute x27, starting transfers between devices, shift(): lax.ppermute(value, axis, [(i, (i + step) % size) for i in range(size)])  41.7 us
    ppermute x27, waiting for transfers between devices, shift(): lax.ppermute(value, axis, [(i, (i + step) % size) for i in range(size)])  38.6 us
    pallas_call x2, Pallas kernels, spectra(): pl.pallas_call(spectra_kernel, in_specs=[pl.BlockSpec(memory_space=pl.ANY...  21.6 us
    all_to_all x1, blocking collectives, per_device(): lax.all_to_all(for_rows, ('x', 'z'), split_axis=0, concat_axis=0, tiled=T...  16.6 us
    all_to_all x1, blocking collectives, per_device(): lax.all_to_all(cols, tile, split_axis=0, concat_axis=0, tiled=True)  9.36 us
    pallas_call x1, Pallas kernels, pick_second(): pl.pallas_call(second_kernel, grid=(GP // GCH,), in_specs=pick_specs() +...  8.99 us
    pallas_call x1, Pallas kernels, pick_first(): pl.pallas_call(first_kernel, grid=(GP // GCH,), in_specs=pick_specs(), ou...  8.96 us
    pallas_call x1, Pallas kernels, product(): pl.pallas_call(product_kernel, in_specs=[pl.BlockSpec(memory_space=pltpu....  8.7 us
  transfers between devices with their start and end apart: 31, of which 14 were waited for; matrix products, arithmetic and copies ran while one was open for 3% of the time, Pallas kernels for 16%

profile of v3, /device:TPU:6, one launch (start us, length us, event | category | flops | bytes accessed | tf_op | source)
XLA Modules:
  0.0 198.4 jit_solution(10774079530650362293)
XLA Ops:
  10.5 3.9 %collective-permute-start.1 = (bf16[1,12,9216]{2,1,0:T(8,128)(2,1)}, bf16[1,12,9216]{2,1,0:T(8,128)(2,1)S(1)}, u32[]{:S(2)}, u32[]{:S(2)}) collective-permute-start(bf16[1,12,9216]{2,1,0:T(8,128)(2,1)} %refs_0_.1), channel_id=1, source_target_pairs={{0,56},{8,0},{16,8},{24,16},{32,24},{40,32},{48,40},{56,48},{1,57}... | collective-permute-start | bytes 663560 | tf_op jit(solution)/shard_map/ppermute | solution.py:366
  14.4 6.7 %collective-permute-done.refs_1_ = bf16[1,12,9216]{2,1,0:T(8,128)(2,1)S(1)} collective-permute-done((bf16[1,12,9216]{2,1,0:T(8,128)(2,1)}, bf16[1,12,9216]{2,1,0:T(8,128)(2,1)S(1)}, u32[]{:S(2)}, u32[]{:S(2)}) %collective-permute-start) | collective-permute-done | bytes 221216 | tf_op jit(solution)/shard_map/ppermute | solution.py:366
  21.1 3.2 %collective-permute-start.7 = (bf16[1,12,9216]{2,1,0:T(8,128)(2,1)S(1)}, bf16[1,12,9216]{2,1,0:T(8,128)(2,1)S(1)}, u32[]{:S(2)}, u32[]{:S(2)}) collective-permute-start(bf16[1,12,9216]{2,1,0:T(8,128)(2,1)S(1)} %collective-permute-done.1.refs_2_), channel_id=1, source_target_pairs={{0,56},{8,0},{16,8},{24,16},{32,24},{40,32},{48,40},{56,48},{1,57}... | collective-permute-start | bytes 663560 | tf_op jit(solution)/shard_map/ppermute | solution.py:366
  35.1 10.9 %spectra.2 = bf16[8,48,1408]{2,1,0:T(8,128)(2,1)} custom-call(bf16[1,12,9216]{2,1,0:T(8,128)(2,1)} %refs_0_.1, bf16[1,12,9216]{2,1,0:T(8,128)(2,1)} %copy-done.15, bf16[1,12,9216]{2,1,0:T(8,128)(2,1)} %copy-done.16, bf16[1,12,9216]{2,1,0:T(8,128)(2,1)} %copy-done.14, bf16[2,12,9216]{2,1,0:T(8,128)(2,1)} %copy.34.refs_4_, bf16[2,12,9216]{2,1,0:T(8,128)(2,1)} %copy-done.1, ...), custom_call_target="tpu_custom_call" | custom-call | tf_op jit(solution)/shard_map/spectra/pallas_call | solution.py:167
  46.0 4.5 %all-to-all-start = ((bf16[8,48,1408]{2,1,0:T(8,128)(2,1)}), bf16[8,48,1408]{2,1,0:T(8,128)(2,1)S(1)}, u32[]{:S(2)}, u32[]{:S(2)}) async-start(bf16[8,48,1408]{2,1,0:T(8,128)(2,1)} %spectra.2), calls=%async_computation | async-start | bytes 2162688 | tf_op jit(solution)/shard_map/all_to_all | solution.py:389
  52.9 10.8 %spectra.3 = bf16[8,48,1408]{2,1,0:T(8,128)(2,1)} custom-call(bf16[1,12,9216]{2,1,0:T(8,128)(2,1)} %copy-done.13, bf16[1,12,9216]{2,1,0:T(8,128)(2,1)} %copy-done.18, bf16[1,12,9216]{2,1,0:T(8,128)(2,1)} %copy-done.19, bf16[1,12,9216]{2,1,0:T(8,128)(2,1)} %copy-done.17, bf16[2,12,9216]{2,1,0:T(8,128)(2,1)} %copy.34.refs_4_, bf16[2,12,9216]{2,1,0:T(8,128)(2,1)} %copy-done.1, ...), custom_call_target="tpu_custom_call" | custom-call | tf_op jit(solution)/shard_map/spectra/pallas_call | solution.py:167
  63.7 3.1 %all-to-all-done = bf16[8,48,1408]{2,1,0:T(8,128)(2,1)S(1)} async-done(((bf16[8,48,1408]{2,1,0:T(8,128)(2,1)}), bf16[8,48,1408]{2,1,0:T(8,128)(2,1)S(1)}, u32[]{:S(2)}, u32[]{:S(2)}) %all-to-all-start) | async-done | bytes 1081376 | tf_op jit(solution)/shard_map/all_to_all | solution.py:389
  66.8 3.6 %all-to-all-start.1 = ((bf16[8,48,1408]{2,1,0:T(8,128)(2,1)}), bf16[8,48,1408]{2,1,0:T(8,128)(2,1)S(1)}, u32[]{:S(2)}, u32[]{:S(2)}) async-start(bf16[8,48,1408]{2,1,0:T(8,128)(2,1)} %spectra.3), calls=%async_computation.1 | async-start | bytes 2162688 | tf_op jit(solution)/shard_map/all_to_all | solution.py:391
  71.6 9.0 %pick_first.1.first_ref = f32[8,12288]{1,0:T(8,128)S(1)} custom-call(bf16[888,256]{1,0:T(8,128)(2,1)S(1)} %lines.3.s_ref, s32[1,12288]{1,0:T(1,128)S(1)} %multiply_add_fusion.a_ref, s32[1,12288]{1,0:T(1,128)S(1)} %get-tuple-element.19.b_ref), custom_call_target="tpu_custom_call" | custom-call | tf_op jit(solution)/shard_map/pick_first/pallas_call | solution.py:245
  80.6 6.0 %all-to-all-done.1 = bf16[8,48,1408]{2,1,0:T(8,128)(2,1)S(1)} async-done(((bf16[8,48,1408]{2,1,0:T(8,128)(2,1)}), bf16[8,48,1408]{2,1,0:T(8,128)(2,1)S(1)}, u32[]{:S(2)}, u32[]{:S(2)}) %all-to-all-start.1) | async-done | bytes 1081376 | tf_op jit(solution)/shard_map/all_to_all | solution.py:391
  87.4 9.0 %pick_second.1 = (bf16[8,8,1536]{2,1,0:T(8,128)(2,1)S(1)}, bf16[32,8,384]{2,1,0:T(8,128)(2,1)S(1)}) custom-call(bf16[888,256]{1,0:T(8,128)(2,1)S(1)} %lines.2.s_ref, s32[1,12288]{1,0:T(1,128)S(1)} %multiply_add_fusion.a_ref, s32[1,12288]{1,0:T(1,128)S(1)} %get-tuple-element.19.b_ref, f32[8,12288]{1,0:T(8,128)S(1)} %pick_first.1.first_ref), custom_call_target="tpu_custom_call" | custom-call | tf_op jit(solution)/shard_map/pick_second/pallas_call | solution.py:258
  96.5 9.4 %all_to_all.20 = bf16[8,8,1536]{2,1,0:T(8,128)(2,1)S(1)} all-to-all(bf16[8,8,1536]{2,1,0:T(8,128)(2,1)S(1)} %get-tuple-element.15), channel_id=1, replica_groups=mesh['x'=4,'z'=8,'y'=4,'core'=2] {'y','core'}, dimensions={0} | all-to-all | bytes 393216 | tf_op jit(solution)/shard_map/all_to_all | solution.py:415
  106.9 3.0 %collective-permute-start.11 = (bf16[64,512]{1,0:T(8,128)(2,1)S(1)}, bf16[64,512]{1,0:T(8,128)(2,1)S(1)}, u32[]{:S(2)}, u32[]{:S(2)}) collective-permute-start(bf16[64,512]{1,0:T(8,128)(2,1)S(1)} %get-tuple-element.21), channel_id=1, source_target_pairs={{0,64},{64,128},{128,192},{192,0},{1,65},{65,129},{129,193},{193,1... | collective-permute-start | bytes 196616 | tf_op jit(solution)/shard_map/ppermute | solution.py:366
  109.9 2.2 %collective-permute-done.12 = bf16[64,512]{1,0:T(8,128)(2,1)S(1)} collective-permute-done((bf16[64,512]{1,0:T(8,128)(2,1)S(1)}, bf16[64,512]{1,0:T(8,128)(2,1)S(1)}, u32[]{:S(2)}, u32[]{:S(2)}) %collective-permute-start.12) | collective-permute-done | bytes 65568 | tf_op jit(solution)/shard_map/ppermute | solution.py:366
  112.2 3.2 %collective-permute-start.13 = (bf16[32,512]{1,0:T(8,128)(2,1)S(1)}, bf16[32,512]{1,0:T(8,128)(2,1)S(1)}, u32[]{:S(2)}, u32[]{:S(2)}) collective-permute-start(bf16[32,512]{1,0:T(8,128)(2,1)S(1)} %slice.43), channel_id=1, source_target_pairs={{0,64},{64,128},{128,192},{192,0},{1,65},{65,129},{129,193},{193,1... | collective-permute-start | bytes 98312 | tf_op jit(solution)/shard_map/ppermute | solution.py:366
  119.3 6.6 %collective-permute-done.16.refs_5_ = bf16[256,512]{1,0:T(8,128)(2,1)S(1)} collective-permute-done((bf16[256,512]{1,0:T(8,128)(2,1)S(1)}, bf16[256,512]{1,0:T(8,128)(2,1)S(1)}, u32[]{:S(2)}, u32[]{:S(2)}) %collective-permute-start.16) | collective-permute-done | bytes 262176 | tf_op jit(solution)/shard_map/ppermute | solution.py:366
  125.9 3.2 %collective-permute-done.15.refs_2_ = bf16[256,512]{1,0:T(8,128)(2,1)S(1)} collective-permute-done((bf16[256,512]{1,0:T(8,128)(2,1)S(1)}, bf16[256,512]{1,0:T(8,128)(2,1)S(1)}, u32[]{:S(2)}, u32[]{:S(2)}) %collective-permute-start.15) | collective-permute-done | bytes 262176 | tf_op jit(solution)/shard_map/ppermute | solution.py:366
  129.2 16.6 %all_to_all.21 = bf16[32,8,384]{2,1,0:T(8,128)(2,1)} all-to-all(bf16[32,8,384]{2,1,0:T(8,128)(2,1)S(1)} %get-tuple-element.16), channel_id=1, replica_groups=mesh['x'=4,'z'=8,'y'=4,'core'=2] {'x','z'}, dimensions={0} | all-to-all | bytes 393216 | tf_op jit(solution)/shard_map/all_to_all | solution.py:423
  146.8 2.5 %collective-permute-start.23 = (bf16[512,1024]{1,0:T(8,128)(2,1)}, bf16[512,1024]{1,0:T(8,128)(2,1)S(1)}, u32[]{:S(2)}, u32[]{:S(2)}) collective-permute-start(bf16[512,1024]{1,0:T(8,128)(2,1)} %all-gather.4.cloned.1.call-done.refs_10_), channel_id=1, source_target_pairs={{0,64},{64,128},{128,192},{192,0},{1,65},{65,129},{129,193},{193,1... | collective-permute-start | bytes 3145736 | tf_op jit(solution)/shard_map/ppermute | solution.py:366
  152.9 6.4 %collective-permute-done.17.refs_3_ = bf16[256,512]{1,0:T(8,128)(2,1)S(1)} collective-permute-done((bf16[256,512]{1,0:T(8,128)(2,1)S(1)}, bf16[256,512]{1,0:T(8,128)(2,1)S(1)}, u32[]{:S(2)}, u32[]{:S(2)}) %collective-permute-start.17) | collective-permute-done | bytes 262176 | tf_op jit(solution)/shard_map/ppermute | solution.py:366
  159.4 3.3 %collective-permute-start.20 = (bf16[256,512]{1,0:T(8,128)(2,1)S(1)}, bf16[256,512]{1,0:T(8,128)(2,1)S(1)}, u32[]{:S(2)}, u32[]{:S(2)}) collective-permute-start(bf16[256,512]{1,0:T(8,128)(2,1)S(1)} %collective-permute-done.19.refs_6_), channel_id=1, source_target_pairs={{0,56},{8,0},{16,8},{24,16},{32,24},{40,32},{48,40},{56,48},{1,57}... | collective-permute-start | bytes 786440 | tf_op jit(solution)/shard_map/ppermute | solution.py:366
  162.9 6.7 %collective-permute-done.24.refs_12_ = bf16[512,1024]{1,0:T(8,128)(2,1)S(1)} collective-permute-done((bf16[512,1024]{1,0:T(8,128)(2,1)}, bf16[512,1024]{1,0:T(8,128)(2,1)S(1)}, u32[]{:S(2)}, u32[]{:S(2)}) %collective-permute-start.24) | collective-permute-done | bytes 1048608 | tf_op jit(solution)/shard_map/ppermute | solution.py:366
  170.7 3.1 %collective-permute-start.25 = (bf16[256,1024]{1,0:T(8,128)(2,1)}, bf16[256,1024]{1,0:T(8,128)(2,1)S(1)}, u32[]{:S(2)}, u32[]{:S(2)}) collective-permute-start(bf16[256,1024]{1,0:T(8,128)(2,1)} %slice.48), channel_id=1, source_target_pairs={{0,64},{64,128},{128,192},{192,0},{1,65},{65,129},{129,193},{193,1... | collective-permute-start | bytes 1572872 | tf_op jit(solution)/shard_map/ppermute | solution.py:366
  182.9 8.7 %product.1 = f32[375,1500]{1,0:T(8,128)} custom-call(s32[2]{0:T(128)} %pad_add_fusion.xz_ref, f32[2048,1]{1,0:T(8,128)} %copy.40.w_ref, bf16[8,32,8,384]{3,2,1,0:T(8,128)(2,1)} %bitcast.21, bf16[256,512]{1,0:T(8,128)(2,1)} %copy-done.12, bf16[256,512]{1,0:T(8,128)(2,1)} %copy-done.21, bf16[256,512]{1,0:T(8,128)(2,1)} %copy-done.22, ...), custom_call_target="tpu_custom_call" | custom-call | tf_op jit(solution)/shard_map/product/pallas_call | solution.py:325
  (150 shorter events, 38.8 us)
Async XLA Ops:
  6.5 17.8 %collective-permute-start.3 = (bf16[2,12,9216]{2,0,1:T(2,128)(2,1)}, bf16[2,12,9216]{2,0,1:T(2,128)(2,1)S(1)}, u32[]{:S(2)}, u32[]{:S(2)}) collective-permute-start(bf16[2,12,9216]{2,0,1:T(2,128)(2,1)} %param.14), channel_id=1, source_target_pairs={{0,64},{64,128},{128,192},{192,0},{1,65},{65,129},{129,193},{193,1... | collective-permute-start | bytes 1327112 | tf_op jit(solution)/shard_map/ppermute | solution.py:366
  8.7 17.5 %collective-permute-start.4 = (bf16[2,12,9216]{2,0,1:T(2,128)(2,1)}, bf16[2,12,9216]{2,0,1:T(2,128)(2,1)S(1)}, u32[]{:S(2)}, u32[]{:S(2)}) collective-permute-start(bf16[2,12,9216]{2,0,1:T(2,128)(2,1)} %param.14), channel_id=1, source_target_pairs={{0,192},{64,0},{128,64},{192,128},{1,193},{65,1},{129,65},{193,129... | collective-permute-start | bytes 1327112 | tf_op jit(solution)/shard_map/ppermute | solution.py:366
  8.8 12.3 %collective-permute-start = (bf16[1,12,9216]{2,1,0:T(8,128)(2,1)}, bf16[1,12,9216]{2,1,0:T(8,128)(2,1)S(1)}, u32[]{:S(2)}, u32[]{:S(2)}) collective-permute-start(bf16[1,12,9216]{2,1,0:T(8,128)(2,1)} %refs_0_.1), channel_id=1, source_target_pairs={{0,8},{8,16},{16,24},{24,32},{32,40},{40,48},{48,56},{56,0},{1,9},... | collective-permute-start | bytes 663560 | tf_op jit(solution)/shard_map/ppermute | solution.py:366
  10.5 10.6 %collective-permute-start.1 = (bf16[1,12,9216]{2,1,0:T(8,128)(2,1)}, bf16[1,12,9216]{2,1,0:T(8,128)(2,1)S(1)}, u32[]{:S(2)}, u32[]{:S(2)}) collective-permute-start(bf16[1,12,9216]{2,1,0:T(8,128)(2,1)} %refs_0_.1), channel_id=1, source_target_pairs={{0,56},{8,0},{16,8},{24,16},{32,24},{40,32},{48,40},{56,48},{1,57}... | collective-permute-start | bytes 663560 | tf_op jit(solution)/shard_map/ppermute | solution.py:366
  21.1 8.8 %collective-permute-start.2 = (bf16[1,12,9216]{2,1,0:T(8,128)(2,1)S(1)}, bf16[1,12,9216]{2,1,0:T(8,128)(2,1)S(1)}, u32[]{:S(2)}, u32[]{:S(2)}) collective-permute-start(bf16[1,12,9216]{2,1,0:T(8,128)(2,1)S(1)} %collective-permute-done.refs_1_), channel_id=1, source_target_pairs={{0,8},{8,16},{16,24},{24,32},{32,40},{40,48},{48,56},{56,0},{1,9},... | collective-permute-start | bytes 663560 | tf_op jit(solution)/shard_map/ppermute | solution.py:366
  21.1 10.2 %collective-permute-start.7 = (bf16[1,12,9216]{2,1,0:T(8,128)(2,1)S(1)}, bf16[1,12,9216]{2,1,0:T(8,128)(2,1)S(1)}, u32[]{:S(2)}, u32[]{:S(2)}) collective-permute-start(bf16[1,12,9216]{2,1,0:T(8,128)(2,1)S(1)} %collective-permute-done.1.refs_2_), channel_id=1, source_target_pairs={{0,56},{8,0},{16,8},{24,16},{32,24},{40,32},{48,40},{56,48},{1,57}... | collective-permute-start | bytes 663560 | tf_op jit(solution)/shard_map/ppermute | solution.py:366
  24.5 8.6 %collective-permute-start.5 = (bf16[1,12,9216]{2,1,0:T(8,128)(2,1)S(1)}, bf16[1,12,9216]{2,1,0:T(8,128)(2,1)S(1)}, u32[]{:S(2)}, u32[]{:S(2)}) collective-permute-start(bf16[1,12,9216]{2,1,0:T(8,128)(2,1)S(1)} %slice.40), channel_id=1, source_target_pairs={{0,64},{64,128},{128,192},{192,0},{1,65},{65,129},{129,193},{193,1... | collective-permute-start | bytes 663560 | tf_op jit(solution)/shard_map/ppermute | solution.py:366
  29.8 21.4 %collective-permute-start.10 = (bf16[1,12,9216]{2,1,0:T(8,128)(2,1)S(1)}, bf16[1,12,9216]{2,1,0:T(8,128)(2,1)S(1)}, u32[]{:S(2)}, u32[]{:S(2)}) collective-permute-start(bf16[1,12,9216]{2,1,0:T(8,128)(2,1)S(1)} %collective-permute-done.2.refs_3_), channel_id=1, source_target_pairs={{0,16},{8,24},{16,32},{24,40},{32,48},{40,56},{48,0},{56,8},{1,17}... | collective-permute-start | bytes 663560 | tf_op jit(solution)/shard_map/ppermute | solution.py:366
  29.9 21.4 %collective-permute-start.8 = (bf16[1,12,9216]{2,1,0:T(8,128)(2,1)S(1)}, bf16[1,12,9216]{2,1,0:T(8,128)(2,1)S(1)}, u32[]{:S(2)}, u32[]{:S(2)}) collective-permute-start(bf16[1,12,9216]{2,1,0:T(8,128)(2,1)S(1)} %collective-permute-done.2.refs_3_), channel_id=1, source_target_pairs={{0,8},{8,16},{16,24},{24,32},{32,40},{40,48},{48,56},{56,0},{1,9},... | collective-permute-start | bytes 663560 | tf_op jit(solution)/shard_map/ppermute | solution.py:366
  31.3 20.0 %collective-permute-start.9 = (bf16[1,12,9216]{2,1,0:T(8,128)(2,1)S(1)}, bf16[1,12,9216]{2,1,0:T(8,128)(2,1)S(1)}, u32[]{:S(2)}, u32[]{:S(2)}) collective-permute-start(bf16[1,12,9216]{2,1,0:T(8,128)(2,1)S(1)} %collective-permute-done.7.refs_0_), channel_id=1, source_target_pairs={{0,56},{8,0},{16,8},{24,16},{32,24},{40,32},{48,40},{56,48},{1,57}... | collective-permute-start | bytes 663560 | tf_op jit(solution)/shard_map/ppermute | solution.py:366
  46.0 20.8 %all-to-all-start = ((bf16[8,48,1408]{2,1,0:T(8,128)(2,1)}), bf16[8,48,1408]{2,1,0:T(8,128)(2,1)S(1)}, u32[]{:S(2)}, u32[]{:S(2)}) async-start(bf16[8,48,1408]{2,1,0:T(8,128)(2,1)} %spectra.2), calls=%async_computation | async-start | bytes 2162688 | tf_op jit(solution)/shard_map/all_to_all | solution.py:389
  66.8 19.8 %all-to-all-start.1 = ((bf16[8,48,1408]{2,1,0:T(8,128)(2,1)}), bf16[8,48,1408]{2,1,0:T(8,128)(2,1)S(1)}, u32[]{:S(2)}, u32[]{:S(2)}) async-start(bf16[8,48,1408]{2,1,0:T(8,128)(2,1)} %spectra.3), calls=%async_computation.1 | async-start | bytes 2162688 | tf_op jit(solution)/shard_map/all_to_all | solution.py:391
  70.4 75.5 %all-gather.4.cloned.1.call-start = ((), (), s32[]{:S(2)}) async-start(), calls=%async_computation.4 | async-start | bytes 1179648 | tf_op jit(solution)/shard_map/all_gather | solution.py:416
  106.5 75.3 %all-gather.6.cloned.1.call-start = ((), (), s32[]{:S(2)}) async-start(), calls=%async_computation.5 | async-start | bytes 1769472 | tf_op jit(solution)/shard_map/all_gather | solution.py:424
  117.3 8.6 %collective-permute-start.16 = (bf16[256,512]{1,0:T(8,128)(2,1)S(1)}, bf16[256,512]{1,0:T(8,128)(2,1)S(1)}, u32[]{:S(2)}, u32[]{:S(2)}) collective-permute-start(bf16[256,512]{1,0:T(8,128)(2,1)S(1)} %constant_dynamic-update-slice_fusion.refs_1_), channel_id=1, source_target_pairs={{0,56},{8,0},{16,8},{24,16},{32,24},{40,32},{48,40},{56,48},{1,57}... | collective-permute-start | bytes 786440 | tf_op jit(solution)/shard_map/ppermute | solution.py:366
  118.4 10.8 %collective-permute-start.15 = (bf16[256,512]{1,0:T(8,128)(2,1)S(1)}, bf16[256,512]{1,0:T(8,128)(2,1)S(1)}, u32[]{:S(2)}, u32[]{:S(2)}) collective-permute-start(bf16[256,512]{1,0:T(8,128)(2,1)S(1)} %constant_dynamic-update-slice_fusion.refs_1_), channel_id=1, source_target_pairs={{0,8},{8,16},{16,24},{24,32},{32,40},{40,48},{48,56},{56,0},{1,9},... | collective-permute-start | bytes 786440 | tf_op jit(solution)/shard_map/ppermute | solution.py:366
  145.8 23.7 %collective-permute-start.24 = (bf16[512,1024]{1,0:T(8,128)(2,1)}, bf16[512,1024]{1,0:T(8,128)(2,1)S(1)}, u32[]{:S(2)}, u32[]{:S(2)}) collective-permute-start(bf16[512,1024]{1,0:T(8,128)(2,1)} %all-gather.4.cloned.1.call-done.refs_10_), channel_id=1, source_target_pairs={{0,192},{64,0},{128,64},{192,128},{1,193},{65,1},{129,65},{193,129... | collective-permute-start | bytes 3145736 | tf_op jit(solution)/shard_map/ppermute | solution.py:366
  146.8 22.8 %collective-permute-start.23 = (bf16[512,1024]{1,0:T(8,128)(2,1)}, bf16[512,1024]{1,0:T(8,128)(2,1)S(1)}, u32[]{:S(2)}, u32[]{:S(2)}) collective-permute-start(bf16[512,1024]{1,0:T(8,128)(2,1)} %all-gather.4.cloned.1.call-done.refs_10_), channel_id=1, source_target_pairs={{0,64},{64,128},{128,192},{192,0},{1,65},{65,129},{129,193},{193,1... | collective-permute-start | bytes 3145736 | tf_op jit(solution)/shard_map/ppermute | solution.py:366
  149.4 10.0 %collective-permute-start.17 = (bf16[256,512]{1,0:T(8,128)(2,1)S(1)}, bf16[256,512]{1,0:T(8,128)(2,1)S(1)}, u32[]{:S(2)}, u32[]{:S(2)}) collective-permute-start(bf16[256,512]{1,0:T(8,128)(2,1)S(1)} %collective-permute-done.15.refs_2_), channel_id=1, source_target_pairs={{0,8},{8,16},{16,24},{24,32},{32,40},{40,48},{48,56},{56,0},{1,9},... | collective-permute-start | bytes 786440 | tf_op jit(solution)/shard_map/ppermute | solution.py:366
  151.2 8.2 %collective-permute-start.19 = (bf16[256,512]{1,0:T(8,128)(2,1)S(1)}, bf16[256,512]{1,0:T(8,128)(2,1)S(1)}, u32[]{:S(2)}, u32[]{:S(2)}) collective-permute-start(bf16[256,512]{1,0:T(8,128)(2,1)S(1)} %collective-permute-done.16.refs_5_), channel_id=1, source_target_pairs={{0,56},{8,0},{16,8},{24,16},{32,24},{40,32},{48,40},{56,48},{1,57}... | collective-permute-start | bytes 786440 | tf_op jit(solution)/shard_map/ppermute | solution.py:366
  159.4 14.7 %collective-permute-start.18 = (bf16[256,512]{1,0:T(8,128)(2,1)S(1)}, bf16[256,512]{1,0:T(8,128)(2,1)S(1)}, u32[]{:S(2)}, u32[]{:S(2)}) collective-permute-start(bf16[256,512]{1,0:T(8,128)(2,1)S(1)} %collective-permute-done.17.refs_3_), channel_id=1, source_target_pairs={{0,8},{8,16},{16,24},{24,32},{32,40},{40,48},{48,56},{56,0},{1,9},... | collective-permute-start | bytes 786440 | tf_op jit(solution)/shard_map/ppermute | solution.py:366
  159.4 16.5 %collective-permute-start.20 = (bf16[256,512]{1,0:T(8,128)(2,1)S(1)}, bf16[256,512]{1,0:T(8,128)(2,1)S(1)}, u32[]{:S(2)}, u32[]{:S(2)}) collective-permute-start(bf16[256,512]{1,0:T(8,128)(2,1)S(1)} %collective-permute-done.19.refs_6_), channel_id=1, source_target_pairs={{0,56},{8,0},{16,8},{24,16},{32,24},{40,32},{48,40},{56,48},{1,57}... | collective-permute-start | bytes 786440 | tf_op jit(solution)/shard_map/ppermute | solution.py:366
  169.6 12.2 %collective-permute-start.26 = (bf16[256,1024]{1,0:T(8,128)(2,1)S(1)}, bf16[256,1024]{1,0:T(8,128)(2,1)S(1)}, u32[]{:S(2)}, u32[]{:S(2)}) collective-permute-start(bf16[256,1024]{1,0:T(8,128)(2,1)S(1)} %slice.49), channel_id=1, source_target_pairs={{0,192},{64,0},{128,64},{192,128},{1,193},{65,1},{129,65},{193,129... | collective-permute-start | bytes 1572872 | tf_op jit(solution)/shard_map/ppermute | solution.py:366
  170.7 11.1 %collective-permute-start.25 = (bf16[256,1024]{1,0:T(8,128)(2,1)}, bf16[256,1024]{1,0:T(8,128)(2,1)S(1)}, u32[]{:S(2)}, u32[]{:S(2)}) collective-permute-start(bf16[256,1024]{1,0:T(8,128)(2,1)} %slice.48), channel_id=1, source_target_pairs={{0,64},{64,128},{128,192},{192,0},{1,65},{65,129},{129,193},{193,1... | collective-permute-start | bytes 1572872 | tf_op jit(solution)/shard_map/ppermute | solution.py:366
  (41 other events, 626.5 us)
Sparse Core Ops, SparseCore 0:
  106.7 37.3 all-gather.3
  145.9 25.5 all-gather.5

commit v4 on v3

--- a/solution.py
+++ b/solution.py
@@ -180,7 +180,7 @@
     )(*operands)
 
 
-def lines_kernel(y_ref, m_ref, s_ref):
+def lines_kernel(y_ref, m_ref, _, s_ref):
     rows = AEI * QC
 
     def line(d, lanes):
@@ -196,23 +196,24 @@
     s_ref[2 * rows :, BTILE:] = s.astype(BF)
 
 
-def lines(y, m):
+def lines(y, m, after):
+    vmem = pl.BlockSpec(memory_space=pltpu.VMEM)
     return pl.pallas_call(
         lines_kernel,
+        in_specs=[vmem, vmem, pl.BlockSpec(memory_space=pl.ANY)],
+        out_specs=vmem,
         out_shape=jax.ShapeDtypeStruct((NGRP * AEI * QC, CODES), BF),
         compiler_params=pltpu.CompilerParams(vmem_limit_bytes=40 * 2**20),
         name="lines",
-    )(y, m)
-
-
-def picked(s_ref, a_ref, b_ref, chunk):
-    codes = lax.broadcasted_iota(jnp.int32, (CODES, CODES), 0)
+    )(y, m, after)
+
+
+def picked(s_ref, a_ref, h_ref, chunk):
     row = lax.broadcasted_iota(jnp.int32, (SB, CODES), 0)
     outs = []
     for g in range(GCH // CODES):
         lanes = pl.ds(g * CODES, CODES)
-        chosen = (codes == b_ref[:, lanes]).astype(F32).astype(BF)
-        r = jnp.dot(s_ref[...], chosen, preferred_element_type=F32)
+        r = jnp.dot(s_ref[...], h_ref[:, lanes], preferred_element_type=F32)
         code = a_ref[:, lanes] - row // QC
         acc = jnp.zeros((SB, CODES), F32)
         for a in range(0, NGRP * AEI, 2):
@@ -222,43 +223,41 @@
     return jnp.concatenate(outs, axis=1)
 
 
-def first_kernel(s_ref, a_ref, b_ref, o_ref):
-    o_ref[...] = picked(s_ref, a_ref, b_ref, 0)
-
-
-def second_kernel(s_ref, a_ref, b_ref, first_ref, oc_ref, or_ref):
-    out = (first_ref[...] + picked(s_ref, a_ref, b_ref, 1)).astype(BF)
+def first_kernel(s_ref, a_ref, b_ref, o_ref, h_ref):
+    codes = lax.broadcasted_iota(jnp.int32, (CODES, GCH), 0)
+    h_ref[...] = (codes == b_ref[...]).astype(F32).astype(BF)
+    o_ref[...] = picked(s_ref, a_ref, h_ref, 0)
+
+
+def second_kernel(s_ref, a_ref, h_ref, first_ref, oc_ref, or_ref):
+    out = (first_ref[...] + picked(s_ref, a_ref, h_ref, 1)).astype(BF)
     oc_ref[0] = out
     for h in range(GCH // RB):
         or_ref[h] = out[:, h * RB : (h + 1) * RB]
 
 
-def pick_specs():
-    return [
-        pl.BlockSpec((NGRP * AEI * QC, CODES), lambda i: (0, 0)),
-        pl.BlockSpec((1, GCH), lambda i: (0, i)),
-        pl.BlockSpec((1, GCH), lambda i: (0, i)),
-    ]
+def along(rows):
+    return pl.BlockSpec((rows, GCH), lambda i: (0, i))
 
 
 def pick_first(s, a, b):
     return pl.pallas_call(
         first_kernel,
         grid=(GP // GCH,),
-        in_specs=pick_specs(),
-        out_specs=pl.BlockSpec((SB, GCH), lambda i: (0, i)),
-        out_shape=jax.ShapeDtypeStruct((SB, GP), F32),
+        in_specs=[pl.BlockSpec((NGRP * AEI * QC, CODES), lambda i: (0, 0)), along(1), along(1)],
+        out_specs=[along(SB), along(CODES)],
+        out_shape=[jax.ShapeDtypeStruct((SB, GP), F32), jax.ShapeDtypeStruct((CODES, GP), BF)],
         compiler_params=pltpu.CompilerParams(vmem_limit_bytes=40 * 2**20),
         name="pick_first",
     )(s, a, b)
 
 
-def pick_second(s, a, b, first):
+def pick_second(s, a, chosen, first):
     per = 4 * RB // GCH
     return pl.pallas_call(
         second_kernel,
         grid=(GP // GCH,),
-        in_specs=pick_specs() + [pl.BlockSpec((SB, GCH), lambda i: (0, i))],
+        in_specs=[pl.BlockSpec((NGRP * AEI * QC, CODES), lambda i: (0, 0)), along(1), along(CODES), along(SB)],
         out_specs=[
             pl.BlockSpec((1, SB, GCH), lambda i: (i // per, 0, i % per)),
             pl.BlockSpec((GCH // RB, SB, RB), lambda i: (i, 0, 0)),
@@ -269,7 +268,7 @@
         ],
         compiler_params=pltpu.CompilerParams(vmem_limit_bytes=40 * 2**20),
         name="pick_second",
-    )(s, a, b, first)
+    )(s, a, chosen, first)
 
 
 KP = NT * SB
@@ -386,9 +385,7 @@
         vs[VB - m] = shift(vs[(VB - m + 1) % VB], "z", NZ, -1)
     vs[VB // 2] = shift(vs[2], "z", NZ, 2)
     specs = [spectra([vs[k] for k in slots], cs, depth, plane) for slots in SLOTS]
-    slabs = [lax.all_to_all(specs[0], tile, split_axis=0, concat_axis=0, tiled=True)]
-    slabs[0], specs[1] = lax.optimization_barrier((slabs[0], specs[1]))
-    slabs.append(lax.all_to_all(specs[1], tile, split_axis=0, concat_axis=0, tiled=True))
+    slabs = [lax.all_to_all(spec, tile, split_axis=0, concat_axis=0, tiled=True) for spec in specs]
 
     valence_level = pick_levels(valence_pick, valence_energy)
     band_level = pick_levels(cond_pick, conduction_energy)
@@ -410,8 +407,8 @@
     a_code = a_code + AEI * (b_code // CODES)
     b_code = b_code % CODES
 
-    first = pick_first(lines(slabs[0].reshape(GRID * QC, YL), kron), a_code, b_code)
-    cols, for_rows = pick_second(lines(slabs[1].reshape(GRID * QC, YL), kron), a_code, b_code, first)
+    first, chosen = pick_first(lines(slabs[0].reshape(GRID * QC, YL), kron, specs[1]), a_code, b_code)
+    cols, for_rows = pick_second(lines(slabs[1].reshape(GRID * QC, YL), kron, specs[1]), a_code, chosen, first)
     cols = lax.all_to_all(cols, tile, split_axis=0, concat_axis=0, tiled=True).reshape(KP, 4 * RB)
     b_bundle = lax.all_gather(cols[:, LA:], "z", axis=0, tiled=True)
     near, far = ring(cols[:, :LA], "x", NX)

time: 200 us -> 211 us (1.055)
  waiting for transfers between devices: 47.9 us -> 54.3 us
  local copies, waits for them, and re-layouts: 8.5 us -> 13.3 us
    all_to_all x2, waiting for transfers between devices: 9.19 us -> 16.3 us  [per_device(): lax.all_to_all(spec, tile, split_axis=0, concat_axis=0, tiled=True)]
    unnamed x75 -> x77, local copies, waits for them, and re-layouts: 4.39 us -> 7.7 us
  transfers between devices with their start and end apart: 31 -> 31, of which waited for: 14 -> 13; matrix products, arithmetic and copies ran while one was open for 3% -> 4% of each run, Pallas kernels for 16% -> 11%
where the time goes in v4:
time: 211 us; the launch traced here: 210 us
  waiting for transfers between devices  54.3 us (26%)
  starting transfers between devices  50.2 us (24%)
  Pallas kernels  50 us (24%)
  blocking collectives  26 us (12%)
  between operations  14 us (7%)
  local copies, waits for them, and re-layouts  13.3 us (6%)
  other arithmetic  2.42 us (1%)
    ppermute x27, starting transfers between devices, shift(): lax.ppermute(value, axis, [(i, (i + step) % size) for i in range(size)])  42 us
    ppermute x27, waiting for transfers between devices, shift(): lax.ppermute(value, axis, [(i, (i + step) % size) for i in range(size)])  37.9 us
    pallas_call x2, Pallas kernels, spectra(): pl.pallas_call(spectra_kernel, in_specs=[pl.BlockSpec(memory_space=pl.ANY...  21.6 us
    all_to_all x1, blocking collectives, per_device(): lax.all_to_all(for_rows, ('x', 'z'), split_axis=0, concat_axis=0, tiled=T...  16.7 us
    all_to_all x2, waiting for transfers between devices, per_device(): lax.all_to_all(spec, tile, split_axis=0, concat_axis=0, tiled=True)  16.3 us
    all_to_all x1, blocking collectives, per_device(): lax.all_to_all(cols, tile, split_axis=0, concat_axis=0, tiled=True)  9.36 us
    pallas_call x1, Pallas kernels, pick_second(): pl.pallas_call(second_kernel, grid=(GP // GCH,), in_specs=[pl.BlockSpec((...  9.08 us
    pallas_call x1, Pallas kernels, pick_first(): pl.pallas_call(first_kernel, grid=(GP // GCH,), in_specs=[pl.BlockSpec((N...  8.92 us
  transfers between devices with their start and end apart: 31, of which 13 were waited for; matrix products, arithmetic and copies ran while one was open for 4% of the time, Pallas kernels for 11%

profile of v4, /device:TPU:6, one launch (start us, length us, event | category | flops | bytes accessed | tf_op | source)
XLA Modules:
  0.0 210.1 jit_solution(4989679686202739966)
XLA Ops:
  8.8 5.7 %collective-permute-start = (bf16[1,12,9216]{2,1,0:T(8,128)(2,1)}, bf16[1,12,9216]{2,1,0:T(8,128)(2,1)S(1)}, u32[]{:S(2)}, u32[]{:S(2)}) collective-permute-start(bf16[1,12,9216]{2,1,0:T(8,128)(2,1)} %refs_0_.1), channel_id=1, source_target_pairs={{0,56},{8,0},{16,8},{24,16},{32,24},{40,32},{48,40},{56,48},{1,57}... | collective-permute-start | bytes 663560 | tf_op jit(solution)/shard_map/ppermute | solution.py:365
  14.4 6.0 %collective-permute-done.refs_2_ = bf16[1,12,9216]{2,1,0:T(8,128)(2,1)S(1)} collective-permute-done((bf16[1,12,9216]{2,1,0:T(8,128)(2,1)}, bf16[1,12,9216]{2,1,0:T(8,128)(2,1)S(1)}, u32[]{:S(2)}, u32[]{:S(2)}) %collective-permute-start) | collective-permute-done | bytes 221216 | tf_op jit(solution)/shard_map/ppermute | solution.py:365
  20.4 3.6 %collective-permute-start.1 = (bf16[1,12,9216]{2,1,0:T(8,128)(2,1)S(1)}, bf16[1,12,9216]{2,1,0:T(8,128)(2,1)S(1)}, u32[]{:S(2)}, u32[]{:S(2)}) collective-permute-start(bf16[1,12,9216]{2,1,0:T(8,128)(2,1)S(1)} %collective-permute-done.refs_2_), channel_id=1, source_target_pairs={{0,56},{8,0},{16,8},{24,16},{32,24},{40,32},{48,40},{56,48},{1,57}... | collective-permute-start | bytes 663560 | tf_op jit(solution)/shard_map/ppermute | solution.py:365
  27.6 5.0 %collective-permute-done.3.refs_3_ = bf16[1,12,9216]{2,1,0:T(8,128)(2,1)S(1)} collective-permute-done((bf16[1,12,9216]{2,1,0:T(8,128)(2,1)}, bf16[1,12,9216]{2,1,0:T(8,128)(2,1)S(1)}, u32[]{:S(2)}, u32[]{:S(2)}) %collective-permute-start.3) | collective-permute-done | bytes 221216 | tf_op jit(solution)/shard_map/ppermute | solution.py:365
  32.7 3.2 %collective-permute-start.5 = (bf16[1,12,9216]{2,1,0:T(8,128)(2,1)S(1)}, bf16[1,12,9216]{2,1,0:T(8,128)(2,1)S(1)}, u32[]{:S(2)}, u32[]{:S(2)}) collective-permute-start(bf16[1,12,9216]{2,1,0:T(8,128)(2,1)S(1)} %collective-permute-done.1.refs_0_), channel_id=1, source_target_pairs={{0,56},{8,0},{16,8},{24,16},{32,24},{40,32},{48,40},{56,48},{1,57}... | collective-permute-start | bytes 663560 | tf_op jit(solution)/shard_map/ppermute | solution.py:365
  37.3 10.9 %spectra.3 = bf16[8,48,1408]{2,1,0:T(8,128)(2,1)} custom-call(bf16[1,12,9216]{2,1,0:T(8,128)(2,1)} %refs_0_.1, bf16[1,12,9216]{2,1,0:T(8,128)(2,1)} %collective-permute-done.2.refs_1_, bf16[1,12,9216]{2,1,0:T(8,128)(2,1)} %copy-done.18, bf16[1,12,9216]{2,1,0:T(8,128)(2,1)} %copy-done.17, bf16[2,12,9216]{2,1,0:T(8,128)(2,1)} %copy.34.refs_4_, ...), custom_call_target="tpu_custom_call" | custom-call | tf_op jit(solution)/shard_map/spectra/pallas_call | solution.py:167
  48.2 4.5 %all-to-all-start.1 = ((bf16[8,48,1408]{2,1,0:T(8,128)(2,1)}), bf16[8,48,1408]{2,1,0:T(8,128)(2,1)S(1)}, u32[]{:S(2)}, u32[]{:S(2)}) async-start(bf16[8,48,1408]{2,1,0:T(8,128)(2,1)} %spectra.3), calls=%async_computation.1 | async-start | bytes 2162688 | tf_op jit(solution)/shard_map/all_to_all | solution.py:388
  55.0 10.8 %spectra.2._ = bf16[8,48,1408]{2,1,0:T(8,128)(2,1)} custom-call(bf16[1,12,9216]{2,1,0:T(8,128)(2,1)} %copy-done.16, bf16[1,12,9216]{2,1,0:T(8,128)(2,1)} %copy-done.20, bf16[1,12,9216]{2,1,0:T(8,128)(2,1)} %copy-done.21, bf16[1,12,9216]{2,1,0:T(8,128)(2,1)} %copy-done.19, bf16[2,12,9216]{2,1,0:T(8,128)(2,1)} %copy.34.refs_4_, ...), custom_call_target="tpu_custom_call" | custom-call | tf_op jit(solution)/shard_map/spectra/pallas_call | solution.py:167
  65.8 3.1 %all-to-all-done.1 = bf16[8,48,1408]{2,1,0:T(8,128)(2,1)S(1)} async-done(((bf16[8,48,1408]{2,1,0:T(8,128)(2,1)}), bf16[8,48,1408]{2,1,0:T(8,128)(2,1)S(1)}, u32[]{:S(2)}, u32[]{:S(2)}) %all-to-all-start.1) | async-done | bytes 1081376 | tf_op jit(solution)/shard_map/all_to_all | solution.py:388
  69.0 3.6 %all-to-all-start = ((bf16[8,48,1408]{2,1,0:T(8,128)(2,1)}), bf16[8,48,1408]{2,1,0:T(8,128)(2,1)S(1)}, u32[]{:S(2)}, u32[]{:S(2)}) async-start(bf16[8,48,1408]{2,1,0:T(8,128)(2,1)} %spectra.2._), calls=%async_computation | async-start | bytes 2162688 | tf_op jit(solution)/shard_map/all_to_all | solution.py:388
  75.6 13.2 %all-to-all-done = bf16[8,48,1408]{2,1,0:T(8,128)(2,1)S(1)} async-done(((bf16[8,48,1408]{2,1,0:T(8,128)(2,1)}), bf16[8,48,1408]{2,1,0:T(8,128)(2,1)S(1)}, u32[]{:S(2)}, u32[]{:S(2)}) %all-to-all-start) | async-done | bytes 1081376 | tf_op jit(solution)/shard_map/all_to_all | solution.py:388
  90.7 8.9 %pick_first.1 = (f32[8,12288]{1,0:T(8,128)S(1)}, bf16[256,12288]{1,0:T(8,128)(2,1)S(1)}) custom-call(bf16[888,256]{1,0:T(8,128)(2,1)S(1)} %copy-done.2, s32[1,12288]{1,0:T(1,128)S(1)} %multiply_add_fusion.a_ref, s32[1,12288]{1,0:T(1,128)S(1)} %get-tuple-element.19.b_ref), custom_call_target="tpu_custom_call" | custom-call | tf_op jit(solution)/shard_map/pick_first/pallas_call | solution.py:244
  99.6 9.1 %pick_second.1 = (bf16[8,8,1536]{2,1,0:T(8,128)(2,1)S(1)}, bf16[32,8,384]{2,1,0:T(8,128)(2,1)S(1)}) custom-call(bf16[888,256]{1,0:T(8,128)(2,1)S(1)} %lines.2.s_ref, s32[1,12288]{1,0:T(1,128)S(1)} %multiply_add_fusion.a_ref, bf16[256,12288]{1,0:T(8,128)(2,1)S(1)} %get-tuple-element.12.h_ref, f32[8,12288]{1,0:T(8,128)S(1)} %get-tuple-element.13.first_ref), custom_call_target="tpu_custom_call" | custom-call | tf_op jit(solution)/shard_map/pick_second/pallas_call | solution.py:257
  108.7 9.4 %all_to_all.20 = bf16[8,8,1536]{2,1,0:T(8,128)(2,1)S(1)} all-to-all(bf16[8,8,1536]{2,1,0:T(8,128)(2,1)S(1)} %get-tuple-element.15), channel_id=1, replica_groups=mesh['x'=4,'z'=8,'y'=4,'core'=2] {'y','core'}, dimensions={0} | all-to-all | bytes 393216 | tf_op jit(solution)/shard_map/all_to_all | solution.py:412
  119.8 2.4 %collective-permute-start.11 = (bf16[64,512]{1,0:T(8,128)(2,1)S(1)}, bf16[64,512]{1,0:T(8,128)(2,1)S(1)}, u32[]{:S(2)}, u32[]{:S(2)}) collective-permute-start(bf16[64,512]{1,0:T(8,128)(2,1)S(1)} %get-tuple-element.21), channel_id=1, source_target_pairs={{0,64},{64,128},{128,192},{192,0},{1,65},{65,129},{129,193},{193,1... | collective-permute-start | bytes 196616 | tf_op jit(solution)/shard_map/ppermute | solution.py:365
  124.5 3.2 %collective-permute-start.13 = (bf16[32,512]{1,0:T(8,128)(2,1)S(1)}, bf16[32,512]{1,0:T(8,128)(2,1)S(1)}, u32[]{:S(2)}, u32[]{:S(2)}) collective-permute-start(bf16[32,512]{1,0:T(8,128)(2,1)S(1)} %slice.43), channel_id=1, source_target_pairs={{0,64},{64,128},{128,192},{192,0},{1,65},{65,129},{129,193},{193,1... | collective-permute-start | bytes 98312 | tf_op jit(solution)/shard_map/ppermute | solution.py:365
  131.7 6.7 %collective-permute-done.16.refs_5_ = bf16[256,512]{1,0:T(8,128)(2,1)S(1)} collective-permute-done((bf16[256,512]{1,0:T(8,128)(2,1)S(1)}, bf16[256,512]{1,0:T(8,128)(2,1)S(1)}, u32[]{:S(2)}, u32[]{:S(2)}) %collective-permute-start.16) | collective-permute-done | bytes 262176 | tf_op jit(solution)/shard_map/ppermute | solution.py:365
  140.6 16.7 %all_to_all.21 = bf16[32,8,384]{2,1,0:T(8,128)(2,1)} all-to-all(bf16[32,8,384]{2,1,0:T(8,128)(2,1)S(1)} %get-tuple-element.16), channel_id=1, replica_groups=mesh['x'=4,'z'=8,'y'=4,'core'=2] {'x','z'}, dimensions={0} | all-to-all | bytes 393216 | tf_op jit(solution)/shard_map/all_to_all | solution.py:420
  158.3 2.5 %collective-permute-start.23 = (bf16[512,1024]{1,0:T(8,128)(2,1)}, bf16[512,1024]{1,0:T(8,128)(2,1)S(1)}, u32[]{:S(2)}, u32[]{:S(2)}) collective-permute-start(bf16[512,1024]{1,0:T(8,128)(2,1)} %all-gather.4.cloned.1.call-done.refs_10_), channel_id=1, source_target_pairs={{0,64},{64,128},{128,192},{192,0},{1,65},{65,129},{129,193},{193,1... | collective-permute-start | bytes 3145736 | tf_op jit(solution)/shard_map/ppermute | solution.py:365
  164.4 6.6 %collective-permute-done.17.refs_3_ = bf16[256,512]{1,0:T(8,128)(2,1)S(1)} collective-permute-done((bf16[256,512]{1,0:T(8,128)(2,1)S(1)}, bf16[256,512]{1,0:T(8,128)(2,1)S(1)}, u32[]{:S(2)}, u32[]{:S(2)}) %collective-permute-start.17) | collective-permute-done | bytes 262176 | tf_op jit(solution)/shard_map/ppermute | solution.py:365
  171.0 3.3 %collective-permute-start.20 = (bf16[256,512]{1,0:T(8,128)(2,1)S(1)}, bf16[256,512]{1,0:T(8,128)(2,1)S(1)}, u32[]{:S(2)}, u32[]{:S(2)}) collective-permute-start(bf16[256,512]{1,0:T(8,128)(2,1)S(1)} %collective-permute-done.19.refs_6_), channel_id=1, source_target_pairs={{0,56},{8,0},{16,8},{24,16},{32,24},{40,32},{48,40},{56,48},{1,57}... | collective-permute-start | bytes 786440 | tf_op jit(solution)/shard_map/ppermute | solution.py:365
  174.5 5.5 %collective-permute-done.24.refs_12_ = bf16[512,1024]{1,0:T(8,128)(2,1)S(1)} collective-permute-done((bf16[512,1024]{1,0:T(8,128)(2,1)}, bf16[512,1024]{1,0:T(8,128)(2,1)S(1)}, u32[]{:S(2)}, u32[]{:S(2)}) %collective-permute-start.24) | collective-permute-done | bytes 1048608 | tf_op jit(solution)/shard_map/ppermute | solution.py:365
  181.7 3.2 %collective-permute-start.25 = (bf16[256,1024]{1,0:T(8,128)(2,1)}, bf16[256,1024]{1,0:T(8,128)(2,1)}, u32[]{:S(2)}, u32[]{:S(2)}) collective-permute-start(bf16[256,1024]{1,0:T(8,128)(2,1)} %slice.48), channel_id=1, source_target_pairs={{0,64},{64,128},{128,192},{192,0},{1,65},{65,129},{129,193},{193,1... | collective-permute-start | bytes 1572872 | tf_op jit(solution)/shard_map/ppermute | solution.py:365
  194.5 8.7 %product.1 = f32[375,1500]{1,0:T(8,128)} custom-call(s32[2]{0:T(128)} %pad_add_fusion.xz_ref, f32[2048,1]{1,0:T(8,128)} %copy.40.w_ref, bf16[8,32,8,384]{3,2,1,0:T(8,128)(2,1)} %bitcast.21, bf16[256,512]{1,0:T(8,128)(2,1)} %copy-done.15, bf16[256,512]{1,0:T(8,128)(2,1)} %copy-done.23, bf16[256,512]{1,0:T(8,128)(2,1)} %copy-done.24, ...), custom_call_target="tpu_custom_call" | custom-call | tf_op jit(solution)/shard_map/product/pallas_call | solution.py:324
  (152 shorter events, 40.5 us)
Async XLA Ops:
  6.5 17.5 %collective-permute-start.7 = (bf16[2,12,9216]{2,0,1:T(2,128)(2,1)}, bf16[2,12,9216]{2,0,1:T(2,128)(2,1)S(1)}, u32[]{:S(2)}, u32[]{:S(2)}) collective-permute-start(bf16[2,12,9216]{2,0,1:T(2,128)(2,1)} %param.14), channel_id=1, source_target_pairs={{0,64},{64,128},{128,192},{192,0},{1,65},{65,129},{129,193},{193,1... | collective-permute-start | bytes 1327112 | tf_op jit(solution)/shard_map/ppermute | solution.py:365
  8.8 17.2 %collective-permute-start.8 = (bf16[2,12,9216]{2,0,1:T(2,128)(2,1)}, bf16[2,12,9216]{2,0,1:T(2,128)(2,1)S(1)}, u32[]{:S(2)}, u32[]{:S(2)}) collective-permute-start(bf16[2,12,9216]{2,0,1:T(2,128)(2,1)} %param.14), channel_id=1, source_target_pairs={{0,192},{64,0},{128,64},{192,128},{1,193},{65,1},{129,65},{193,129... | collective-permute-start | bytes 1327112 | tf_op jit(solution)/shard_map/ppermute | solution.py:365
  8.8 11.7 %collective-permute-start = (bf16[1,12,9216]{2,1,0:T(8,128)(2,1)}, bf16[1,12,9216]{2,1,0:T(8,128)(2,1)S(1)}, u32[]{:S(2)}, u32[]{:S(2)}) collective-permute-start(bf16[1,12,9216]{2,1,0:T(8,128)(2,1)} %refs_0_.1), channel_id=1, source_target_pairs={{0,56},{8,0},{16,8},{24,16},{32,24},{40,32},{48,40},{56,48},{1,57}... | collective-permute-start | bytes 663560 | tf_op jit(solution)/shard_map/ppermute | solution.py:365
  14.4 9.6 %collective-permute-start.2 = (bf16[1,12,9216]{2,1,0:T(8,128)(2,1)}, bf16[1,12,9216]{2,1,0:T(8,128)(2,1)}, u32[]{:S(2)}, u32[]{:S(2)}) collective-permute-start(bf16[1,12,9216]{2,1,0:T(8,128)(2,1)} %refs_0_.1), channel_id=1, source_target_pairs={{0,8},{8,16},{16,24},{24,32},{32,40},{40,48},{48,56},{56,0},{1,9},... | collective-permute-start | bytes 663560 | tf_op jit(solution)/shard_map/ppermute | solution.py:365
  20.4 12.2 %collective-permute-start.1 = (bf16[1,12,9216]{2,1,0:T(8,128)(2,1)S(1)}, bf16[1,12,9216]{2,1,0:T(8,128)(2,1)S(1)}, u32[]{:S(2)}, u32[]{:S(2)}) collective-permute-start(bf16[1,12,9216]{2,1,0:T(8,128)(2,1)S(1)} %collective-permute-done.refs_2_), channel_id=1, source_target_pairs={{0,56},{8,0},{16,8},{24,16},{32,24},{40,32},{48,40},{56,48},{1,57}... | collective-permute-start | bytes 663560 | tf_op jit(solution)/shard_map/ppermute | solution.py:365
  24.0 8.6 %collective-permute-start.3 = (bf16[1,12,9216]{2,1,0:T(8,128)(2,1)}, bf16[1,12,9216]{2,1,0:T(8,128)(2,1)S(1)}, u32[]{:S(2)}, u32[]{:S(2)}) collective-permute-start(bf16[1,12,9216]{2,1,0:T(8,128)(2,1)} %collective-permute-done.2.refs_1_), channel_id=1, source_target_pairs={{0,8},{8,16},{16,24},{24,32},{32,40},{40,48},{48,56},{56,0},{1,9},... | collective-permute-start | bytes 663560 | tf_op jit(solution)/shard_map/ppermute | solution.py:365
  24.2 11.7 %collective-permute-start.9 = (bf16[1,12,9216]{2,1,0:T(8,128)(2,1)S(1)}, bf16[1,12,9216]{2,1,0:T(8,128)(2,1)S(1)}, u32[]{:S(2)}, u32[]{:S(2)}) collective-permute-start(bf16[1,12,9216]{2,1,0:T(8,128)(2,1)S(1)} %slice.40), channel_id=1, source_target_pairs={{0,64},{64,128},{128,192},{192,0},{1,65},{65,129},{129,193},{193,1... | collective-permute-start | bytes 663560 | tf_op jit(solution)/shard_map/ppermute | solution.py:365
  26.1 9.8 %collective-permute-start.10 = (bf16[1,12,9216]{2,1,0:T(8,128)(2,1)S(1)}, bf16[1,12,9216]{2,1,0:T(8,128)(2,1)S(1)}, u32[]{:S(2)}, u32[]{:S(2)}) collective-permute-start(bf16[1,12,9216]{2,1,0:T(8,128)(2,1)S(1)} %slice.41), channel_id=1, source_target_pairs={{0,192},{64,0},{128,64},{192,128},{1,193},{65,1},{129,65},{193,129... | collective-permute-start | bytes 663560 | tf_op jit(solution)/shard_map/ppermute | solution.py:365
  32.6 20.8 %collective-permute-start.6 = (bf16[1,12,9216]{2,1,0:T(8,128)(2,1)S(1)}, bf16[1,12,9216]{2,1,0:T(8,128)(2,1)S(1)}, u32[]{:S(2)}, u32[]{:S(2)}) collective-permute-start(bf16[1,12,9216]{2,1,0:T(8,128)(2,1)S(1)} %collective-permute-done.3.refs_3_), channel_id=1, source_target_pairs={{0,16},{8,24},{16,32},{24,40},{32,48},{40,56},{48,0},{56,8},{1,17}... | collective-permute-start | bytes 663560 | tf_op jit(solution)/shard_map/ppermute | solution.py:365
  32.6 20.9 %collective-permute-start.4 = (bf16[1,12,9216]{2,1,0:T(8,128)(2,1)S(1)}, bf16[1,12,9216]{2,1,0:T(8,128)(2,1)S(1)}, u32[]{:S(2)}, u32[]{:S(2)}) collective-permute-start(bf16[1,12,9216]{2,1,0:T(8,128)(2,1)S(1)} %collective-permute-done.3.refs_3_), channel_id=1, source_target_pairs={{0,8},{8,16},{16,24},{24,32},{32,40},{40,48},{48,56},{56,0},{1,9},... | collective-permute-start | bytes 663560 | tf_op jit(solution)/shard_map/ppermute | solution.py:365
  32.7 20.8 %collective-permute-start.5 = (bf16[1,12,9216]{2,1,0:T(8,128)(2,1)S(1)}, bf16[1,12,9216]{2,1,0:T(8,128)(2,1)S(1)}, u32[]{:S(2)}, u32[]{:S(2)}) collective-permute-start(bf16[1,12,9216]{2,1,0:T(8,128)(2,1)S(1)} %collective-permute-done.1.refs_0_), channel_id=1, source_target_pairs={{0,56},{8,0},{16,8},{24,16},{32,24},{40,32},{48,40},{56,48},{1,57}... | collective-permute-start | bytes 663560 | tf_op jit(solution)/shard_map/ppermute | solution.py:365
  48.2 20.8 %all-to-all-start.1 = ((bf16[8,48,1408]{2,1,0:T(8,128)(2,1)}), bf16[8,48,1408]{2,1,0:T(8,128)(2,1)S(1)}, u32[]{:S(2)}, u32[]{:S(2)}) async-start(bf16[8,48,1408]{2,1,0:T(8,128)(2,1)} %spectra.3), calls=%async_computation.1 | async-start | bytes 2162688 | tf_op jit(solution)/shard_map/all_to_all | solution.py:388
  69.0 19.8 %all-to-all-start = ((bf16[8,48,1408]{2,1,0:T(8,128)(2,1)}), bf16[8,48,1408]{2,1,0:T(8,128)(2,1)S(1)}, u32[]{:S(2)}, u32[]{:S(2)}) async-start(bf16[8,48,1408]{2,1,0:T(8,128)(2,1)} %spectra.2._), calls=%async_computation | async-start | bytes 2162688 | tf_op jit(solution)/shard_map/all_to_all | solution.py:388
  72.5 84.7 %all-gather.4.cloned.1.call-start = ((), (), s32[]{:S(2)}) async-start(), calls=%async_computation.4 | async-start | bytes 1179648 | tf_op jit(solution)/shard_map/all_gather | solution.py:413
  118.8 74.9 %all-gather.6.cloned.1.call-start = ((), (), s32[]{:S(2)}) async-start(), calls=%async_computation.5 | async-start | bytes 1769472 | tf_op jit(solution)/shard_map/all_gather | solution.py:421
  129.6 8.7 %collective-permute-start.16 = (bf16[256,512]{1,0:T(8,128)(2,1)S(1)}, bf16[256,512]{1,0:T(8,128)(2,1)S(1)}, u32[]{:S(2)}, u32[]{:S(2)}) collective-permute-start(bf16[256,512]{1,0:T(8,128)(2,1)S(1)} %constant_dynamic-update-slice_fusion.refs_1_), channel_id=1, source_target_pairs={{0,56},{8,0},{16,8},{24,16},{32,24},{40,32},{48,40},{56,48},{1,57}... | collective-permute-start | bytes 786440 | tf_op jit(solution)/shard_map/ppermute | solution.py:365
  131.2 9.4 %collective-permute-start.15 = (bf16[256,512]{1,0:T(8,128)(2,1)S(1)}, bf16[256,512]{1,0:T(8,128)(2,1)S(1)}, u32[]{:S(2)}, u32[]{:S(2)}) collective-permute-start(bf16[256,512]{1,0:T(8,128)(2,1)S(1)} %constant_dynamic-update-slice_fusion.refs_1_), channel_id=1, source_target_pairs={{0,8},{8,16},{16,24},{24,32},{32,40},{40,48},{48,56},{56,0},{1,9},... | collective-permute-start | bytes 786440 | tf_op jit(solution)/shard_map/ppermute | solution.py:365
  157.3 22.7 %collective-permute-start.24 = (bf16[512,1024]{1,0:T(8,128)(2,1)}, bf16[512,1024]{1,0:T(8,128)(2,1)S(1)}, u32[]{:S(2)}, u32[]{:S(2)}) collective-permute-start(bf16[512,1024]{1,0:T(8,128)(2,1)} %all-gather.4.cloned.1.call-done.refs_10_), channel_id=1, source_target_pairs={{0,192},{64,0},{128,64},{192,128},{1,193},{65,1},{129,65},{193,129... | collective-permute-start | bytes 3145736 | tf_op jit(solution)/shard_map/ppermute | solution.py:365
  158.3 22.5 %collective-permute-start.23 = (bf16[512,1024]{1,0:T(8,128)(2,1)}, bf16[512,1024]{1,0:T(8,128)(2,1)S(1)}, u32[]{:S(2)}, u32[]{:S(2)}) collective-permute-start(bf16[512,1024]{1,0:T(8,128)(2,1)} %all-gather.4.cloned.1.call-done.refs_10_), channel_id=1, source_target_pairs={{0,64},{64,128},{128,192},{192,0},{1,65},{65,129},{129,193},{193,1... | collective-permute-start | bytes 3145736 | tf_op jit(solution)/shard_map/ppermute | solution.py:365
  160.8 10.2 %collective-permute-start.17 = (bf16[256,512]{1,0:T(8,128)(2,1)S(1)}, bf16[256,512]{1,0:T(8,128)(2,1)S(1)}, u32[]{:S(2)}, u32[]{:S(2)}) collective-permute-start(bf16[256,512]{1,0:T(8,128)(2,1)S(1)} %collective-permute-done.15.refs_2_), channel_id=1, source_target_pairs={{0,8},{8,16},{16,24},{24,32},{32,40},{40,48},{48,56},{56,0},{1,9},... | collective-permute-start | bytes 786440 | tf_op jit(solution)/shard_map/ppermute | solution.py:365
  171.0 14.3 %collective-permute-start.18 = (bf16[256,512]{1,0:T(8,128)(2,1)S(1)}, bf16[256,512]{1,0:T(8,128)(2,1)S(1)}, u32[]{:S(2)}, u32[]{:S(2)}) collective-permute-start(bf16[256,512]{1,0:T(8,128)(2,1)S(1)} %collective-permute-done.17.refs_3_), channel_id=1, source_target_pairs={{0,8},{8,16},{16,24},{24,32},{32,40},{40,48},{48,56},{56,0},{1,9},... | collective-permute-start | bytes 786440 | tf_op jit(solution)/shard_map/ppermute | solution.py:365
  171.0 16.7 %collective-permute-start.20 = (bf16[256,512]{1,0:T(8,128)(2,1)S(1)}, bf16[256,512]{1,0:T(8,128)(2,1)S(1)}, u32[]{:S(2)}, u32[]{:S(2)}) collective-permute-start(bf16[256,512]{1,0:T(8,128)(2,1)S(1)} %collective-permute-done.19.refs_6_), channel_id=1, source_target_pairs={{0,56},{8,0},{16,8},{24,16},{32,24},{40,32},{48,40},{56,48},{1,57}... | collective-permute-start | bytes 786440 | tf_op jit(solution)/shard_map/ppermute | solution.py:365
  180.8 12.9 %collective-permute-start.26 = (bf16[256,1024]{1,0:T(8,128)(2,1)}, bf16[256,1024]{1,0:T(8,128)(2,1)S(1)}, u32[]{:S(2)}, u32[]{:S(2)}) collective-permute-start(bf16[256,1024]{1,0:T(8,128)(2,1)} %slice.49), channel_id=1, source_target_pairs={{0,192},{64,0},{128,64},{192,128},{1,193},{65,1},{129,65},{193,129... | collective-permute-start | bytes 1572872 | tf_op jit(solution)/shard_map/ppermute | solution.py:365
  181.7 12.0 %collective-permute-start.25 = (bf16[256,1024]{1,0:T(8,128)(2,1)}, bf16[256,1024]{1,0:T(8,128)(2,1)}, u32[]{:S(2)}, u32[]{:S(2)}) collective-permute-start(bf16[256,1024]{1,0:T(8,128)(2,1)} %slice.48), channel_id=1, source_target_pairs={{0,64},{64,128},{128,192},{192,0},{1,65},{65,129},{129,193},{193,1... | collective-permute-start | bytes 1572872 | tf_op jit(solution)/shard_map/ppermute | solution.py:365
  (42 other events, 729.4 us)
Sparse Core Ops, SparseCore 0:
  118.9 36.4 all-gather.3
  157.4 25.2 all-gather.5

commit v5 on v3

--- a/solution.py
+++ b/solution.py
@@ -109,11 +109,13 @@
     o_ref, dens, zs, sems = refs[n], *refs[2 * n + 1 :]
     spaces = refs[n + 1 : 2 * n + 1]
     v_refs, c_refs, (t_ref, w_ref) = spaces[:VC], spaces[VC : n - 2], spaces[n - 2 :]
-    tables = copy_in(refs[n - 2 : n], spaces[n - 2 :], sems.at[NCUT])
+    tables = copy_in([refs[n - 2]], [t_ref], sems.at[NCUT])
     cuts = []
     for cut in range(NCUT):
         lanes = pl.ds(cut * (GRID * GRID // NCUT), GRID * GRID // NCUT)
         cuts.append(copy_in([r.at[:, :, lanes] for r in refs[: n - 2]], [r.at[:, :, lanes] for r in spaces[: n - 2]], sems.at[cut]))
+    tables.append(pltpu.make_async_copy(refs[n - 1], w_ref, sems.at[NCUT, 1]))
+    tables[1].start()
     tables[0].wait()
 
     def body(step, _):
@@ -273,7 +275,9 @@
 
 
 KP = NT * SB
-LA = 512
+LA = 640
+LB = 4 * RB - LA
+LG = 1024
 XORDER = (0, 1, 3, 2)
 ZORDER = (0, 1, 2, 3, 7, 6, 5, 4)
 
@@ -413,12 +417,19 @@
     first = pick_first(lines(slabs[0].reshape(GRID * QC, YL), kron), a_code, b_code)
     cols, for_rows = pick_second(lines(slabs[1].reshape(GRID * QC, YL), kron), a_code, b_code, first)
     cols = lax.all_to_all(cols, tile, split_axis=0, concat_axis=0, tiled=True).reshape(KP, 4 * RB)
-    b_bundle = lax.all_gather(cols[:, LA:], "z", axis=0, tiled=True)
-    near, far = ring(cols[:, :LA], "x", NX)
-    a_bundle = jnp.concatenate(near + far, axis=0)
+    b_part = jnp.concatenate([cols[:, LA:], cols[:, LA : LA + LG - LB]], axis=1)
+    b_bundle = lax.all_gather(b_part, "z", axis=0, tiled=True)[:, :LB]
+    a_part = cols[:, :LA]
+    a_bundle = jnp.concatenate([a_part] + [shift(a_part, "x", NX, step) for step in (1, -1, 2)], axis=0)
     a_up, a_down = shift(a_bundle, "z", NZ, 1), shift(a_bundle, "z", NZ, -1)
     for_rows, a_up, a_down = lax.optimization_barrier((for_rows, a_up, a_down))
-    a_cols, a_far = ring_on(a_bundle, a_up, a_down, "z", NZ)
+    ups, downs = [a_up], [a_down]
+    for _ in range(2):
+        ups.append(shift(ups[-1], "z", NZ, 1))
+        downs.append(shift(downs[-1], "z", NZ, -1))
+    half = a_bundle.shape[0] // 2
+    a_far = [shift(ups[1][:half], "z", NZ, 2), shift(downs[1][half:], "z", NZ, -2)]
+    a_cols = [a_bundle] + ups + downs
     b_cols, b_far = ring(b_bundle, "x", NX)
     rows = lax.all_to_all(for_rows, ("x", "z"), split_axis=0, concat_axis=0, tiled=True)
     rows = lax.all_gather(rows, ("y", "core"), axis=0, tiled=False)

time: 200 us -> 206 us (1.030)
  waiting for transfers between devices: 47.9 us -> 54 us
  starting transfers between devices: 49.8 us -> 47.3 us
    ppermute x27 -> x26, waiting for transfers between devices: 38.6 us -> 44 us  [shift(): lax.ppermute(value, axis, [(i, (i + step) % size) for i in range(size)])]
    pallas_call x1, Pallas kernels: 8.7 us -> 11.2 us  [product(): pl.pallas_call(product_kernel, in_specs=[pl.BlockSpec(memory_space=pltpu....]
    ppermute x27 -> x26, starting transfers between devices: 41.7 us -> 39.2 us  [shift(): lax.ppermute(value, axis, [(i, (i + step) % size) for i in range(size)])]
    unnamed x75 -> x66, local copies, waits for them, and re-layouts: 4.39 us -> 4.94 us
  transfers between devices with their start and end apart: 31 -> 30, of which waited for: 14 -> 14; matrix products, arithmetic and copies ran while one was open for 3% -> 4% of each run, Pallas kernels for 16% -> 14%
where the time goes in v5:
time: 206 us
  waiting for transfers between devices  54 us (26%)
  Pallas kernels  50.8 us (25%)
  starting transfers between devices  47.3 us (23%)
  blocking collectives  27.7 us (13%)
  between operations  13.9 us (7%)
  local copies, waits for them, and re-layouts  8.73 us (4%)
  other arithmetic  3.1 us (2%)
    ppermute x26, waiting for transfers between devices, shift(): lax.ppermute(value, axis, [(i, (i + step) % size) for i in range(size)])  44 us
    ppermute x26, starting transfers between devices, shift(): lax.ppermute(value, axis, [(i, (i + step) % size) for i in range(size)])  39.2 us
    pallas_call x2, Pallas kernels, spectra(): pl.pallas_call(spectra_kernel, in_specs=[pl.BlockSpec(memory_space=pl.ANY...  20 us
    all_to_all x1, blocking collectives, per_device(): lax.all_to_all(for_rows, ('x', 'z'), split_axis=0, concat_axis=0, tiled=T...  18.5 us
    pallas_call x1, Pallas kernels, product(): pl.pallas_call(product_kernel, in_specs=[pl.BlockSpec(memory_space=pltpu....  11.2 us
    all_to_all x1, blocking collectives, per_device(): lax.all_to_all(cols, tile, split_axis=0, concat_axis=0, tiled=True)  9.23 us
    pallas_call x1, Pallas kernels, pick_second(): pl.pallas_call(second_kernel, grid=(GP // GCH,), in_specs=pick_specs() +...  8.99 us
    pallas_call x1, Pallas kernels, pick_first(): pl.pallas_call(first_kernel, grid=(GP // GCH,), in_specs=pick_specs(), ou...  8.96 us
  transfers between devices with their start and end apart: 30, of which 14 were waited for; matrix products, arithmetic and copies ran while one was open for 4% of the time, Pallas kernels for 14%

profile of v5, /device:TPU:6, one launch (start us, length us, event | category | flops | bytes accessed | tf_op | source)
XLA Modules:
  0.0 205.6 jit_solution(3302824047973972690)
XLA Ops:
  10.5 3.9 %collective-permute-start.1 = (bf16[1,12,9216]{2,1,0:T(8,128)(2,1)}, bf16[1,12,9216]{2,1,0:T(8,128)(2,1)S(1)}, u32[]{:S(2)}, u32[]{:S(2)}) collective-permute-start(bf16[1,12,9216]{2,1,0:T(8,128)(2,1)} %refs_0_.1), channel_id=1, source_target_pairs={{0,56},{8,0},{16,8},{24,16},{32,24},{40,32},{48,40},{56,48},{1,57}... | collective-permute-start | bytes 663560 | tf_op jit(solution)/shard_map/ppermute | solution.py:370
  14.4 6.7 %collective-permute-done.refs_1_ = bf16[1,12,9216]{2,1,0:T(8,128)(2,1)S(1)} collective-permute-done((bf16[1,12,9216]{2,1,0:T(8,128)(2,1)}, bf16[1,12,9216]{2,1,0:T(8,128)(2,1)S(1)}, u32[]{:S(2)}, u32[]{:S(2)}) %collective-permute-start) | collective-permute-done | bytes 221216 | tf_op jit(solution)/shard_map/ppermute | solution.py:370
  21.1 3.2 %collective-permute-start.7 = (bf16[1,12,9216]{2,1,0:T(8,128)(2,1)S(1)}, bf16[1,12,9216]{2,1,0:T(8,128)(2,1)S(1)}, u32[]{:S(2)}, u32[]{:S(2)}) collective-permute-start(bf16[1,12,9216]{2,1,0:T(8,128)(2,1)S(1)} %collective-permute-done.1.refs_2_), channel_id=1, source_target_pairs={{0,56},{8,0},{16,8},{24,16},{32,24},{40,32},{48,40},{56,48},{1,57}... | collective-permute-start | bytes 663560 | tf_op jit(solution)/shard_map/ppermute | solution.py:370
  35.1 10.0 %spectra.2 = bf16[8,48,1408]{2,1,0:T(8,128)(2,1)} custom-call(bf16[1,12,9216]{2,1,0:T(8,128)(2,1)} %refs_0_.1, bf16[1,12,9216]{2,1,0:T(8,128)(2,1)} %copy-done.17, bf16[1,12,9216]{2,1,0:T(8,128)(2,1)} %copy-done.18, bf16[1,12,9216]{2,1,0:T(8,128)(2,1)} %copy-done.16, bf16[2,12,9216]{2,1,0:T(8,128)(2,1)} %copy.34.refs_4_, bf16[2,12,9216]{2,1,0:T(8,128)(2,1)} %copy-done.1, ...), custom_call_target="tpu_custom_call" | custom-call | tf_op jit(solution)/shard_map/spectra/pallas_call | solution.py:169
  45.2 4.5 %all-to-all-start = ((bf16[8,48,1408]{2,1,0:T(8,128)(2,1)}), bf16[8,48,1408]{2,1,0:T(8,128)(2,1)S(1)}, u32[]{:S(2)}, u32[]{:S(2)}) async-start(bf16[8,48,1408]{2,1,0:T(8,128)(2,1)} %spectra.2), calls=%async_computation | async-start | bytes 2162688 | tf_op jit(solution)/shard_map/all_to_all | solution.py:393
  52.0 10.0 %spectra.3 = bf16[8,48,1408]{2,1,0:T(8,128)(2,1)} custom-call(bf16[1,12,9216]{2,1,0:T(8,128)(2,1)} %copy-done.15, bf16[1,12,9216]{2,1,0:T(8,128)(2,1)} %copy-done.20, bf16[1,12,9216]{2,1,0:T(8,128)(2,1)} %copy-done.21, bf16[1,12,9216]{2,1,0:T(8,128)(2,1)} %copy-done.19, bf16[2,12,9216]{2,1,0:T(8,128)(2,1)} %copy.34.refs_4_, bf16[2,12,9216]{2,1,0:T(8,128)(2,1)} %copy-done.1, ...), custom_call_target="tpu_custom_call" | custom-call | tf_op jit(solution)/shard_map/spectra/pallas_call | solution.py:169
  62.1 3.9 %all-to-all-done = bf16[8,48,1408]{2,1,0:T(8,128)(2,1)S(1)} async-done(((bf16[8,48,1408]{2,1,0:T(8,128)(2,1)}), bf16[8,48,1408]{2,1,0:T(8,128)(2,1)S(1)}, u32[]{:S(2)}, u32[]{:S(2)}) %all-to-all-start) | async-done | bytes 1081376 | tf_op jit(solution)/shard_map/all_to_all | solution.py:393
  66.0 3.6 %all-to-all-start.1 = ((bf16[8,48,1408]{2,1,0:T(8,128)(2,1)}), bf16[8,48,1408]{2,1,0:T(8,128)(2,1)S(1)}, u32[]{:S(2)}, u32[]{:S(2)}) async-start(bf16[8,48,1408]{2,1,0:T(8,128)(2,1)} %spectra.3), calls=%async_computation.1 | async-start | bytes 2162688 | tf_op jit(solution)/shard_map/all_to_all | solution.py:395
  70.8 9.0 %pick_first.1.first_ref = f32[8,12288]{1,0:T(8,128)S(1)} custom-call(bf16[888,256]{1,0:T(8,128)(2,1)S(1)} %lines.3.s_ref, s32[1,12288]{1,0:T(1,128)S(1)} %multiply_add_fusion.a_ref, s32[1,12288]{1,0:T(1,128)S(1)} %get-tuple-element.19.b_ref), custom_call_target="tpu_custom_call" | custom-call | tf_op jit(solution)/shard_map/pick_first/pallas_call | solution.py:247
  79.7 6.1 %all-to-all-done.1 = bf16[8,48,1408]{2,1,0:T(8,128)(2,1)S(1)} async-done(((bf16[8,48,1408]{2,1,0:T(8,128)(2,1)}), bf16[8,48,1408]{2,1,0:T(8,128)(2,1)S(1)}, u32[]{:S(2)}, u32[]{:S(2)}) %all-to-all-start.1) | async-done | bytes 1081376 | tf_op jit(solution)/shard_map/all_to_all | solution.py:395
  86.6 9.0 %pick_second.1 = (bf16[8,8,1536]{2,1,0:T(8,128)(2,1)S(1)}, bf16[32,8,384]{2,1,0:T(8,128)(2,1)S(1)}) custom-call(bf16[888,256]{1,0:T(8,128)(2,1)S(1)} %lines.2.s_ref, s32[1,12288]{1,0:T(1,128)S(1)} %multiply_add_fusion.a_ref, s32[1,12288]{1,0:T(1,128)S(1)} %get-tuple-element.19.b_ref, f32[8,12288]{1,0:T(8,128)S(1)} %pick_first.1.first_ref), custom_call_target="tpu_custom_call" | custom-call | tf_op jit(solution)/shard_map/pick_second/pallas_call | solution.py:260
  95.6 9.2 %all_to_all.20 = bf16[8,8,1536]{2,1,0:T(8,128)(2,1)S(1)} all-to-all(bf16[8,8,1536]{2,1,0:T(8,128)(2,1)S(1)} %get-tuple-element.15), channel_id=1, replica_groups=mesh['x'=4,'z'=8,'y'=4,'core'=2] {'y','core'}, dimensions={0} | all-to-all | bytes 393216 | tf_op jit(solution)/shard_map/all_to_all | solution.py:419
  109.7 2.3 %collective-permute-done.13 = bf16[64,640]{1,0:T(8,128)(2,1)S(1)} collective-permute-done((bf16[64,640]{1,0:T(8,128)(2,1)S(1)}, bf16[64,640]{1,0:T(8,128)(2,1)S(1)}, u32[]{:S(2)}, u32[]{:S(2)}) %collective-permute-start.13) | collective-permute-done | bytes 81952 | tf_op jit(solution)/shard_map/ppermute | solution.py:370
  115.0 9.1 %collective-permute-done.15.refs_5_ = bf16[256,640]{1,0:T(8,128)(2,1)} collective-permute-done((bf16[256,640]{1,0:T(8,128)(2,1)S(1)}, bf16[256,640]{1,0:T(8,128)(2,1)}, u32[]{:S(2)}, u32[]{:S(2)}) %collective-permute-start.15) | collective-permute-done | bytes 327712 | tf_op jit(solution)/shard_map/ppermute | solution.py:370
  124.2 2.9 %collective-permute-done.14.refs_2_ = bf16[256,640]{1,0:T(8,128)(2,1)S(1)} collective-permute-done((bf16[256,640]{1,0:T(8,128)(2,1)S(1)}, bf16[256,640]{1,0:T(8,128)(2,1)S(1)}, u32[]{:S(2)}, u32[]{:S(2)}) %collective-permute-start.14) | collective-permute-done | bytes 327712 | tf_op jit(solution)/shard_map/ppermute | solution.py:370
  127.1 18.5 %all_to_all.21 = bf16[32,8,384]{2,1,0:T(8,128)(2,1)} all-to-all(bf16[32,8,384]{2,1,0:T(8,128)(2,1)S(1)} %get-tuple-element.16), channel_id=1, replica_groups=mesh['x'=4,'z'=8,'y'=4,'core'=2] {'x','z'}, dimensions={0} | all-to-all | bytes 393216 | tf_op jit(solution)/shard_map/all_to_all | solution.py:434
  147.5 2.7 %collective-permute-start.22 = (bf16[512,896]{1,0:T(8,128)(2,1)S(1)}, bf16[512,896]{1,0:T(8,128)(2,1)S(1)}, u32[]{:S(2)}, u32[]{:S(2)}) collective-permute-start(bf16[512,896]{1,0:T(8,128)(2,1)S(1)} %slice.47.refs_10_), channel_id=1, source_target_pairs={{0,64},{64,128},{128,192},{192,0},{1,65},{65,129},{129,193},{193,1... | collective-permute-start | bytes 2752520 | tf_op jit(solution)/shard_map/ppermute | solution.py:370
  154.1 4.5 %collective-permute-done.16.refs_3_ = bf16[256,640]{1,0:T(8,128)(2,1)S(1)} collective-permute-done((bf16[256,640]{1,0:T(8,128)(2,1)S(1)}, bf16[256,640]{1,0:T(8,128)(2,1)S(1)}, u32[]{:S(2)}, u32[]{:S(2)}) %collective-permute-start.16) | collective-permute-done | bytes 327712 | tf_op jit(solution)/shard_map/ppermute | solution.py:370
  159.5 8.6 %collective-permute-done.23.refs_12_ = bf16[512,896]{1,0:T(8,128)(2,1)S(1)} collective-permute-done((bf16[512,896]{1,0:T(8,128)(2,1)S(1)}, bf16[512,896]{1,0:T(8,128)(2,1)S(1)}, u32[]{:S(2)}, u32[]{:S(2)}) %collective-permute-start.23) | collective-permute-done | bytes 917536 | tf_op jit(solution)/shard_map/ppermute | solution.py:370
  168.3 3.3 %collective-permute-start.24 = (bf16[256,896]{1,0:T(8,128)(2,1)S(1)}, bf16[256,896]{1,0:T(8,128)(2,1)S(1)}, u32[]{:S(2)}, u32[]{:S(2)}) collective-permute-start(bf16[256,896]{1,0:T(8,128)(2,1)S(1)} %slice.48), channel_id=1, source_target_pairs={{0,64},{64,128},{128,192},{192,0},{1,65},{65,129},{129,193},{193,1... | collective-permute-start | bytes 1376264 | tf_op jit(solution)/shard_map/ppermute | solution.py:370
  172.6 2.3 %collective-permute-start.21 = (bf16[128,640]{1,0:T(8,128)(2,1)}, bf16[128,640]{1,0:T(8,128)(2,1)}, u32[]{:S(2)}, u32[]{:S(2)}) collective-permute-start(bf16[128,640]{1,0:T(8,128)(2,1)} %slice.44), channel_id=1, source_target_pairs={{0,48},{8,56},{16,0},{24,8},{32,16},{40,24},{48,32},{56,40},{1,49}... | collective-permute-start | bytes 491528 | tf_op jit(solution)/shard_map/ppermute | solution.py:370
  176.1 2.8 %collective-permute-start.19 = (bf16[256,640]{1,0:T(8,128)(2,1)S(1)}, bf16[256,640]{1,0:T(8,128)(2,1)}, u32[]{:S(2)}, u32[]{:S(2)}) collective-permute-start(bf16[256,640]{1,0:T(8,128)(2,1)S(1)} %collective-permute-done.18.refs_6_), channel_id=1, source_target_pairs={{0,56},{8,0},{16,8},{24,16},{32,24},{40,32},{48,40},{56,48},{1,57}... | collective-permute-start | bytes 983048 | tf_op jit(solution)/shard_map/ppermute | solution.py:370
  183.3 3.3 %collective-permute-done.19.refs_7_ = bf16[256,640]{1,0:T(8,128)(2,1)} collective-permute-done((bf16[256,640]{1,0:T(8,128)(2,1)S(1)}, bf16[256,640]{1,0:T(8,128)(2,1)}, u32[]{:S(2)}, u32[]{:S(2)}) %collective-permute-start.19) | collective-permute-done | bytes 327712 | tf_op jit(solution)/shard_map/ppermute | solution.py:370
  187.6 11.2 %product.1 = f32[375,1500]{1,0:T(8,128)} custom-call(s32[2]{0:T(128)} %pad_add_fusion.xz_ref, f32[2048,1]{1,0:T(8,128)} %copy.40.w_ref, bf16[8,32,8,384]{3,2,1,0:T(8,128)(2,1)} %bitcast.21, bf16[256,640]{1,0:T(8,128)(2,1)} %copy-done.6, bf16[256,640]{1,0:T(8,128)(2,1)} %copy-done.14, bf16[256,640]{1,0:T(8,128)(2,1)} %copy-done.9, ...), custom_call_target="tpu_custom_call" | custom-call | tf_op jit(solution)/shard_map/product/pallas_call | solution.py:329
  (140 shorter events, 41.0 us)
Async XLA Ops:
  6.5 17.8 %collective-permute-start.3 = (bf16[2,12,9216]{2,0,1:T(2,128)(2,1)}, bf16[2,12,9216]{2,0,1:T(2,128)(2,1)S(1)}, u32[]{:S(2)}, u32[]{:S(2)}) collective-permute-start(bf16[2,12,9216]{2,0,1:T(2,128)(2,1)} %param.14), channel_id=1, source_target_pairs={{0,64},{64,128},{128,192},{192,0},{1,65},{65,129},{129,193},{193,1... | collective-permute-start | bytes 1327112 | tf_op jit(solution)/shard_map/ppermute | solution.py:370
  8.7 17.5 %collective-permute-start.4 = (bf16[2,12,9216]{2,0,1:T(2,128)(2,1)}, bf16[2,12,9216]{2,0,1:T(2,128)(2,1)S(1)}, u32[]{:S(2)}, u32[]{:S(2)}) collective-permute-start(bf16[2,12,9216]{2,0,1:T(2,128)(2,1)} %param.14), channel_id=1, source_target_pairs={{0,192},{64,0},{128,64},{192,128},{1,193},{65,1},{129,65},{193,129... | collective-permute-start | bytes 1327112 | tf_op jit(solution)/shard_map/ppermute | solution.py:370
  8.8 12.3 %collective-permute-start = (bf16[1,12,9216]{2,1,0:T(8,128)(2,1)}, bf16[1,12,9216]{2,1,0:T(8,128)(2,1)S(1)}, u32[]{:S(2)}, u32[]{:S(2)}) collective-permute-start(bf16[1,12,9216]{2,1,0:T(8,128)(2,1)} %refs_0_.1), channel_id=1, source_target_pairs={{0,8},{8,16},{16,24},{24,32},{32,40},{40,48},{48,56},{56,0},{1,9},... | collective-permute-start | bytes 663560 | tf_op jit(solution)/shard_map/ppermute | solution.py:370
  10.5 10.6 %collective-permute-start.1 = (bf16[1,12,9216]{2,1,0:T(8,128)(2,1)}, bf16[1,12,9216]{2,1,0:T(8,128)(2,1)S(1)}, u32[]{:S(2)}, u32[]{:S(2)}) collective-permute-start(bf16[1,12,9216]{2,1,0:T(8,128)(2,1)} %refs_0_.1), channel_id=1, source_target_pairs={{0,56},{8,0},{16,8},{24,16},{32,24},{40,32},{48,40},{56,48},{1,57}... | collective-permute-start | bytes 663560 | tf_op jit(solution)/shard_map/ppermute | solution.py:370
  21.1 8.8 %collective-permute-start.2 = (bf16[1,12,9216]{2,1,0:T(8,128)(2,1)S(1)}, bf16[1,12,9216]{2,1,0:T(8,128)(2,1)S(1)}, u32[]{:S(2)}, u32[]{:S(2)}) collective-permute-start(bf16[1,12,9216]{2,1,0:T(8,128)(2,1)S(1)} %collective-permute-done.refs_1_), channel_id=1, source_target_pairs={{0,8},{8,16},{16,24},{24,32},{32,40},{40,48},{48,56},{56,0},{1,9},... | collective-permute-start | bytes 663560 | tf_op jit(solution)/shard_map/ppermute | solution.py:370
  21.1 10.2 %collective-permute-start.7 = (bf16[1,12,9216]{2,1,0:T(8,128)(2,1)S(1)}, bf16[1,12,9216]{2,1,0:T(8,128)(2,1)S(1)}, u32[]{:S(2)}, u32[]{:S(2)}) collective-permute-start(bf16[1,12,9216]{2,1,0:T(8,128)(2,1)S(1)} %collective-permute-done.1.refs_2_), channel_id=1, source_target_pairs={{0,56},{8,0},{16,8},{24,16},{32,24},{40,32},{48,40},{56,48},{1,57}... | collective-permute-start | bytes 663560 | tf_op jit(solution)/shard_map/ppermute | solution.py:370
  24.5 8.6 %collective-permute-start.5 = (bf16[1,12,9216]{2,1,0:T(8,128)(2,1)S(1)}, bf16[1,12,9216]{2,1,0:T(8,128)(2,1)S(1)}, u32[]{:S(2)}, u32[]{:S(2)}) collective-permute-start(bf16[1,12,9216]{2,1,0:T(8,128)(2,1)S(1)} %slice.40), channel_id=1, source_target_pairs={{0,64},{64,128},{128,192},{192,0},{1,65},{65,129},{129,193},{193,1... | collective-permute-start | bytes 663560 | tf_op jit(solution)/shard_map/ppermute | solution.py:370
  29.8 20.6 %collective-permute-start.10 = (bf16[1,12,9216]{2,1,0:T(8,128)(2,1)S(1)}, bf16[1,12,9216]{2,1,0:T(8,128)(2,1)S(1)}, u32[]{:S(2)}, u32[]{:S(2)}) collective-permute-start(bf16[1,12,9216]{2,1,0:T(8,128)(2,1)S(1)} %collective-permute-done.2.refs_3_), channel_id=1, source_target_pairs={{0,16},{8,24},{16,32},{24,40},{32,48},{40,56},{48,0},{56,8},{1,17}... | collective-permute-start | bytes 663560 | tf_op jit(solution)/shard_map/ppermute | solution.py:370
  29.9 20.6 %collective-permute-start.8 = (bf16[1,12,9216]{2,1,0:T(8,128)(2,1)S(1)}, bf16[1,12,9216]{2,1,0:T(8,128)(2,1)S(1)}, u32[]{:S(2)}, u32[]{:S(2)}) collective-permute-start(bf16[1,12,9216]{2,1,0:T(8,128)(2,1)S(1)} %collective-permute-done.2.refs_3_), channel_id=1, source_target_pairs={{0,8},{8,16},{16,24},{24,32},{32,40},{40,48},{48,56},{56,0},{1,9},... | collective-permute-start | bytes 663560 | tf_op jit(solution)/shard_map/ppermute | solution.py:370
  31.3 19.2 %collective-permute-start.9 = (bf16[1,12,9216]{2,1,0:T(8,128)(2,1)S(1)}, bf16[1,12,9216]{2,1,0:T(8,128)(2,1)S(1)}, u32[]{:S(2)}, u32[]{:S(2)}) collective-permute-start(bf16[1,12,9216]{2,1,0:T(8,128)(2,1)S(1)} %collective-permute-done.7.refs_0_), channel_id=1, source_target_pairs={{0,56},{8,0},{16,8},{24,16},{32,24},{40,32},{48,40},{56,48},{1,57}... | collective-permute-start | bytes 663560 | tf_op jit(solution)/shard_map/ppermute | solution.py:370
  45.2 20.8 %all-to-all-start = ((bf16[8,48,1408]{2,1,0:T(8,128)(2,1)}), bf16[8,48,1408]{2,1,0:T(8,128)(2,1)S(1)}, u32[]{:S(2)}, u32[]{:S(2)}) async-start(bf16[8,48,1408]{2,1,0:T(8,128)(2,1)} %spectra.2), calls=%async_computation | async-start | bytes 2162688 | tf_op jit(solution)/shard_map/all_to_all | solution.py:393
  66.0 19.8 %all-to-all-start.1 = ((bf16[8,48,1408]{2,1,0:T(8,128)(2,1)}), bf16[8,48,1408]{2,1,0:T(8,128)(2,1)S(1)}, u32[]{:S(2)}, u32[]{:S(2)}) async-start(bf16[8,48,1408]{2,1,0:T(8,128)(2,1)} %spectra.3), calls=%async_computation.1 | async-start | bytes 2162688 | tf_op jit(solution)/shard_map/all_to_all | solution.py:395
  69.6 76.1 %all-gather.4.cloned.1.call-start = ((), (), s32[]{:S(2)}) async-start(), calls=%async_computation.4 | async-start | bytes 1179648 | tf_op jit(solution)/shard_map/all_gather | solution.py:421
  105.5 81.2 %all-gather.6.cloned.1.call-start = ((), (), s32[]{:S(2)}) async-start(), calls=%async_computation.5 | async-start | bytes 1769472 | tf_op jit(solution)/shard_map/all_gather | solution.py:435
  112.9 11.3 %collective-permute-start.15 = (bf16[256,640]{1,0:T(8,128)(2,1)S(1)}, bf16[256,640]{1,0:T(8,128)(2,1)}, u32[]{:S(2)}, u32[]{:S(2)}) collective-permute-start(bf16[256,640]{1,0:T(8,128)(2,1)S(1)} %pad_maximum_fusion.refs_1_), channel_id=1, source_target_pairs={{0,56},{8,0},{16,8},{24,16},{32,24},{40,32},{48,40},{56,48},{1,57}... | collective-permute-start | bytes 983048 | tf_op jit(solution)/shard_map/ppermute | solution.py:370
  114.2 13.0 %collective-permute-start.14 = (bf16[256,640]{1,0:T(8,128)(2,1)S(1)}, bf16[256,640]{1,0:T(8,128)(2,1)S(1)}, u32[]{:S(2)}, u32[]{:S(2)}) collective-permute-start(bf16[256,640]{1,0:T(8,128)(2,1)S(1)} %pad_maximum_fusion.refs_1_), channel_id=1, source_target_pairs={{0,8},{8,16},{16,24},{24,32},{32,40},{40,48},{48,56},{56,0},{1,9},... | collective-permute-start | bytes 983048 | tf_op jit(solution)/shard_map/ppermute | solution.py:370
  147.0 21.1 %collective-permute-start.23 = (bf16[512,896]{1,0:T(8,128)(2,1)S(1)}, bf16[512,896]{1,0:T(8,128)(2,1)S(1)}, u32[]{:S(2)}, u32[]{:S(2)}) collective-permute-start(bf16[512,896]{1,0:T(8,128)(2,1)S(1)} %slice.47.refs_10_), channel_id=1, source_target_pairs={{0,192},{64,0},{128,64},{192,128},{1,193},{65,1},{129,65},{193,129... | collective-permute-start | bytes 2752520 | tf_op jit(solution)/shard_map/ppermute | solution.py:370
  147.5 20.6 %collective-permute-start.22 = (bf16[512,896]{1,0:T(8,128)(2,1)S(1)}, bf16[512,896]{1,0:T(8,128)(2,1)S(1)}, u32[]{:S(2)}, u32[]{:S(2)}) collective-permute-start(bf16[512,896]{1,0:T(8,128)(2,1)S(1)} %slice.47.refs_10_), channel_id=1, source_target_pairs={{0,64},{64,128},{128,192},{192,0},{1,65},{65,129},{129,193},{193,1... | collective-permute-start | bytes 2752520 | tf_op jit(solution)/shard_map/ppermute | solution.py:370
  152.2 19.7 %collective-permute-start.18 = (bf16[256,640]{1,0:T(8,128)(2,1)}, bf16[256,640]{1,0:T(8,128)(2,1)S(1)}, u32[]{:S(2)}, u32[]{:S(2)}) collective-permute-start(bf16[256,640]{1,0:T(8,128)(2,1)} %collective-permute-done.15.refs_5_), channel_id=1, source_target_pairs={{0,56},{8,0},{16,8},{24,16},{32,24},{40,32},{48,40},{56,48},{1,57}... | collective-permute-start | bytes 983048 | tf_op jit(solution)/shard_map/ppermute | solution.py:370
  158.6 16.8 %collective-permute-start.20 = (bf16[128,640]{1,0:T(8,128)(2,1)S(1)}, bf16[128,640]{1,0:T(8,128)(2,1)S(1)}, u32[]{:S(2)}, u32[]{:S(2)}) collective-permute-start(bf16[128,640]{1,0:T(8,128)(2,1)S(1)} %slice.43), channel_id=1, source_target_pairs={{0,16},{8,24},{16,32},{24,40},{32,48},{40,56},{48,0},{56,8},{1,17}... | collective-permute-start | bytes 491528 | tf_op jit(solution)/shard_map/ppermute | solution.py:370
  168.1 18.6 %collective-permute-start.25 = (bf16[256,896]{1,0:T(8,128)(2,1)S(1)}, bf16[256,896]{1,0:T(8,128)(2,1)S(1)}, u32[]{:S(2)}, u32[]{:S(2)}) collective-permute-start(bf16[256,896]{1,0:T(8,128)(2,1)S(1)} %slice.49), channel_id=1, source_target_pairs={{0,192},{64,0},{128,64},{192,128},{1,193},{65,1},{129,65},{193,129... | collective-permute-start | bytes 1376264 | tf_op jit(solution)/shard_map/ppermute | solution.py:370
  168.3 18.4 %collective-permute-start.24 = (bf16[256,896]{1,0:T(8,128)(2,1)S(1)}, bf16[256,896]{1,0:T(8,128)(2,1)S(1)}, u32[]{:S(2)}, u32[]{:S(2)}) collective-permute-start(bf16[256,896]{1,0:T(8,128)(2,1)S(1)} %slice.48), channel_id=1, source_target_pairs={{0,64},{64,128},{128,192},{192,0},{1,65},{65,129},{129,193},{193,1... | collective-permute-start | bytes 1376264 | tf_op jit(solution)/shard_map/ppermute | solution.py:370
  172.6 10.5 %collective-permute-start.21 = (bf16[128,640]{1,0:T(8,128)(2,1)}, bf16[128,640]{1,0:T(8,128)(2,1)}, u32[]{:S(2)}, u32[]{:S(2)}) collective-permute-start(bf16[128,640]{1,0:T(8,128)(2,1)} %slice.44), channel_id=1, source_target_pairs={{0,48},{8,56},{16,0},{24,8},{32,16},{40,24},{48,32},{56,40},{1,49}... | collective-permute-start | bytes 491528 | tf_op jit(solution)/shard_map/ppermute | solution.py:370
  176.1 10.6 %collective-permute-start.19 = (bf16[256,640]{1,0:T(8,128)(2,1)S(1)}, bf16[256,640]{1,0:T(8,128)(2,1)}, u32[]{:S(2)}, u32[]{:S(2)}) collective-permute-start(bf16[256,640]{1,0:T(8,128)(2,1)S(1)} %collective-permute-done.18.refs_6_), channel_id=1, source_target_pairs={{0,56},{8,0},{16,8},{24,16},{32,24},{40,32},{48,40},{56,48},{1,57}... | collective-permute-start | bytes 983048 | tf_op jit(solution)/shard_map/ppermute | solution.py:370
  (37 other events, 308.2 us)
Sparse Core Ops, SparseCore 0:
  105.7 38.0 all-gather.3
  145.8 24.9 all-gather.5

commit v6 on v3

--- a/solution.py
+++ b/solution.py
@@ -109,11 +109,13 @@
     o_ref, dens, zs, sems = refs[n], *refs[2 * n + 1 :]
     spaces = refs[n + 1 : 2 * n + 1]
     v_refs, c_refs, (t_ref, w_ref) = spaces[:VC], spaces[VC : n - 2], spaces[n - 2 :]
-    tables = copy_in(refs[n - 2 : n], spaces[n - 2 :], sems.at[NCUT])
+    tables = copy_in([refs[n - 2]], [t_ref], sems.at[NCUT])
     cuts = []
     for cut in range(NCUT):
         lanes = pl.ds(cut * (GRID * GRID // NCUT), GRID * GRID // NCUT)
         cuts.append(copy_in([r.at[:, :, lanes] for r in refs[: n - 2]], [r.at[:, :, lanes] for r in spaces[: n - 2]], sems.at[cut]))
+    tables.append(pltpu.make_async_copy(refs[n - 1], w_ref, sems.at[NCUT, 1]))
+    tables[1].start()
     tables[0].wait()
 
     def body(step, _):
@@ -414,10 +416,11 @@
     cols, for_rows = pick_second(lines(slabs[1].reshape(GRID * QC, YL), kron), a_code, b_code, first)
     cols = lax.all_to_all(cols, tile, split_axis=0, concat_axis=0, tiled=True).reshape(KP, 4 * RB)
     b_bundle = lax.all_gather(cols[:, LA:], "z", axis=0, tiled=True)
-    near, far = ring(cols[:, :LA], "x", NX)
-    a_bundle = jnp.concatenate(near + far, axis=0)
+    a_part = cols[:, :LA]
+    a_bundle = jnp.concatenate([a_part] + [shift(a_part, "x", NX, step) for step in (1, -1, 2)], axis=0)
+    for_rows, a_bundle = lax.optimization_barrier((for_rows, a_bundle))
     a_up, a_down = shift(a_bundle, "z", NZ, 1), shift(a_bundle, "z", NZ, -1)
-    for_rows, a_up, a_down = lax.optimization_barrier((for_rows, a_up, a_down))
+    b_bundle, a_up, a_down = lax.optimization_barrier((b_bundle, a_up, a_down))
     a_cols, a_far = ring_on(a_bundle, a_up, a_down, "z", NZ)
     b_cols, b_far = ring(b_bundle, "x", NX)
     rows = lax.all_to_all(for_rows, ("x", "z"), split_axis=0, concat_axis=0, tiled=True)

time: 200 us -> 199 us (level)
  blocking collectives: 26 us -> 28.5 us
  starting transfers between devices: 49.8 us -> 47.4 us
    ppermute x27 -> x26, waiting for transfers between devices: 38.6 us -> 33.7 us  [shift(): lax.ppermute(value, axis, [(i, (i + step) % size) for i in range(size)])]
    all_gather x1, waiting for transfers between devices: 0.02 us -> 3.48 us  [per_device(): b_bundle = lax.all_gather(cols[:, LA:], 'z', axis=0, tiled=True)]
    all_to_all x1, blocking collectives: 16.6 us -> 19.1 us  [per_device(): lax.all_to_all(for_rows, ('x', 'z'), split_axis=0, concat_axis=0, tiled=T...]
    ppermute x27 -> x26, starting transfers between devices: 41.7 us -> 39.3 us  [shift(): lax.ppermute(value, axis, [(i, (i + step) % size) for i in range(size)])]
    unnamed x75 -> x72, local copies, waits for them, and re-layouts: 4.39 us -> 4.37 us
  transfers between devices with their start and end apart: 31 -> 30, of which waited for: 14 -> 14; matrix products, arithmetic and copies ran while one was open for 3% -> 3% of each run, Pallas kernels for 16% -> 15%
where the time goes in v6:
time: 199 us; the launch traced here: 196 us
  Pallas kernels  48.3 us (24%)
  starting transfers between devices  47.4 us (24%)
  waiting for transfers between devices  47.2 us (24%)
  blocking collectives  28.5 us (14%)
  between operations  13.9 us (7%)
  local copies, waits for them, and re-layouts  8.37 us (4%)
  other arithmetic  2.43 us (1%)
    ppermute x26, starting transfers between devices, shift(): lax.ppermute(value, axis, [(i, (i + step) % size) for i in range(size)])  39.3 us
    ppermute x26, waiting for transfers between devices, shift(): lax.ppermute(value, axis, [(i, (i + step) % size) for i in range(size)])  33.7 us
    pallas_call x2, Pallas kernels, spectra(): pl.pallas_call(spectra_kernel, in_specs=[pl.BlockSpec(memory_space=pl.ANY...  20 us
    all_to_all x1, blocking collectives, per_device(): lax.all_to_all(for_rows, ('x', 'z'), split_axis=0, concat_axis=0, tiled=T...  19.1 us
    all_to_all x1, blocking collectives, per_device(): lax.all_to_all(cols, tile, split_axis=0, concat_axis=0, tiled=True)  9.36 us
    pallas_call x1, Pallas kernels, pick_second(): pl.pallas_call(second_kernel, grid=(GP // GCH,), in_specs=pick_specs() +...  8.99 us
    pallas_call x1, Pallas kernels, pick_first(): pl.pallas_call(first_kernel, grid=(GP // GCH,), in_specs=pick_specs(), ou...  8.96 us
    pallas_call x1, Pallas kernels, product(): pl.pallas_call(product_kernel, in_specs=[pl.BlockSpec(memory_space=pltpu....  8.7 us
  transfers between devices with their start and end apart: 30, of which 14 were waited for; matrix products, arithmetic and copies ran while one was open for 3% of the time, Pallas kernels for 15%

profile of v6, /device:TPU:6, one launch (start us, length us, event | category | flops | bytes accessed | tf_op | source)
XLA Modules:
  0.0 196.2 jit_solution(9900068266893895797)
XLA Ops:
  6.5 2.2 %collective-permute-start.3 = (bf16[2,12,9216]{2,0,1:T(2,128)(2,1)}, bf16[2,12,9216]{2,0,1:T(2,128)(2,1)S(1)}, u32[]{:S(2)}, u32[]{:S(2)}) collective-permute-start(bf16[2,12,9216]{2,0,1:T(2,128)(2,1)} %param.14), channel_id=1, source_target_pairs={{0,64},{64,128},{128,192},{192,0},{1,65},{65,129},{129,193},{193,1... | collective-permute-start | bytes 1327112 | tf_op jit(solution)/shard_map/ppermute | solution.py:368
  10.5 3.9 %collective-permute-start.1 = (bf16[1,12,9216]{2,1,0:T(8,128)(2,1)}, bf16[1,12,9216]{2,1,0:T(8,128)(2,1)S(1)}, u32[]{:S(2)}, u32[]{:S(2)}) collective-permute-start(bf16[1,12,9216]{2,1,0:T(8,128)(2,1)} %refs_0_.1), channel_id=1, source_target_pairs={{0,56},{8,0},{16,8},{24,16},{32,24},{40,32},{48,40},{56,48},{1,57}... | collective-permute-start | bytes 663560 | tf_op jit(solution)/shard_map/ppermute | solution.py:368
  14.4 6.7 %collective-permute-done.refs_1_ = bf16[1,12,9216]{2,1,0:T(8,128)(2,1)S(1)} collective-permute-done((bf16[1,12,9216]{2,1,0:T(8,128)(2,1)}, bf16[1,12,9216]{2,1,0:T(8,128)(2,1)S(1)}, u32[]{:S(2)}, u32[]{:S(2)}) %collective-permute-start) | collective-permute-done | bytes 221216 | tf_op jit(solution)/shard_map/ppermute | solution.py:368
  21.1 3.2 %collective-permute-start.7 = (bf16[1,12,9216]{2,1,0:T(8,128)(2,1)S(1)}, bf16[1,12,9216]{2,1,0:T(8,128)(2,1)S(1)}, u32[]{:S(2)}, u32[]{:S(2)}) collective-permute-start(bf16[1,12,9216]{2,1,0:T(8,128)(2,1)S(1)} %collective-permute-done.1.refs_2_), channel_id=1, source_target_pairs={{0,56},{8,0},{16,8},{24,16},{32,24},{40,32},{48,40},{56,48},{1,57}... | collective-permute-start | bytes 663560 | tf_op jit(solution)/shard_map/ppermute | solution.py:368
  35.1 10.1 %spectra.2 = bf16[8,48,1408]{2,1,0:T(8,128)(2,1)} custom-call(bf16[1,12,9216]{2,1,0:T(8,128)(2,1)} %refs_0_.1, bf16[1,12,9216]{2,1,0:T(8,128)(2,1)} %copy-done.15, bf16[1,12,9216]{2,1,0:T(8,128)(2,1)} %copy-done.16, bf16[1,12,9216]{2,1,0:T(8,128)(2,1)} %copy-done.14, bf16[2,12,9216]{2,1,0:T(8,128)(2,1)} %copy.34.refs_4_, bf16[2,12,9216]{2,1,0:T(8,128)(2,1)} %copy-done.1, ...), custom_call_target="tpu_custom_call" | custom-call | tf_op jit(solution)/shard_map/spectra/pallas_call | solution.py:169
  45.2 4.5 %all-to-all-start = ((bf16[8,48,1408]{2,1,0:T(8,128)(2,1)}), bf16[8,48,1408]{2,1,0:T(8,128)(2,1)S(1)}, u32[]{:S(2)}, u32[]{:S(2)}) async-start(bf16[8,48,1408]{2,1,0:T(8,128)(2,1)} %spectra.2), calls=%async_computation | async-start | bytes 2162688 | tf_op jit(solution)/shard_map/all_to_all | solution.py:391
  52.0 10.0 %spectra.3 = bf16[8,48,1408]{2,1,0:T(8,128)(2,1)} custom-call(bf16[1,12,9216]{2,1,0:T(8,128)(2,1)} %copy-done.13, bf16[1,12,9216]{2,1,0:T(8,128)(2,1)} %copy-done.18, bf16[1,12,9216]{2,1,0:T(8,128)(2,1)} %copy-done.19, bf16[1,12,9216]{2,1,0:T(8,128)(2,1)} %copy-done.17, bf16[2,12,9216]{2,1,0:T(8,128)(2,1)} %copy.34.refs_4_, bf16[2,12,9216]{2,1,0:T(8,128)(2,1)} %copy-done.1, ...), custom_call_target="tpu_custom_call" | custom-call | tf_op jit(solution)/shard_map/spectra/pallas_call | solution.py:169
  62.1 3.9 %all-to-all-done = bf16[8,48,1408]{2,1,0:T(8,128)(2,1)S(1)} async-done(((bf16[8,48,1408]{2,1,0:T(8,128)(2,1)}), bf16[8,48,1408]{2,1,0:T(8,128)(2,1)S(1)}, u32[]{:S(2)}, u32[]{:S(2)}) %all-to-all-start) | async-done | bytes 1081376 | tf_op jit(solution)/shard_map/all_to_all | solution.py:391
  66.0 3.6 %all-to-all-start.1 = ((bf16[8,48,1408]{2,1,0:T(8,128)(2,1)}), bf16[8,48,1408]{2,1,0:T(8,128)(2,1)S(1)}, u32[]{:S(2)}, u32[]{:S(2)}) async-start(bf16[8,48,1408]{2,1,0:T(8,128)(2,1)} %spectra.3), calls=%async_computation.1 | async-start | bytes 2162688 | tf_op jit(solution)/shard_map/all_to_all | solution.py:393
  70.8 9.0 %pick_first.1.first_ref = f32[8,12288]{1,0:T(8,128)S(1)} custom-call(bf16[888,256]{1,0:T(8,128)(2,1)S(1)} %lines.3.s_ref, s32[1,12288]{1,0:T(1,128)S(1)} %multiply_add_fusion.a_ref, s32[1,12288]{1,0:T(1,128)S(1)} %get-tuple-element.23.b_ref), custom_call_target="tpu_custom_call" | custom-call | tf_op jit(solution)/shard_map/pick_first/pallas_call | solution.py:247
  79.8 6.1 %all-to-all-done.1 = bf16[8,48,1408]{2,1,0:T(8,128)(2,1)S(1)} async-done(((bf16[8,48,1408]{2,1,0:T(8,128)(2,1)}), bf16[8,48,1408]{2,1,0:T(8,128)(2,1)S(1)}, u32[]{:S(2)}, u32[]{:S(2)}) %all-to-all-start.1) | async-done | bytes 1081376 | tf_op jit(solution)/shard_map/all_to_all | solution.py:393
  86.6 9.0 %pick_second.1 = (bf16[8,8,1536]{2,1,0:T(8,128)(2,1)S(1)}, bf16[32,8,384]{2,1,0:T(8,128)(2,1)S(1)}) custom-call(bf16[888,256]{1,0:T(8,128)(2,1)S(1)} %lines.2.s_ref, s32[1,12288]{1,0:T(1,128)S(1)} %multiply_add_fusion.a_ref, s32[1,12288]{1,0:T(1,128)S(1)} %get-tuple-element.23.b_ref, f32[8,12288]{1,0:T(8,128)S(1)} %pick_first.1.first_ref), custom_call_target="tpu_custom_call" | custom-call | tf_op jit(solution)/shard_map/pick_second/pallas_call | solution.py:260
  95.7 9.4 %all_to_all.20 = bf16[8,8,1536]{2,1,0:T(8,128)(2,1)S(1)} all-to-all(bf16[8,8,1536]{2,1,0:T(8,128)(2,1)S(1)} %get-tuple-element.17), channel_id=1, replica_groups=mesh['x'=4,'z'=8,'y'=4,'core'=2] {'y','core'}, dimensions={0} | all-to-all | bytes 393216 | tf_op jit(solution)/shard_map/all_to_all | solution.py:417
  112.4 19.1 %all_to_all.21 = bf16[32,8,384]{2,1,0:T(8,128)(2,1)} all-to-all(bf16[32,8,384]{2,1,0:T(8,128)(2,1)S(1)} %get-tuple-element.18), channel_id=1, replica_groups=mesh['x'=4,'z'=8,'y'=4,'core'=2] {'x','z'}, dimensions={0} | all-to-all | bytes 393216 | tf_op jit(solution)/shard_map/all_to_all | solution.py:426
  133.7 6.1 %collective-permute-done.15.refs_5_ = bf16[256,512]{1,0:T(8,128)(2,1)S(1)} collective-permute-done((bf16[256,512]{1,0:T(8,128)(2,1)S(1)}, bf16[256,512]{1,0:T(8,128)(2,1)S(1)}, u32[]{:S(2)}, u32[]{:S(2)}) %collective-permute-start.15) | collective-permute-done | bytes 262176 | tf_op jit(solution)/shard_map/ppermute | solution.py:368
  141.3 3.5 %all-gather.4.cloned.1.call-done.refs_10_ = bf16[512,1024]{1,0:T(8,128)(2,1)} async-done(((bf16[64,1024]{1,0:T(8,128)(2,1)}), bf16[512,1024]{1,0:T(8,128)(2,1)}) %all-gather.4.cloned.1.call-update) | async-done | bytes 1048592 | tf_op jit(solution)/shard_map/all_gather | solution.py:418
  145.8 2.2 %collective-permute-start.22 = (bf16[512,1024]{1,0:T(8,128)(2,1)}, bf16[512,1024]{1,0:T(8,128)(2,1)S(1)}, u32[]{:S(2)}, u32[]{:S(2)}) collective-permute-start(bf16[512,1024]{1,0:T(8,128)(2,1)} %all-gather.4.cloned.1.call-done.refs_10_), channel_id=1, source_target_pairs={{0,64},{64,128},{128,192},{192,0},{1,65},{65,129},{129,193},{193,1... | collective-permute-start | bytes 3145736 | tf_op jit(solution)/shard_map/ppermute | solution.py:368
  148.4 2.9 %collective-permute-start.18 = (bf16[256,512]{1,0:T(8,128)(2,1)S(1)}, bf16[256,512]{1,0:T(8,128)(2,1)S(1)}, u32[]{:S(2)}, u32[]{:S(2)}) collective-permute-start(bf16[256,512]{1,0:T(8,128)(2,1)S(1)} %collective-permute-done.15.refs_5_), channel_id=1, source_target_pairs={{0,56},{8,0},{16,8},{24,16},{32,24},{40,32},{48,40},{56,48},{1,57}... | collective-permute-start | bytes 786440 | tf_op jit(solution)/shard_map/ppermute | solution.py:368
  151.6 5.2 %collective-permute-done.16.refs_3_ = bf16[256,512]{1,0:T(8,128)(2,1)S(1)} collective-permute-done((bf16[256,512]{1,0:T(8,128)(2,1)S(1)}, bf16[256,512]{1,0:T(8,128)(2,1)S(1)}, u32[]{:S(2)}, u32[]{:S(2)}) %collective-permute-start.16) | collective-permute-done | bytes 262176 | tf_op jit(solution)/shard_map/ppermute | solution.py:368
  156.9 3.3 %collective-permute-start.19 = (bf16[256,512]{1,0:T(8,128)(2,1)S(1)}, bf16[256,512]{1,0:T(8,128)(2,1)S(1)}, u32[]{:S(2)}, u32[]{:S(2)}) collective-permute-start(bf16[256,512]{1,0:T(8,128)(2,1)S(1)} %collective-permute-done.18.refs_6_), channel_id=1, source_target_pairs={{0,56},{8,0},{16,8},{24,16},{32,24},{40,32},{48,40},{56,48},{1,57}... | collective-permute-start | bytes 786440 | tf_op jit(solution)/shard_map/ppermute | solution.py:368
  160.4 7.8 %collective-permute-done.23.refs_12_ = bf16[512,1024]{1,0:T(8,128)(2,1)S(1)} collective-permute-done((bf16[512,1024]{1,0:T(8,128)(2,1)}, bf16[512,1024]{1,0:T(8,128)(2,1)S(1)}, u32[]{:S(2)}, u32[]{:S(2)}) %collective-permute-start.23) | collective-permute-done | bytes 1048608 | tf_op jit(solution)/shard_map/ppermute | solution.py:368
  169.4 3.0 %collective-permute-start.24 = (bf16[256,1024]{1,0:T(8,128)(2,1)}, bf16[256,1024]{1,0:T(8,128)(2,1)S(1)}, u32[]{:S(2)}, u32[]{:S(2)}) collective-permute-start(bf16[256,1024]{1,0:T(8,128)(2,1)} %slice.38), channel_id=1, source_target_pairs={{0,64},{64,128},{128,192},{192,0},{1,65},{65,129},{129,193},{193,1... | collective-permute-start | bytes 1572872 | tf_op jit(solution)/shard_map/ppermute | solution.py:368
  174.4 2.4 %collective-permute-start.21 = (bf16[128,512]{1,0:T(8,128)(2,1)}, bf16[128,512]{1,0:T(8,128)(2,1)S(1)}, u32[]{:S(2)}, u32[]{:S(2)}) collective-permute-start(bf16[128,512]{1,0:T(8,128)(2,1)} %slice.37), channel_id=1, source_target_pairs={{0,56},{8,0},{16,8},{24,16},{32,24},{40,32},{48,40},{56,48},{1,57}... | collective-permute-start | bytes 393224 | tf_op jit(solution)/shard_map/ppermute | solution.py:368
  180.7 8.7 %product.1 = f32[375,1500]{1,0:T(8,128)} custom-call(s32[2]{0:T(128)} %pad_add_fusion.xz_ref, f32[2048,1]{1,0:T(8,128)} %copy.40.w_ref, bf16[8,32,8,384]{3,2,1,0:T(8,128)(2,1)} %bitcast.21, bf16[256,512]{1,0:T(8,128)(2,1)} %copy-done.7, bf16[256,512]{1,0:T(8,128)(2,1)} %copy-done.21, bf16[256,512]{1,0:T(8,128)(2,1)} %copy-done.22, ...), custom_call_target="tpu_custom_call" | custom-call | tf_op jit(solution)/shard_map/product/pallas_call | solution.py:327
  (143 shorter events, 36.6 us)
Async XLA Ops:
  6.5 17.8 %collective-permute-start.3 = (bf16[2,12,9216]{2,0,1:T(2,128)(2,1)}, bf16[2,12,9216]{2,0,1:T(2,128)(2,1)S(1)}, u32[]{:S(2)}, u32[]{:S(2)}) collective-permute-start(bf16[2,12,9216]{2,0,1:T(2,128)(2,1)} %param.14), channel_id=1, source_target_pairs={{0,64},{64,128},{128,192},{192,0},{1,65},{65,129},{129,193},{193,1... | collective-permute-start | bytes 1327112 | tf_op jit(solution)/shard_map/ppermute | solution.py:368
  8.7 17.5 %collective-permute-start.4 = (bf16[2,12,9216]{2,0,1:T(2,128)(2,1)}, bf16[2,12,9216]{2,0,1:T(2,128)(2,1)S(1)}, u32[]{:S(2)}, u32[]{:S(2)}) collective-permute-start(bf16[2,12,9216]{2,0,1:T(2,128)(2,1)} %param.14), channel_id=1, source_target_pairs={{0,192},{64,0},{128,64},{192,128},{1,193},{65,1},{129,65},{193,129... | collective-permute-start | bytes 1327112 | tf_op jit(solution)/shard_map/ppermute | solution.py:368
  8.8 12.3 %collective-permute-start = (bf16[1,12,9216]{2,1,0:T(8,128)(2,1)}, bf16[1,12,9216]{2,1,0:T(8,128)(2,1)S(1)}, u32[]{:S(2)}, u32[]{:S(2)}) collective-permute-start(bf16[1,12,9216]{2,1,0:T(8,128)(2,1)} %refs_0_.1), channel_id=1, source_target_pairs={{0,8},{8,16},{16,24},{24,32},{32,40},{40,48},{48,56},{56,0},{1,9},... | collective-permute-start | bytes 663560 | tf_op jit(solution)/shard_map/ppermute | solution.py:368
  10.5 10.6 %collective-permute-start.1 = (bf16[1,12,9216]{2,1,0:T(8,128)(2,1)}, bf16[1,12,9216]{2,1,0:T(8,128)(2,1)S(1)}, u32[]{:S(2)}, u32[]{:S(2)}) collective-permute-start(bf16[1,12,9216]{2,1,0:T(8,128)(2,1)} %refs_0_.1), channel_id=1, source_target_pairs={{0,56},{8,0},{16,8},{24,16},{32,24},{40,32},{48,40},{56,48},{1,57}... | collective-permute-start | bytes 663560 | tf_op jit(solution)/shard_map/ppermute | solution.py:368
  21.1 8.8 %collective-permute-start.2 = (bf16[1,12,9216]{2,1,0:T(8,128)(2,1)S(1)}, bf16[1,12,9216]{2,1,0:T(8,128)(2,1)S(1)}, u32[]{:S(2)}, u32[]{:S(2)}) collective-permute-start(bf16[1,12,9216]{2,1,0:T(8,128)(2,1)S(1)} %collective-permute-done.refs_1_), channel_id=1, source_target_pairs={{0,8},{8,16},{16,24},{24,32},{32,40},{40,48},{48,56},{56,0},{1,9},... | collective-permute-start | bytes 663560 | tf_op jit(solution)/shard_map/ppermute | solution.py:368
  21.1 10.2 %collective-permute-start.7 = (bf16[1,12,9216]{2,1,0:T(8,128)(2,1)S(1)}, bf16[1,12,9216]{2,1,0:T(8,128)(2,1)S(1)}, u32[]{:S(2)}, u32[]{:S(2)}) collective-permute-start(bf16[1,12,9216]{2,1,0:T(8,128)(2,1)S(1)} %collective-permute-done.1.refs_2_), channel_id=1, source_target_pairs={{0,56},{8,0},{16,8},{24,16},{32,24},{40,32},{48,40},{56,48},{1,57}... | collective-permute-start | bytes 663560 | tf_op jit(solution)/shard_map/ppermute | solution.py:368
  24.5 8.6 %collective-permute-start.5 = (bf16[1,12,9216]{2,1,0:T(8,128)(2,1)S(1)}, bf16[1,12,9216]{2,1,0:T(8,128)(2,1)S(1)}, u32[]{:S(2)}, u32[]{:S(2)}) collective-permute-start(bf16[1,12,9216]{2,1,0:T(8,128)(2,1)S(1)} %slice.32), channel_id=1, source_target_pairs={{0,64},{64,128},{128,192},{192,0},{1,65},{65,129},{129,193},{193,1... | collective-permute-start | bytes 663560 | tf_op jit(solution)/shard_map/ppermute | solution.py:368
  29.8 20.6 %collective-permute-start.10 = (bf16[1,12,9216]{2,1,0:T(8,128)(2,1)S(1)}, bf16[1,12,9216]{2,1,0:T(8,128)(2,1)S(1)}, u32[]{:S(2)}, u32[]{:S(2)}) collective-permute-start(bf16[1,12,9216]{2,1,0:T(8,128)(2,1)S(1)} %collective-permute-done.2.refs_3_), channel_id=1, source_target_pairs={{0,16},{8,24},{16,32},{24,40},{32,48},{40,56},{48,0},{56,8},{1,17}... | collective-permute-start | bytes 663560 | tf_op jit(solution)/shard_map/ppermute | solution.py:368
  29.9 20.7 %collective-permute-start.8 = (bf16[1,12,9216]{2,1,0:T(8,128)(2,1)S(1)}, bf16[1,12,9216]{2,1,0:T(8,128)(2,1)S(1)}, u32[]{:S(2)}, u32[]{:S(2)}) collective-permute-start(bf16[1,12,9216]{2,1,0:T(8,128)(2,1)S(1)} %collective-permute-done.2.refs_3_), channel_id=1, source_target_pairs={{0,8},{8,16},{16,24},{24,32},{32,40},{40,48},{48,56},{56,0},{1,9},... | collective-permute-start | bytes 663560 | tf_op jit(solution)/shard_map/ppermute | solution.py:368
  31.3 19.2 %collective-permute-start.9 = (bf16[1,12,9216]{2,1,0:T(8,128)(2,1)S(1)}, bf16[1,12,9216]{2,1,0:T(8,128)(2,1)S(1)}, u32[]{:S(2)}, u32[]{:S(2)}) collective-permute-start(bf16[1,12,9216]{2,1,0:T(8,128)(2,1)S(1)} %collective-permute-done.7.refs_0_), channel_id=1, source_target_pairs={{0,56},{8,0},{16,8},{24,16},{32,24},{40,32},{48,40},{56,48},{1,57}... | collective-permute-start | bytes 663560 | tf_op jit(solution)/shard_map/ppermute | solution.py:368
  45.2 20.8 %all-to-all-start = ((bf16[8,48,1408]{2,1,0:T(8,128)(2,1)}), bf16[8,48,1408]{2,1,0:T(8,128)(2,1)S(1)}, u32[]{:S(2)}, u32[]{:S(2)}) async-start(bf16[8,48,1408]{2,1,0:T(8,128)(2,1)} %spectra.2), calls=%async_computation | async-start | bytes 2162688 | tf_op jit(solution)/shard_map/all_to_all | solution.py:391
  66.0 19.8 %all-to-all-start.1 = ((bf16[8,48,1408]{2,1,0:T(8,128)(2,1)}), bf16[8,48,1408]{2,1,0:T(8,128)(2,1)S(1)}, u32[]{:S(2)}, u32[]{:S(2)}) async-start(bf16[8,48,1408]{2,1,0:T(8,128)(2,1)} %spectra.3), calls=%async_computation.1 | async-start | bytes 2162688 | tf_op jit(solution)/shard_map/all_to_all | solution.py:393
  69.6 75.2 %all-gather.4.cloned.1.call-start = ((), (), s32[]{:S(2)}) async-start(), calls=%async_computation.4 | async-start | bytes 1179648 | tf_op jit(solution)/shard_map/all_gather | solution.py:418
  105.7 73.9 %all-gather.6.cloned.1.call-start = ((), (), s32[]{:S(2)}) async-start(), calls=%async_computation.5 | async-start | bytes 1769472 | tf_op jit(solution)/shard_map/all_gather | solution.py:427
  131.6 8.2 %collective-permute-start.15 = (bf16[256,512]{1,0:T(8,128)(2,1)S(1)}, bf16[256,512]{1,0:T(8,128)(2,1)S(1)}, u32[]{:S(2)}, u32[]{:S(2)}) collective-permute-start(bf16[256,512]{1,0:T(8,128)(2,1)S(1)} %pad_maximum_fusion.refs_1_), channel_id=1, source_target_pairs={{0,56},{8,0},{16,8},{24,16},{32,24},{40,32},{48,40},{56,48},{1,57}... | collective-permute-start | bytes 786440 | tf_op jit(solution)/shard_map/ppermute | solution.py:368
  132.7 8.6 %collective-permute-start.14 = (bf16[256,512]{1,0:T(8,128)(2,1)S(1)}, bf16[256,512]{1,0:T(8,128)(2,1)S(1)}, u32[]{:S(2)}, u32[]{:S(2)}) collective-permute-start(bf16[256,512]{1,0:T(8,128)(2,1)S(1)} %pad_maximum_fusion.refs_1_), channel_id=1, source_target_pairs={{0,8},{8,16},{16,24},{24,32},{32,40},{40,48},{48,56},{56,0},{1,9},... | collective-permute-start | bytes 786440 | tf_op jit(solution)/shard_map/ppermute | solution.py:368
  144.8 23.4 %collective-permute-start.23 = (bf16[512,1024]{1,0:T(8,128)(2,1)}, bf16[512,1024]{1,0:T(8,128)(2,1)S(1)}, u32[]{:S(2)}, u32[]{:S(2)}) collective-permute-start(bf16[512,1024]{1,0:T(8,128)(2,1)} %all-gather.4.cloned.1.call-done.refs_10_), channel_id=1, source_target_pairs={{0,192},{64,0},{128,64},{192,128},{1,193},{65,1},{129,65},{193,129... | collective-permute-start | bytes 3145736 | tf_op jit(solution)/shard_map/ppermute | solution.py:368
  145.8 22.8 %collective-permute-start.22 = (bf16[512,1024]{1,0:T(8,128)(2,1)}, bf16[512,1024]{1,0:T(8,128)(2,1)S(1)}, u32[]{:S(2)}, u32[]{:S(2)}) collective-permute-start(bf16[512,1024]{1,0:T(8,128)(2,1)} %all-gather.4.cloned.1.call-done.refs_10_), channel_id=1, source_target_pairs={{0,64},{64,128},{128,192},{192,0},{1,65},{65,129},{129,193},{193,1... | collective-permute-start | bytes 3145736 | tf_op jit(solution)/shard_map/ppermute | solution.py:368
  148.0 8.8 %collective-permute-start.16 = (bf16[256,512]{1,0:T(8,128)(2,1)S(1)}, bf16[256,512]{1,0:T(8,128)(2,1)S(1)}, u32[]{:S(2)}, u32[]{:S(2)}) collective-permute-start(bf16[256,512]{1,0:T(8,128)(2,1)S(1)} %collective-permute-done.14.refs_2_), channel_id=1, source_target_pairs={{0,8},{8,16},{16,24},{24,32},{32,40},{40,48},{48,56},{56,0},{1,9},... | collective-permute-start | bytes 786440 | tf_op jit(solution)/shard_map/ppermute | solution.py:368
  148.4 8.5 %collective-permute-start.18 = (bf16[256,512]{1,0:T(8,128)(2,1)S(1)}, bf16[256,512]{1,0:T(8,128)(2,1)S(1)}, u32[]{:S(2)}, u32[]{:S(2)}) collective-permute-start(bf16[256,512]{1,0:T(8,128)(2,1)S(1)} %collective-permute-done.15.refs_5_), channel_id=1, source_target_pairs={{0,56},{8,0},{16,8},{24,16},{32,24},{40,32},{48,40},{56,48},{1,57}... | collective-permute-start | bytes 786440 | tf_op jit(solution)/shard_map/ppermute | solution.py:368
  156.8 15.9 %collective-permute-start.17 = (bf16[256,512]{1,0:T(8,128)(2,1)S(1)}, bf16[256,512]{1,0:T(8,128)(2,1)S(1)}, u32[]{:S(2)}, u32[]{:S(2)}) collective-permute-start(bf16[256,512]{1,0:T(8,128)(2,1)S(1)} %collective-permute-done.16.refs_3_), channel_id=1, source_target_pairs={{0,8},{8,16},{16,24},{24,32},{32,40},{40,48},{48,56},{56,0},{1,9},... | collective-permute-start | bytes 786440 | tf_op jit(solution)/shard_map/ppermute | solution.py:368
  156.9 16.8 %collective-permute-start.19 = (bf16[256,512]{1,0:T(8,128)(2,1)S(1)}, bf16[256,512]{1,0:T(8,128)(2,1)S(1)}, u32[]{:S(2)}, u32[]{:S(2)}) collective-permute-start(bf16[256,512]{1,0:T(8,128)(2,1)S(1)} %collective-permute-done.18.refs_6_), channel_id=1, source_target_pairs={{0,56},{8,0},{16,8},{24,16},{32,24},{40,32},{48,40},{56,48},{1,57}... | collective-permute-start | bytes 786440 | tf_op jit(solution)/shard_map/ppermute | solution.py:368
  168.2 11.4 %collective-permute-start.25 = (bf16[256,1024]{1,0:T(8,128)(2,1)S(1)}, bf16[256,1024]{1,0:T(8,128)(2,1)S(1)}, u32[]{:S(2)}, u32[]{:S(2)}) collective-permute-start(bf16[256,1024]{1,0:T(8,128)(2,1)S(1)} %slice.39), channel_id=1, source_target_pairs={{0,192},{64,0},{128,64},{192,128},{1,193},{65,1},{129,65},{193,129... | collective-permute-start | bytes 1572872 | tf_op jit(solution)/shard_map/ppermute | solution.py:368
  169.4 10.2 %collective-permute-start.24 = (bf16[256,1024]{1,0:T(8,128)(2,1)}, bf16[256,1024]{1,0:T(8,128)(2,1)S(1)}, u32[]{:S(2)}, u32[]{:S(2)}) collective-permute-start(bf16[256,1024]{1,0:T(8,128)(2,1)} %slice.38), channel_id=1, source_target_pairs={{0,64},{64,128},{128,192},{192,0},{1,65},{65,129},{129,193},{193,1... | collective-permute-start | bytes 1572872 | tf_op jit(solution)/shard_map/ppermute | solution.py:368
  (40 other events, 617.0 us)
Sparse Core Ops, SparseCore 0:
  105.9 38.8 all-gather.3
  146.6 24.9 all-gather.5

commit v7 on v6

--- a/solution.py
+++ b/solution.py
@@ -290,54 +290,99 @@
     return whole + [[(2, z) for z in range(NZ // 2)], [(2, z) for z in range(NZ // 2, NZ)]]
 
 
-def product_kernel(xz_ref, w_ref, *refs):
-    na, nb = len(a_pieces()), len(b_pieces())
-    n = 1 + na + nb
-    o_ref, spaces, (wr, acc_ref, sems) = refs[n], refs[n + 1 : 2 * n + 1], refs[2 * n + 1 :]
+A_NEAR = 7
+B_NEAR = 3
+
+
+def owner_of(xz_ref, dx, z):
+    return lax.rem(xz_ref[0] + (NX - dx), NX) * NZ + z
+
+
+def z_back(xz_ref, dz):
+    return lax.rem(xz_ref[1] + (NZ - dz), NZ)
+
+
+def matched(lhs, ref):
+    return lax.dot_general(jnp.concatenate(lhs, axis=0), ref[...], (((0,), (0,)), ((), ())), preferred_element_type=F32)
+
+
+def near_kernel(xz_ref, w_ref, *refs):
+    n = 1 + A_NEAR + B_NEAR
+    acc_ref, wr, spaces, sems = refs[n], refs[n + 1], refs[n + 2 : 2 * n + 2], refs[2 * n + 2]
     copies = copy_in(refs[:n], spaces, sems)
-    r_ref, a_refs, b_refs = spaces[0], spaces[1 : 1 + na], spaces[1 + na :]
+    r_ref = spaces[0]
     copies[0].wait()
     for p in range(32):
         rows = jnp.concatenate([r_ref[t, p].astype(F32) for t in range(NT)], axis=0)
         wr[p] = (rows * w_ref[KP * p : KP * (p + 1), :]).astype(BF)
 
-    def part(pieces, ref, z_of):
-        lhs = [wr[lax.rem(xz_ref[0] + (NX - dx), NX) * NZ + z_of(dz)] for dx, dz in pieces]
-        return lax.dot_general(
-            jnp.concatenate(lhs, axis=0), ref[...], (((0,), (0,)), ((), ())), preferred_element_type=F32
-        )
-
     def total(pieces, operands, waits, z_of):
         acc = None
         for piece, ref, copy in zip(pieces, operands, waits):
             copy.wait()
-            more = part(piece, ref, z_of)
+            more = matched([wr[owner_of(xz_ref, dx, z_of(z))] for dx, z in piece], ref)
             acc = more if acc is None else acc + more
         return acc
 
-    acc_ref[:, :LA] = total(a_pieces(), a_refs, copies[1 : 1 + na], lambda dz: lax.rem(xz_ref[1] + (NZ - dz), NZ))
-    acc_ref[:, LA:] = total(b_pieces(), b_refs, copies[1 + na :], lambda z: z)
-    for q in range(4):
-        o_ref[:, 375 * q : 375 * (q + 1)] = acc_ref[:375, RB * q : RB * q + 375]
-
-
-def product(place, rows, weight, a_cols, b_cols):
+    a_end = 1 + A_NEAR
+    acc_ref[:, :LA] = total(a_pieces()[:A_NEAR], spaces[1:a_end], copies[1:a_end], lambda dz: z_back(xz_ref, dz))
+    acc_ref[:, LA:] = total(b_pieces()[:B_NEAR], spaces[a_end:], copies[a_end:], lambda z: z)
+
+
+def product_near(place, rows, weight, a_cols, b_cols):
     operands = [rows, *a_cols, *b_cols]
     vmem = pl.BlockSpec(memory_space=pltpu.VMEM)
     return pl.pallas_call(
-        product_kernel,
+        near_kernel,
         in_specs=[pl.BlockSpec(memory_space=pltpu.SMEM), vmem] + [pl.BlockSpec(memory_space=pl.ANY)] * len(operands),
-        out_specs=vmem,
+        out_specs=[vmem, vmem],
+        out_shape=[jax.ShapeDtypeStruct((RB, 4 * RB), F32), jax.ShapeDtypeStruct((32, KP, RB), BF)],
+        scratch_shapes=[pltpu.VMEM(x.shape, BF) for x in operands] + [pltpu.SemaphoreType.DMA((len(operands),))],
+        compiler_params=pltpu.CompilerParams(vmem_limit_bytes=58 * 2**20),
+        name="product_near",
+    )(place, weight, *operands)
+
+
+def far_blocks():
+    return a_pieces()[A_NEAR:], b_pieces()[B_NEAR:]
+
+
+def far_kernel(xz_ref, acc_any, wr_any, *refs):
+    a_far, b_far = far_blocks()
+    n = len(a_far) + len(b_far)
+    o_ref, acc, lhs, spaces, sems, row_sems = refs[n], refs[n + 1], refs[n + 2], refs[n + 3 : 2 * n + 3], *refs[2 * n + 3 :]
+    owners = [owner_of(xz_ref, dx, z_back(xz_ref, dz)) for piece in a_far for dx, dz in piece]
+    owners += [owner_of(xz_ref, dx, z) for piece in b_far for dx, z in piece]
+    row_copies = [pltpu.make_async_copy(wr_any.at[p], lhs.at[i], row_sems.at[i]) for i, p in enumerate(owners)]
+    for copy in row_copies:
+        copy.start()
+    copies = copy_in([*refs[:n], acc_any], [*spaces, acc], sems)
+    for copy in row_copies + copies:
+        copy.wait()
+
+    first = 0
+    for half, pieces, operands in ((slice(0, LA), a_far, spaces[: len(a_far)]), (slice(LA, None), b_far, spaces[len(a_far) :])):
+        for piece, ref in zip(pieces, operands):
+            acc[:, half] += matched([lhs[first + i] for i in range(len(piece))], ref)
+            first += len(piece)
+    for q in range(4):
+        o_ref[:, 375 * q : 375 * (q + 1)] = acc[:375, RB * q : RB * q + 375]
+
+
+def product_far(place, acc, wr, a_cols, b_cols):
+    operands = [*a_cols, *b_cols]
+    count = sum(len(piece) for pieces in far_blocks() for piece in pieces)
+    return pl.pallas_call(
+        far_kernel,
+        in_specs=[pl.BlockSpec(memory_space=pltpu.SMEM)] + [pl.BlockSpec(memory_space=pl.ANY)] * (2 + len(operands)),
+        out_specs=pl.BlockSpec(memory_space=pltpu.VMEM),
         out_shape=jax.ShapeDtypeStruct((375, 1500), F32),
-        scratch_shapes=[pltpu.VMEM(x.shape, BF) for x in operands]
-        + [
-            pltpu.VMEM((32, KP, RB), BF),
-            pltpu.VMEM((RB, 4 * RB), F32),
-            pltpu.SemaphoreType.DMA((len(operands),)),
-        ],
+        scratch_shapes=[pltpu.VMEM((RB, 4 * RB), F32), pltpu.VMEM((count, KP, RB), BF)]
+        + [pltpu.VMEM(x.shape, BF) for x in operands]
+        + [pltpu.SemaphoreType.DMA((len(operands) + 1,)), pltpu.SemaphoreType.DMA((count,))],
         compiler_params=pltpu.CompilerParams(vmem_limit_bytes=58 * 2**20),
-        name="product",
-    )(place, weight, *operands)
+        name="product_far",
+    )(place, acc, wr, *operands)
 
 
 def ring(value, axis, size):
@@ -426,7 +471,8 @@
     rows = lax.all_to_all(for_rows, ("x", "z"), split_axis=0, concat_axis=0, tiled=True)
     rows = lax.all_gather(rows, ("y", "core"), axis=0, tiled=False)
     place = jnp.stack([lax.axis_index("x"), lax.axis_index("z")]).astype(jnp.int32)
-    return product(place, rows, weight, a_cols + a_far, b_cols + b_far)
+    acc, wr = product_near(place, rows, weight, a_cols, b_cols)
+    return product_far(place, acc, wr, a_far, b_far)
 
 
 def solution(mesh):

time: 199 us -> 200 us (level)
  Pallas kernels: 48.3 us -> 52.8 us
  starting transfers between devices: 47.4 us -> 44.9 us
    pallas_call x1 -> x2, Pallas kernels: 8.7 us -> 13.2 us  [the longest x1 7.46 us: product_near(): pl.pallas_call(near_kernel, in_specs=[pl.BlockSpec(memory_space=pltpu.SME...]
    ppermute x26, starting transfers between devices: 39.3 us -> 36.8 us  [shift(): lax.ppermute(value, axis, [(i, (i + step) % size) for i in range(size)])]
    unnamed x72 -> x66, local copies, waits for them, and re-layouts: 4.37 us -> 4.19 us
  transfers between devices with their start and end apart: 30 -> 30, of which waited for: 14 -> 13; matrix products, arithmetic and copies ran while one was open for 3% -> 4% of each run, Pallas kernels for 15% -> 19%
where the time goes in v7:
time: 200 us; the launch traced here: 198 us
  Pallas kernels  52.8 us (26%)
  waiting for transfers between devices  47.3 us (24%)
  starting transfers between devices  44.9 us (22%)
  blocking collectives  26.6 us (13%)
  between operations  13.9 us (7%)
  local copies, waits for them, and re-layouts  9.73 us (5%)
  other arithmetic  2.35 us (1%)
    ppermute x26, starting transfers between devices, shift(): lax.ppermute(value, axis, [(i, (i + step) % size) for i in range(size)])  36.8 us
    ppermute x26, waiting for transfers between devices, shift(): lax.ppermute(value, axis, [(i, (i + step) % size) for i in range(size)])  34.6 us
    pallas_call x2, Pallas kernels, spectra(): pl.pallas_call(spectra_kernel, in_specs=[pl.BlockSpec(memory_space=pl.ANY...  20.1 us
    all_to_all x1, blocking collectives, per_device(): lax.all_to_all(for_rows, ('x', 'z'), split_axis=0, concat_axis=0, tiled=T...  17.4 us
    all_to_all x1, blocking collectives, per_device(): lax.all_to_all(cols, tile, split_axis=0, concat_axis=0, tiled=True)  9.23 us
    pallas_call x1, Pallas kernels, pick_second(): pl.pallas_call(second_kernel, grid=(GP // GCH,), in_specs=pick_specs() +...  8.99 us
    pallas_call x1, Pallas kernels, pick_first(): pl.pallas_call(first_kernel, grid=(GP // GCH,), in_specs=pick_specs(), ou...  8.96 us
    pallas_call x1, Pallas kernels, product_near(): pl.pallas_call(near_kernel, in_specs=[pl.BlockSpec(memory_space=pltpu.SME...  7.46 us
  transfers between devices with their start and end apart: 30, of which 13 were waited for; matrix products, arithmetic and copies ran while one was open for 4% of the time, Pallas kernels for 19%

profile of v7, /device:TPU:6, one launch (start us, length us, event | category | flops | bytes accessed | tf_op | source)
XLA Modules:
  0.0 197.6 jit_solution(4055042327585832447)
XLA Ops:
  6.5 2.2 %collective-permute-start.3 = (bf16[2,12,9216]{2,0,1:T(2,128)(2,1)}, bf16[2,12,9216]{2,0,1:T(2,128)(2,1)S(1)}, u32[]{:S(2)}, u32[]{:S(2)}) collective-permute-start(bf16[2,12,9216]{2,0,1:T(2,128)(2,1)} %param.14), channel_id=1, source_target_pairs={{0,64},{64,128},{128,192},{192,0},{1,65},{65,129},{129,193},{193,1... | collective-permute-start | bytes 1327112 | tf_op jit(solution)/shard_map/ppermute | solution.py:413
  10.5 3.9 %collective-permute-start.1 = (bf16[1,12,9216]{2,1,0:T(8,128)(2,1)}, bf16[1,12,9216]{2,1,0:T(8,128)(2,1)}, u32[]{:S(2)}, u32[]{:S(2)}) collective-permute-start(bf16[1,12,9216]{2,1,0:T(8,128)(2,1)} %refs_0_.1), channel_id=1, source_target_pairs={{0,56},{8,0},{16,8},{24,16},{32,24},{40,32},{48,40},{56,48},{1,57}... | collective-permute-start | bytes 663560 | tf_op jit(solution)/shard_map/ppermute | solution.py:413
  14.4 6.7 %collective-permute-done.refs_1_ = bf16[1,12,9216]{2,1,0:T(8,128)(2,1)S(1)} collective-permute-done((bf16[1,12,9216]{2,1,0:T(8,128)(2,1)}, bf16[1,12,9216]{2,1,0:T(8,128)(2,1)S(1)}, u32[]{:S(2)}, u32[]{:S(2)}) %collective-permute-start) | collective-permute-done | bytes 221216 | tf_op jit(solution)/shard_map/ppermute | solution.py:413
  21.1 3.2 %collective-permute-start.7 = (bf16[1,12,9216]{2,1,0:T(8,128)(2,1)}, bf16[1,12,9216]{2,1,0:T(8,128)(2,1)S(1)}, u32[]{:S(2)}, u32[]{:S(2)}) collective-permute-start(bf16[1,12,9216]{2,1,0:T(8,128)(2,1)} %collective-permute-done.1.refs_2_), channel_id=1, source_target_pairs={{0,56},{8,0},{16,8},{24,16},{32,24},{40,32},{48,40},{56,48},{1,57}... | collective-permute-start | bytes 663560 | tf_op jit(solution)/shard_map/ppermute | solution.py:413
  35.1 10.1 %spectra.2 = bf16[8,48,1408]{2,1,0:T(8,128)(2,1)} custom-call(bf16[1,12,9216]{2,1,0:T(8,128)(2,1)} %refs_0_.1, bf16[1,12,9216]{2,1,0:T(8,128)(2,1)} %copy-done.14, bf16[1,12,9216]{2,1,0:T(8,128)(2,1)} %collective-permute-done.1.refs_2_, bf16[1,12,9216]{2,1,0:T(8,128)(2,1)} %copy-done.13, bf16[2,12,9216]{2,1,0:T(8,128)(2,1)} %copy.34.refs_4_, ...), custom_call_target="tpu_custom_call" | custom-call | tf_op jit(solution)/shard_map/spectra/pallas_call | solution.py:169
  45.2 4.5 %all-to-all-start = ((bf16[8,48,1408]{2,1,0:T(8,128)(2,1)}), bf16[8,48,1408]{2,1,0:T(8,128)(2,1)S(1)}, u32[]{:S(2)}, u32[]{:S(2)}) async-start(bf16[8,48,1408]{2,1,0:T(8,128)(2,1)} %spectra.2), calls=%async_computation | async-start | bytes 2162688 | tf_op jit(solution)/shard_map/all_to_all | solution.py:436
  52.0 10.0 %spectra.3 = bf16[8,48,1408]{2,1,0:T(8,128)(2,1)} custom-call(bf16[1,12,9216]{2,1,0:T(8,128)(2,1)} %copy-done.12, bf16[1,12,9216]{2,1,0:T(8,128)(2,1)} %copy-done.16, bf16[1,12,9216]{2,1,0:T(8,128)(2,1)} %copy-done.17, bf16[1,12,9216]{2,1,0:T(8,128)(2,1)} %copy-done.15, bf16[2,12,9216]{2,1,0:T(8,128)(2,1)} %copy.34.refs_4_, bf16[2,12,9216]{2,1,0:T(8,128)(2,1)} %copy-done.1, ...), custom_call_target="tpu_custom_call" | custom-call | tf_op jit(solution)/shard_map/spectra/pallas_call | solution.py:169
  62.1 3.9 %all-to-all-done = bf16[8,48,1408]{2,1,0:T(8,128)(2,1)S(1)} async-done(((bf16[8,48,1408]{2,1,0:T(8,128)(2,1)}), bf16[8,48,1408]{2,1,0:T(8,128)(2,1)S(1)}, u32[]{:S(2)}, u32[]{:S(2)}) %all-to-all-start) | async-done | bytes 1081376 | tf_op jit(solution)/shard_map/all_to_all | solution.py:436
  66.0 3.6 %all-to-all-start.1 = ((bf16[8,48,1408]{2,1,0:T(8,128)(2,1)}), bf16[8,48,1408]{2,1,0:T(8,128)(2,1)S(1)}, u32[]{:S(2)}, u32[]{:S(2)}) async-start(bf16[8,48,1408]{2,1,0:T(8,128)(2,1)} %spectra.3), calls=%async_computation.1 | async-start | bytes 2162688 | tf_op jit(solution)/shard_map/all_to_all | solution.py:438
  70.8 9.0 %pick_first.1.first_ref = f32[8,12288]{1,0:T(8,128)S(1)} custom-call(bf16[888,256]{1,0:T(8,128)(2,1)S(1)} %lines.3.s_ref, s32[1,12288]{1,0:T(1,128)S(1)} %multiply_add_fusion.a_ref, s32[1,12288]{1,0:T(1,128)S(1)} %get-tuple-element.27.b_ref), custom_call_target="tpu_custom_call" | custom-call | tf_op jit(solution)/shard_map/pick_first/pallas_call | solution.py:247
  79.7 6.1 %all-to-all-done.1 = bf16[8,48,1408]{2,1,0:T(8,128)(2,1)S(1)} async-done(((bf16[8,48,1408]{2,1,0:T(8,128)(2,1)}), bf16[8,48,1408]{2,1,0:T(8,128)(2,1)S(1)}, u32[]{:S(2)}, u32[]{:S(2)}) %all-to-all-start.1) | async-done | bytes 1081376 | tf_op jit(solution)/shard_map/all_to_all | solution.py:438
  86.7 9.0 %pick_second.1 = (bf16[8,8,1536]{2,1,0:T(8,128)(2,1)S(1)}, bf16[32,8,384]{2,1,0:T(8,128)(2,1)S(1)}) custom-call(bf16[888,256]{1,0:T(8,128)(2,1)S(1)} %lines.2.s_ref, s32[1,12288]{1,0:T(1,128)S(1)} %multiply_add_fusion.a_ref, s32[1,12288]{1,0:T(1,128)S(1)} %get-tuple-element.27.b_ref, f32[8,12288]{1,0:T(8,128)S(1)} %pick_first.1.first_ref), custom_call_target="tpu_custom_call" | custom-call | tf_op jit(solution)/shard_map/pick_second/pallas_call | solution.py:260
  95.6 9.2 %all_to_all.20 = bf16[8,8,1536]{2,1,0:T(8,128)(2,1)S(1)} all-to-all(bf16[8,8,1536]{2,1,0:T(8,128)(2,1)S(1)} %get-tuple-element.19), channel_id=1, replica_groups=mesh['x'=4,'z'=8,'y'=4,'core'=2] {'y','core'}, dimensions={0} | all-to-all | bytes 393216 | tf_op jit(solution)/shard_map/all_to_all | solution.py:462
  110.0 2.3 %collective-permute-done.12 = bf16[64,512]{1,0:T(8,128)(2,1)S(1)} collective-permute-done((bf16[64,512]{1,0:T(8,128)(2,1)S(1)}, bf16[64,512]{1,0:T(8,128)(2,1)S(1)}, u32[]{:S(2)}, u32[]{:S(2)}) %collective-permute-start.12) | collective-permute-done | bytes 65568 | tf_op jit(solution)/shard_map/ppermute | solution.py:413
  113.6 17.4 %all_to_all.21 = bf16[32,8,384]{2,1,0:T(8,128)(2,1)} all-to-all(bf16[32,8,384]{2,1,0:T(8,128)(2,1)S(1)} %get-tuple-element.20), channel_id=1, replica_groups=mesh['x'=4,'z'=8,'y'=4,'core'=2] {'x','z'}, dimensions={0} | all-to-all | bytes 393216 | tf_op jit(solution)/shard_map/all_to_all | solution.py:471
  130.9 2.3 %collective-permute-start.14 = (bf16[256,512]{1,0:T(8,128)(2,1)S(1)}, bf16[256,512]{1,0:T(8,128)(2,1)S(1)}, u32[]{:S(2)}, u32[]{:S(2)}) collective-permute-start(bf16[256,512]{1,0:T(8,128)(2,1)S(1)} %pad_maximum_fusion.refs_1_), channel_id=1, source_target_pairs={{0,8},{8,16},{16,24},{24,32},{32,40},{40,48},{48,56},{56,0},{1,9},... | collective-permute-start | bytes 786440 | tf_op jit(solution)/shard_map/ppermute | solution.py:413
  134.3 6.4 %collective-permute-done.14.refs_2_ = bf16[256,512]{1,0:T(8,128)(2,1)S(1)} collective-permute-done((bf16[256,512]{1,0:T(8,128)(2,1)S(1)}, bf16[256,512]{1,0:T(8,128)(2,1)S(1)}, u32[]{:S(2)}, u32[]{:S(2)}) %collective-permute-start.14) | collective-permute-done | bytes 262176 | tf_op jit(solution)/shard_map/ppermute | solution.py:413
  140.9 2.7 %all-gather.4.cloned.1.call-done.refs_8_ = bf16[512,1024]{1,0:T(8,128)(2,1)} async-done(((bf16[64,1024]{1,0:T(8,128)(2,1)}), bf16[512,1024]{1,0:T(8,128)(2,1)}) %all-gather.4.cloned.1.call-update) | async-done | bytes 1048592 | tf_op jit(solution)/shard_map/all_gather | solution.py:463
  145.7 2.2 %collective-permute-start.16 = (bf16[256,512]{1,0:T(8,128)(2,1)S(1)}, bf16[256,512]{1,0:T(8,128)(2,1)S(1)}, u32[]{:S(2)}, u32[]{:S(2)}) collective-permute-start(bf16[256,512]{1,0:T(8,128)(2,1)S(1)} %collective-permute-done.14.refs_2_), channel_id=1, source_target_pairs={{0,8},{8,16},{16,24},{24,32},{32,40},{40,48},{48,56},{56,0},{1,9},... | collective-permute-start | bytes 786440 | tf_op jit(solution)/shard_map/ppermute | solution.py:413
  149.2 5.4 %collective-permute-done.16.refs_3_ = bf16[256,512]{1,0:T(8,128)(2,1)S(1)} collective-permute-done((bf16[256,512]{1,0:T(8,128)(2,1)S(1)}, bf16[256,512]{1,0:T(8,128)(2,1)S(1)}, u32[]{:S(2)}, u32[]{:S(2)}) %collective-permute-start.16) | collective-permute-done | bytes 262176 | tf_op jit(solution)/shard_map/ppermute | solution.py:413
  158.3 7.7 %collective-permute-done.20.refs_9_ = bf16[512,1024]{1,0:T(8,128)(2,1)S(1)} collective-permute-done((bf16[512,1024]{1,0:T(8,128)(2,1)}, bf16[512,1024]{1,0:T(8,128)(2,1)S(1)}, u32[]{:S(2)}, u32[]{:S(2)}) %collective-permute-start.20) | collective-permute-done | bytes 1048608 | tf_op jit(solution)/shard_map/ppermute | solution.py:413
  170.8 2.3 %collective-permute-start.22 = (bf16[128,512]{1,0:T(8,128)(2,1)}, bf16[128,512]{1,0:T(8,128)(2,1)S(1)}, u32[]{:S(2)}, u32[]{:S(2)}) collective-permute-start(bf16[128,512]{1,0:T(8,128)(2,1)} %slice.36), channel_id=1, source_target_pairs={{0,8},{8,16},{16,24},{24,32},{32,40},{40,48},{48,56},{56,0},{1,9},... | collective-permute-start | bytes 393224 | tf_op jit(solution)/shard_map/ppermute | solution.py:413
  176.7 7.5 %product_near.1 = (f32[384,1536]{1,0:T(8,128)}, bf16[32,64,384]{2,1,0:T(8,128)(2,1)}) custom-call(s32[2]{0:T(128)} %pad_add_fusion.xz_ref, f32[2048,1]{1,0:T(8,128)} %copy.40.w_ref, bf16[8,32,8,384]{3,2,1,0:T(8,128)(2,1)} %bitcast.21, bf16[256,512]{1,0:T(8,128)(2,1)} %copy-done.7, bf16[256,512]{1,0:T(8,128)(2,1)} %copy-done.18, bf16[256,512]{1,0:T(8,128)(2,1)} %copy-done.20, ...), custom_call_target="tpu_custom_call" | custom-call | tf_op jit(solution)/shard_map/product_near/pallas_call | solution.py:335
  185.0 5.7 %product_far.1 = f32[375,1500]{1,0:T(8,128)} custom-call(s32[2]{0:T(128)} %pad_add_fusion.xz_ref, f32[384,1536]{1,0:T(8,128)} %get-tuple-element.25.acc_any, bf16[32,64,384]{2,1,0:T(8,128)(2,1)} %get-tuple-element.26.wr_any, bf16[128,512]{1,0:T(8,128)(2,1)} %copy-done.22, bf16[128,512]{1,0:T(8,128)(2,1)} %collective-permute-done.23.refs_1_, ...), custom_call_target="tpu_custom_call" | custom-call | tf_op jit(solution)/shard_map/product_far/pallas_call | solution.py:375
  (138 shorter events, 40.5 us)
Async XLA Ops:
  6.5 17.8 %collective-permute-start.3 = (bf16[2,12,9216]{2,0,1:T(2,128)(2,1)}, bf16[2,12,9216]{2,0,1:T(2,128)(2,1)S(1)}, u32[]{:S(2)}, u32[]{:S(2)}) collective-permute-start(bf16[2,12,9216]{2,0,1:T(2,128)(2,1)} %param.14), channel_id=1, source_target_pairs={{0,64},{64,128},{128,192},{192,0},{1,65},{65,129},{129,193},{193,1... | collective-permute-start | bytes 1327112 | tf_op jit(solution)/shard_map/ppermute | solution.py:413
  8.8 17.5 %collective-permute-start.4 = (bf16[2,12,9216]{2,0,1:T(2,128)(2,1)}, bf16[2,12,9216]{2,0,1:T(2,128)(2,1)S(1)}, u32[]{:S(2)}, u32[]{:S(2)}) collective-permute-start(bf16[2,12,9216]{2,0,1:T(2,128)(2,1)} %param.14), channel_id=1, source_target_pairs={{0,192},{64,0},{128,64},{192,128},{1,193},{65,1},{129,65},{193,129... | collective-permute-start | bytes 1327112 | tf_op jit(solution)/shard_map/ppermute | solution.py:413
  8.8 12.3 %collective-permute-start = (bf16[1,12,9216]{2,1,0:T(8,128)(2,1)}, bf16[1,12,9216]{2,1,0:T(8,128)(2,1)S(1)}, u32[]{:S(2)}, u32[]{:S(2)}) collective-permute-start(bf16[1,12,9216]{2,1,0:T(8,128)(2,1)} %refs_0_.1), channel_id=1, source_target_pairs={{0,8},{8,16},{16,24},{24,32},{32,40},{40,48},{48,56},{56,0},{1,9},... | collective-permute-start | bytes 663560 | tf_op jit(solution)/shard_map/ppermute | solution.py:413
  10.5 10.6 %collective-permute-start.1 = (bf16[1,12,9216]{2,1,0:T(8,128)(2,1)}, bf16[1,12,9216]{2,1,0:T(8,128)(2,1)}, u32[]{:S(2)}, u32[]{:S(2)}) collective-permute-start(bf16[1,12,9216]{2,1,0:T(8,128)(2,1)} %refs_0_.1), channel_id=1, source_target_pairs={{0,56},{8,0},{16,8},{24,16},{32,24},{40,32},{48,40},{56,48},{1,57}... | collective-permute-start | bytes 663560 | tf_op jit(solution)/shard_map/ppermute | solution.py:413
  21.1 8.8 %collective-permute-start.2 = (bf16[1,12,9216]{2,1,0:T(8,128)(2,1)S(1)}, bf16[1,12,9216]{2,1,0:T(8,128)(2,1)S(1)}, u32[]{:S(2)}, u32[]{:S(2)}) collective-permute-start(bf16[1,12,9216]{2,1,0:T(8,128)(2,1)S(1)} %collective-permute-done.refs_1_), channel_id=1, source_target_pairs={{0,8},{8,16},{16,24},{24,32},{32,40},{40,48},{48,56},{56,0},{1,9},... | collective-permute-start | bytes 663560 | tf_op jit(solution)/shard_map/ppermute | solution.py:413
  21.1 10.2 %collective-permute-start.7 = (bf16[1,12,9216]{2,1,0:T(8,128)(2,1)}, bf16[1,12,9216]{2,1,0:T(8,128)(2,1)S(1)}, u32[]{:S(2)}, u32[]{:S(2)}) collective-permute-start(bf16[1,12,9216]{2,1,0:T(8,128)(2,1)} %collective-permute-done.1.refs_2_), channel_id=1, source_target_pairs={{0,56},{8,0},{16,8},{24,16},{32,24},{40,32},{48,40},{56,48},{1,57}... | collective-permute-start | bytes 663560 | tf_op jit(solution)/shard_map/ppermute | solution.py:413
  29.8 20.6 %collective-permute-start.10 = (bf16[1,12,9216]{2,1,0:T(8,128)(2,1)S(1)}, bf16[1,12,9216]{2,1,0:T(8,128)(2,1)S(1)}, u32[]{:S(2)}, u32[]{:S(2)}) collective-permute-start(bf16[1,12,9216]{2,1,0:T(8,128)(2,1)S(1)} %collective-permute-done.2.refs_3_), channel_id=1, source_target_pairs={{0,16},{8,24},{16,32},{24,40},{32,48},{40,56},{48,0},{56,8},{1,17}... | collective-permute-start | bytes 663560 | tf_op jit(solution)/shard_map/ppermute | solution.py:413
  29.9 20.6 %collective-permute-start.8 = (bf16[1,12,9216]{2,1,0:T(8,128)(2,1)S(1)}, bf16[1,12,9216]{2,1,0:T(8,128)(2,1)S(1)}, u32[]{:S(2)}, u32[]{:S(2)}) collective-permute-start(bf16[1,12,9216]{2,1,0:T(8,128)(2,1)S(1)} %collective-permute-done.2.refs_3_), channel_id=1, source_target_pairs={{0,8},{8,16},{16,24},{24,32},{32,40},{40,48},{48,56},{56,0},{1,9},... | collective-permute-start | bytes 663560 | tf_op jit(solution)/shard_map/ppermute | solution.py:413
  31.3 19.2 %collective-permute-start.9 = (bf16[1,12,9216]{2,1,0:T(8,128)(2,1)S(1)}, bf16[1,12,9216]{2,1,0:T(8,128)(2,1)S(1)}, u32[]{:S(2)}, u32[]{:S(2)}) collective-permute-start(bf16[1,12,9216]{2,1,0:T(8,128)(2,1)S(1)} %collective-permute-done.7.refs_0_), channel_id=1, source_target_pairs={{0,56},{8,0},{16,8},{24,16},{32,24},{40,32},{48,40},{56,48},{1,57}... | collective-permute-start | bytes 663560 | tf_op jit(solution)/shard_map/ppermute | solution.py:413
  45.2 20.8 %all-to-all-start = ((bf16[8,48,1408]{2,1,0:T(8,128)(2,1)}), bf16[8,48,1408]{2,1,0:T(8,128)(2,1)S(1)}, u32[]{:S(2)}, u32[]{:S(2)}) async-start(bf16[8,48,1408]{2,1,0:T(8,128)(2,1)} %spectra.2), calls=%async_computation | async-start | bytes 2162688 | tf_op jit(solution)/shard_map/all_to_all | solution.py:436
  66.0 19.8 %all-to-all-start.1 = ((bf16[8,48,1408]{2,1,0:T(8,128)(2,1)}), bf16[8,48,1408]{2,1,0:T(8,128)(2,1)S(1)}, u32[]{:S(2)}, u32[]{:S(2)}) async-start(bf16[8,48,1408]{2,1,0:T(8,128)(2,1)} %spectra.3), calls=%async_computation.1 | async-start | bytes 2162688 | tf_op jit(solution)/shard_map/all_to_all | solution.py:438
  69.5 74.1 %all-gather.4.cloned.1.call-start = ((), (), s32[]{:S(2)}) async-start(), calls=%async_computation.4 | async-start | bytes 1179648 | tf_op jit(solution)/shard_map/all_gather | solution.py:463
  105.6 71.1 %all-gather.6.cloned.1.call-start = ((), (), s32[]{:S(2)}) async-start(), calls=%async_computation.5 | async-start | bytes 1769472 | tf_op jit(solution)/shard_map/all_gather | solution.py:472
  130.9 9.7 %collective-permute-start.14 = (bf16[256,512]{1,0:T(8,128)(2,1)S(1)}, bf16[256,512]{1,0:T(8,128)(2,1)S(1)}, u32[]{:S(2)}, u32[]{:S(2)}) collective-permute-start(bf16[256,512]{1,0:T(8,128)(2,1)S(1)} %pad_maximum_fusion.refs_1_), channel_id=1, source_target_pairs={{0,8},{8,16},{16,24},{24,32},{32,40},{40,48},{48,56},{56,0},{1,9},... | collective-permute-start | bytes 786440 | tf_op jit(solution)/shard_map/ppermute | solution.py:413
  143.6 22.3 %collective-permute-start.20 = (bf16[512,1024]{1,0:T(8,128)(2,1)}, bf16[512,1024]{1,0:T(8,128)(2,1)S(1)}, u32[]{:S(2)}, u32[]{:S(2)}) collective-permute-start(bf16[512,1024]{1,0:T(8,128)(2,1)} %all-gather.4.cloned.1.call-done.refs_8_), channel_id=1, source_target_pairs={{0,64},{64,128},{128,192},{192,0},{1,65},{65,129},{129,193},{193,1... | collective-permute-start | bytes 3145736 | tf_op jit(solution)/shard_map/ppermute | solution.py:413
  144.3 23.8 %collective-permute-start.21 = (bf16[512,1024]{1,0:T(8,128)(2,1)}, bf16[512,1024]{1,0:T(8,128)(2,1)S(1)}, u32[]{:S(2)}, u32[]{:S(2)}) collective-permute-start(bf16[512,1024]{1,0:T(8,128)(2,1)} %all-gather.4.cloned.1.call-done.refs_8_), channel_id=1, source_target_pairs={{0,192},{64,0},{128,64},{192,128},{1,193},{65,1},{129,65},{193,129... | collective-permute-start | bytes 3145736 | tf_op jit(solution)/shard_map/ppermute | solution.py:413
  145.7 9.0 %collective-permute-start.16 = (bf16[256,512]{1,0:T(8,128)(2,1)S(1)}, bf16[256,512]{1,0:T(8,128)(2,1)S(1)}, u32[]{:S(2)}, u32[]{:S(2)}) collective-permute-start(bf16[256,512]{1,0:T(8,128)(2,1)S(1)} %collective-permute-done.14.refs_2_), channel_id=1, source_target_pairs={{0,8},{8,16},{16,24},{24,32},{32,40},{40,48},{48,56},{56,0},{1,9},... | collective-permute-start | bytes 786440 | tf_op jit(solution)/shard_map/ppermute | solution.py:413
  147.8 8.7 %collective-permute-start.18 = (bf16[256,512]{1,0:T(8,128)(2,1)S(1)}, bf16[256,512]{1,0:T(8,128)(2,1)S(1)}, u32[]{:S(2)}, u32[]{:S(2)}) collective-permute-start(bf16[256,512]{1,0:T(8,128)(2,1)S(1)} %collective-permute-done.15.refs_5_), channel_id=1, source_target_pairs={{0,56},{8,0},{16,8},{24,16},{32,24},{40,32},{48,40},{56,48},{1,57}... | collective-permute-start | bytes 786440 | tf_op jit(solution)/shard_map/ppermute | solution.py:413
  154.6 15.4 %collective-permute-start.17 = (bf16[256,512]{1,0:T(8,128)(2,1)S(1)}, bf16[256,512]{1,0:T(8,128)(2,1)S(1)}, u32[]{:S(2)}, u32[]{:S(2)}) collective-permute-start(bf16[256,512]{1,0:T(8,128)(2,1)S(1)} %collective-permute-done.16.refs_3_), channel_id=1, source_target_pairs={{0,8},{8,16},{16,24},{24,32},{32,40},{40,48},{48,56},{56,0},{1,9},... | collective-permute-start | bytes 786440 | tf_op jit(solution)/shard_map/ppermute | solution.py:413
  156.5 16.5 %collective-permute-start.19 = (bf16[256,512]{1,0:T(8,128)(2,1)S(1)}, bf16[256,512]{1,0:T(8,128)(2,1)S(1)}, u32[]{:S(2)}, u32[]{:S(2)}) collective-permute-start(bf16[256,512]{1,0:T(8,128)(2,1)S(1)} %collective-permute-done.18.refs_6_), channel_id=1, source_target_pairs={{0,56},{8,0},{16,8},{24,16},{32,24},{40,32},{48,40},{56,48},{1,57}... | collective-permute-start | bytes 786440 | tf_op jit(solution)/shard_map/ppermute | solution.py:413
  166.9 17.3 %collective-permute-start.24 = (bf16[256,1024]{1,0:T(8,128)(2,1)}, bf16[256,1024]{1,0:T(8,128)(2,1)S(1)}, u32[]{:S(2)}, u32[]{:S(2)}) collective-permute-start(bf16[256,1024]{1,0:T(8,128)(2,1)} %slice.38), channel_id=1, source_target_pairs={{0,64},{64,128},{128,192},{192,0},{1,65},{65,129},{129,193},{193,1... | collective-permute-start | bytes 1572872 | tf_op jit(solution)/shard_map/ppermute | solution.py:413
  168.9 15.3 %collective-permute-start.25 = (bf16[256,1024]{1,0:T(8,128)(2,1)}, bf16[256,1024]{1,0:T(8,128)(2,1)}, u32[]{:S(2)}, u32[]{:S(2)}) collective-permute-start(bf16[256,1024]{1,0:T(8,128)(2,1)} %slice.39), channel_id=1, source_target_pairs={{0,192},{64,0},{128,64},{192,128},{1,193},{65,1},{129,65},{193,129... | collective-permute-start | bytes 1572872 | tf_op jit(solution)/shard_map/ppermute | solution.py:413
  170.8 13.4 %collective-permute-start.22 = (bf16[128,512]{1,0:T(8,128)(2,1)}, bf16[128,512]{1,0:T(8,128)(2,1)S(1)}, u32[]{:S(2)}, u32[]{:S(2)}) collective-permute-start(bf16[128,512]{1,0:T(8,128)(2,1)} %slice.36), channel_id=1, source_target_pairs={{0,8},{8,16},{16,24},{24,32},{32,40},{40,48},{48,56},{56,0},{1,9},... | collective-permute-start | bytes 393224 | tf_op jit(solution)/shard_map/ppermute | solution.py:413
  173.8 10.4 %collective-permute-start.23 = (bf16[128,512]{1,0:T(8,128)(2,1)}, bf16[128,512]{1,0:T(8,128)(2,1)}, u32[]{:S(2)}, u32[]{:S(2)}) collective-permute-start(bf16[128,512]{1,0:T(8,128)(2,1)} %slice.37), channel_id=1, source_target_pairs={{0,56},{8,0},{16,8},{24,16},{32,24},{40,32},{48,40},{56,48},{1,57}... | collective-permute-start | bytes 393224 | tf_op jit(solution)/shard_map/ppermute | solution.py:413
  (37 other events, 722.1 us)
Sparse Core Ops, SparseCore 0:
  105.7 37.8 all-gather.3
  145.5 26.1 all-gather.5

commit v8 on v7

--- a/solution.py
+++ b/solution.py
@@ -433,10 +433,6 @@
         vs[VB - m] = shift(vs[(VB - m + 1) % VB], "z", NZ, -1)
     vs[VB // 2] = shift(vs[2], "z", NZ, 2)
     specs = [spectra([vs[k] for k in slots], cs, depth, plane) for slots in SLOTS]
-    slabs = [lax.all_to_all(specs[0], tile, split_axis=0, concat_axis=0, tiled=True)]
-    slabs[0], specs[1] = lax.optimization_barrier((slabs[0], specs[1]))
-    slabs.append(lax.all_to_all(specs[1], tile, split_axis=0, concat_axis=0, tiled=True))
-
     valence_level = pick_levels(valence_pick, valence_energy)
     band_level = pick_levels(cond_pick, conduction_energy)
     slot_codes = jnp.arange(NC, dtype=jnp.int32)
@@ -456,6 +452,10 @@
     b_code = (rest % HALF) * KEPT + rest // HALF
     a_code = a_code + AEI * (b_code // CODES)
     b_code = b_code % CODES
+
+    slabs = [lax.all_to_all(specs[0], tile, split_axis=0, concat_axis=0, tiled=True)]
+    slabs[0], specs[1], weight = lax.optimization_barrier((slabs[0], specs[1], weight))
+    slabs.append(lax.all_to_all(specs[1], tile, split_axis=0, concat_axis=0, tiled=True))
 
     first = pick_first(lines(slabs[0].reshape(GRID * QC, YL), kron), a_code, b_code)
     cols, for_rows = pick_second(lines(slabs[1].reshape(GRID * QC, YL), kron), a_code, b_code, first)

time: 200 us -> 229 us (1.15)
  waiting for transfers between devices: 47.3 us -> 73.6 us
  starting transfers between devices: 44.9 us -> 47.7 us
    ppermute x26, waiting for transfers between devices: 34.6 us -> 64.6 us  [shift(): lax.ppermute(value, axis, [(i, (i + step) % size) for i in range(size)])]
    all_to_all x1, waiting for transfers between devices: 3.92 us -> 0.01 us  [per_device(): lax.all_to_all(specs[0], tile, split_axis=0, concat_axis=0, tiled=True)]
  transfers between devices with their start and end apart: 30 -> 30, of which waited for: 13 -> 15; matrix products, arithmetic and copies ran while one was open for 4% -> 4% of each run, Pallas kernels for 19% -> 12%
where the time goes in v8:
time: 229 us; the launch traced here: 227 us
  waiting for transfers between devices  73.6 us (32%)
  Pallas kernels  52.8 us (23%)
  starting transfers between devices  47.7 us (21%)
  blocking collectives  27.1 us (12%)
  between operations  13.9 us (6%)
  local copies, waits for them, and re-layouts  9.6 us (4%)
  other arithmetic  2.39 us (1%)
    ppermute x26, waiting for transfers between devices, shift(): lax.ppermute(value, axis, [(i, (i + step) % size) for i in range(size)])  64.6 us
    ppermute x26, starting transfers between devices, shift(): lax.ppermute(value, axis, [(i, (i + step) % size) for i in range(size)])  38.4 us
    pallas_call x2, Pallas kernels, spectra(): pl.pallas_call(spectra_kernel, in_specs=[pl.BlockSpec(memory_space=pl.ANY...  20.1 us
    all_to_all x1, blocking collectives, per_device(): lax.all_to_all(for_rows, ('x', 'z'), split_axis=0, concat_axis=0, tiled=T...  17.9 us
    all_to_all x1, blocking collectives, per_device(): lax.all_to_all(cols, tile, split_axis=0, concat_axis=0, tiled=True)  9.23 us
    pallas_call x1, Pallas kernels, pick_second(): pl.pallas_call(second_kernel, grid=(GP // GCH,), in_specs=pick_specs() +...  8.99 us
    pallas_call x1, Pallas kernels, pick_first(): pl.pallas_call(first_kernel, grid=(GP // GCH,), in_specs=pick_specs(), ou...  8.96 us
    pallas_call x1, Pallas kernels, product_near(): pl.pallas_call(near_kernel, in_specs=[pl.BlockSpec(memory_space=pltpu.SME...  7.46 us
  transfers between devices with their start and end apart: 30, of which 15 were waited for; matrix products, arithmetic and copies ran while one was open for 4% of the time, Pallas kernels for 12%

profile of v8, /device:TPU:6, one launch (start us, length us, event | category | flops | bytes accessed | tf_op | source)
XLA Modules:
  0.0 227.2 jit_solution(9793406428129351817)
XLA Ops:
  10.5 3.9 %collective-permute-start.1 = (bf16[1,12,9216]{2,1,0:T(8,128)(2,1)}, bf16[1,12,9216]{2,1,0:T(8,128)(2,1)S(1)}, u32[]{:S(2)}, u32[]{:S(2)}) collective-permute-start(bf16[1,12,9216]{2,1,0:T(8,128)(2,1)} %refs_0_.1), channel_id=1, source_target_pairs={{0,56},{8,0},{16,8},{24,16},{32,24},{40,32},{48,40},{56,48},{1,57}... | collective-permute-start | bytes 663560 | tf_op jit(solution)/shard_map/ppermute | solution.py:413
  14.4 6.7 %collective-permute-done.refs_1_ = bf16[1,12,9216]{2,1,0:T(8,128)(2,1)S(1)} collective-permute-done((bf16[1,12,9216]{2,1,0:T(8,128)(2,1)}, bf16[1,12,9216]{2,1,0:T(8,128)(2,1)S(1)}, u32[]{:S(2)}, u32[]{:S(2)}) %collective-permute-start) | collective-permute-done | bytes 221216 | tf_op jit(solution)/shard_map/ppermute | solution.py:413
  24.7 5.1 %collective-permute-done.2.refs_3_ = bf16[1,12,9216]{2,1,0:T(8,128)(2,1)S(1)} collective-permute-done((bf16[1,12,9216]{2,1,0:T(8,128)(2,1)S(1)}, bf16[1,12,9216]{2,1,0:T(8,128)(2,1)S(1)}, u32[]{:S(2)}, u32[]{:S(2)}) %collective-permute-start.2) | collective-permute-done | bytes 221216 | tf_op jit(solution)/shard_map/ppermute | solution.py:413
  32.4 10.1 %spectra.2 = bf16[8,48,1408]{2,1,0:T(8,128)(2,1)} custom-call(bf16[1,12,9216]{2,1,0:T(8,128)(2,1)} %refs_0_.1, bf16[1,12,9216]{2,1,0:T(8,128)(2,1)} %copy-done.16, bf16[1,12,9216]{2,1,0:T(8,128)(2,1)} %copy-done.14, bf16[1,12,9216]{2,1,0:T(8,128)(2,1)} %copy-done.12, bf16[2,12,9216]{2,1,0:T(8,128)(2,1)} %copy.34.refs_4_, bf16[2,12,9216]{2,1,0:T(8,128)(2,1)} %copy-done.1, ...), custom_call_target="tpu_custom_call" | custom-call | tf_op jit(solution)/shard_map/spectra/pallas_call | solution.py:169
  42.6 4.6 %all-to-all-start = ((bf16[8,48,1408]{2,1,0:T(8,128)(2,1)}), bf16[8,48,1408]{2,1,0:T(8,128)(2,1)S(1)}, u32[]{:S(2)}, u32[]{:S(2)}) async-start(bf16[8,48,1408]{2,1,0:T(8,128)(2,1)} %spectra.2), calls=%async_computation | async-start | bytes 2162688 | tf_op jit(solution)/shard_map/all_to_all | solution.py:456
  48.5 3.8 %collective-permute-start.7 = (bf16[1,12,9216]{2,1,0:T(8,128)(2,1)S(1)}, bf16[1,12,9216]{2,1,0:T(8,128)(2,1)S(1)}, u32[]{:S(2)}, u32[]{:S(2)}) collective-permute-start(bf16[1,12,9216]{2,1,0:T(8,128)(2,1)S(1)} %copy-done.15), channel_id=1, source_target_pairs={{0,56},{8,0},{16,8},{24,16},{32,24},{40,32},{48,40},{56,48},{1,57}... | collective-permute-start | bytes 663560 | tf_op jit(solution)/shard_map/ppermute | solution.py:413
  53.8 5.4 %collective-permute-done.7.refs_0_ = bf16[1,12,9216]{2,1,0:T(8,128)(2,1)S(1)} collective-permute-done((bf16[1,12,9216]{2,1,0:T(8,128)(2,1)S(1)}, bf16[1,12,9216]{2,1,0:T(8,128)(2,1)S(1)}, u32[]{:S(2)}, u32[]{:S(2)}) %collective-permute-start.7) | collective-permute-done | bytes 221216 | tf_op jit(solution)/shard_map/ppermute | solution.py:413
  59.3 3.7 %collective-permute-start.9 = (bf16[1,12,9216]{2,1,0:T(8,128)(2,1)S(1)}, bf16[1,12,9216]{2,1,0:T(8,128)(2,1)S(1)}, u32[]{:S(2)}, u32[]{:S(2)}) collective-permute-start(bf16[1,12,9216]{2,1,0:T(8,128)(2,1)S(1)} %collective-permute-done.7.refs_0_), channel_id=1, source_target_pairs={{0,56},{8,0},{16,8},{24,16},{32,24},{40,32},{48,40},{56,48},{1,57}... | collective-permute-start | bytes 663560 | tf_op jit(solution)/shard_map/ppermute | solution.py:413
  63.0 7.5 %collective-permute-done.10.refs_3_ = bf16[1,12,9216]{2,1,0:T(8,128)(2,1)S(1)} collective-permute-done((bf16[1,12,9216]{2,1,0:T(8,128)(2,1)S(1)}, bf16[1,12,9216]{2,1,0:T(8,128)(2,1)S(1)}, u32[]{:S(2)}, u32[]{:S(2)}) %collective-permute-start.10) | collective-permute-done | bytes 221216 | tf_op jit(solution)/shard_map/ppermute | solution.py:413
  70.5 3.3 %collective-permute-done.8.refs_1_ = bf16[1,12,9216]{2,1,0:T(8,128)(2,1)S(1)} collective-permute-done((bf16[1,12,9216]{2,1,0:T(8,128)(2,1)S(1)}, bf16[1,12,9216]{2,1,0:T(8,128)(2,1)S(1)}, u32[]{:S(2)}, u32[]{:S(2)}) %collective-permute-start.8) | collective-permute-done | bytes 221216 | tf_op jit(solution)/shard_map/ppermute | solution.py:413
  75.3 10.0 %spectra.3 = bf16[8,48,1408]{2,1,0:T(8,128)(2,1)} custom-call(bf16[1,12,9216]{2,1,0:T(8,128)(2,1)} %copy-done.17, bf16[1,12,9216]{2,1,0:T(8,128)(2,1)} %copy-done.19, bf16[1,12,9216]{2,1,0:T(8,128)(2,1)} %copy-done.20, bf16[1,12,9216]{2,1,0:T(8,128)(2,1)} %copy-done.18, bf16[2,12,9216]{2,1,0:T(8,128)(2,1)} %copy.34.refs_4_, bf16[2,12,9216]{2,1,0:T(8,128)(2,1)} %copy-done.1, ...), custom_call_target="tpu_custom_call" | custom-call | tf_op jit(solution)/shard_map/spectra/pallas_call | solution.py:169
  85.3 4.6 %all-to-all-start.1 = ((bf16[8,48,1408]{2,1,0:T(8,128)(2,1)}), bf16[8,48,1408]{2,1,0:T(8,128)(2,1)S(1)}, u32[]{:S(2)}, u32[]{:S(2)}) async-start(bf16[8,48,1408]{2,1,0:T(8,128)(2,1)} %spectra.3), calls=%async_computation.1 | async-start | bytes 2162688 | tf_op jit(solution)/shard_map/all_to_all | solution.py:458
  91.1 9.0 %pick_first.1.first_ref = f32[8,12288]{1,0:T(8,128)S(1)} custom-call(bf16[888,256]{1,0:T(8,128)(2,1)S(1)} %lines.3.s_ref, s32[1,12288]{1,0:T(1,128)S(1)} %multiply_add_fusion.a_ref, s32[1,12288]{1,0:T(1,128)S(1)} %get-tuple-element.29.b_ref), custom_call_target="tpu_custom_call" | custom-call | tf_op jit(solution)/shard_map/pick_first/pallas_call | solution.py:247
  100.1 6.1 %all-to-all-done.1 = bf16[8,48,1408]{2,1,0:T(8,128)(2,1)S(1)} async-done(((bf16[8,48,1408]{2,1,0:T(8,128)(2,1)}), bf16[8,48,1408]{2,1,0:T(8,128)(2,1)S(1)}, u32[]{:S(2)}, u32[]{:S(2)}) %all-to-all-start.1) | async-done | bytes 1081376 | tf_op jit(solution)/shard_map/all_to_all | solution.py:458
  107.0 9.0 %pick_second.1 = (bf16[8,8,1536]{2,1,0:T(8,128)(2,1)S(1)}, bf16[32,8,384]{2,1,0:T(8,128)(2,1)S(1)}) custom-call(bf16[888,256]{1,0:T(8,128)(2,1)S(1)} %lines.2.s_ref, s32[1,12288]{1,0:T(1,128)S(1)} %multiply_add_fusion.a_ref, s32[1,12288]{1,0:T(1,128)S(1)} %get-tuple-element.29.b_ref, f32[8,12288]{1,0:T(8,128)S(1)} %pick_first.1.first_ref), custom_call_target="tpu_custom_call" | custom-call | tf_op jit(solution)/shard_map/pick_second/pallas_call | solution.py:260
  116.0 9.2 %all_to_all.20 = bf16[8,8,1536]{2,1,0:T(8,128)(2,1)S(1)} all-to-all(bf16[8,8,1536]{2,1,0:T(8,128)(2,1)S(1)} %get-tuple-element.21), channel_id=1, replica_groups=mesh['x'=4,'z'=8,'y'=4,'core'=2] {'y','core'}, dimensions={0} | all-to-all | bytes 393216 | tf_op jit(solution)/shard_map/all_to_all | solution.py:462
  133.9 17.9 %all_to_all.21 = bf16[32,8,384]{2,1,0:T(8,128)(2,1)} all-to-all(bf16[32,8,384]{2,1,0:T(8,128)(2,1)S(1)} %get-tuple-element.22), channel_id=1, replica_groups=mesh['x'=4,'z'=8,'y'=4,'core'=2] {'x','z'}, dimensions={0} | all-to-all | bytes 393216 | tf_op jit(solution)/shard_map/all_to_all | solution.py:471
  155.1 6.3 %collective-permute-done.14.refs_2_ = bf16[256,512]{1,0:T(8,128)(2,1)S(1)} collective-permute-done((bf16[256,512]{1,0:T(8,128)(2,1)S(1)}, bf16[256,512]{1,0:T(8,128)(2,1)S(1)}, u32[]{:S(2)}, u32[]{:S(2)}) %collective-permute-start.14) | collective-permute-done | bytes 262176 | tf_op jit(solution)/shard_map/ppermute | solution.py:413
  161.6 2.9 %all-gather.4.cloned.1.call-done.refs_8_ = bf16[512,1024]{1,0:T(8,128)(2,1)} async-done(((bf16[64,1024]{1,0:T(8,128)(2,1)}), bf16[512,1024]{1,0:T(8,128)(2,1)}) %all-gather.4.cloned.1.call-update) | async-done | bytes 1048592 | tf_op jit(solution)/shard_map/all_gather | solution.py:463
  169.7 17.1 %collective-permute-done.20.refs_9_ = bf16[512,1024]{1,0:T(8,128)(2,1)S(1)} collective-permute-done((bf16[512,1024]{1,0:T(8,128)(2,1)}, bf16[512,1024]{1,0:T(8,128)(2,1)S(1)}, u32[]{:S(2)}, u32[]{:S(2)}) %collective-permute-start.20) | collective-permute-done | bytes 1048608 | tf_op jit(solution)/shard_map/ppermute | solution.py:413
  194.0 5.6 %collective-permute-done.17.refs_4_ = bf16[256,512]{1,0:T(8,128)(2,1)S(1)} collective-permute-done((bf16[256,512]{1,0:T(8,128)(2,1)S(1)}, bf16[256,512]{1,0:T(8,128)(2,1)S(1)}, u32[]{:S(2)}, u32[]{:S(2)}) %collective-permute-start.17) | collective-permute-done | bytes 262176 | tf_op jit(solution)/shard_map/ppermute | solution.py:413
  201.5 2.7 %collective-permute-start.23 = (bf16[128,512]{1,0:T(8,128)(2,1)}, bf16[128,512]{1,0:T(8,128)(2,1)}, u32[]{:S(2)}, u32[]{:S(2)}) collective-permute-start(bf16[128,512]{1,0:T(8,128)(2,1)} %slice.37), channel_id=1, source_target_pairs={{0,56},{8,0},{16,8},{24,16},{32,24},{40,32},{48,40},{56,48},{1,57}... | collective-permute-start | bytes 393224 | tf_op jit(solution)/shard_map/ppermute | solution.py:413
  206.3 7.5 %product_near.1 = (f32[384,1536]{1,0:T(8,128)}, bf16[32,64,384]{2,1,0:T(8,128)(2,1)}) custom-call(s32[2]{0:T(128)} %pad_add_fusion.xz_ref, f32[2048,1]{1,0:T(8,128)} %copy.40.w_ref, bf16[8,32,8,384]{3,2,1,0:T(8,128)(2,1)} %bitcast.21, bf16[256,512]{1,0:T(8,128)(2,1)} %copy-done.7, bf16[256,512]{1,0:T(8,128)(2,1)} %copy-done.21, bf16[256,512]{1,0:T(8,128)(2,1)} %copy-done.23, ...), custom_call_target="tpu_custom_call" | custom-call | tf_op jit(solution)/shard_map/product_near/pallas_call | solution.py:335
  214.6 5.7 %product_far.1 = f32[375,1500]{1,0:T(8,128)} custom-call(s32[2]{0:T(128)} %pad_add_fusion.xz_ref, f32[384,1536]{1,0:T(8,128)} %get-tuple-element.27.acc_any, bf16[32,64,384]{2,1,0:T(8,128)(2,1)} %get-tuple-element.28.wr_any, bf16[128,512]{1,0:T(8,128)(2,1)} %copy-done.25, bf16[128,512]{1,0:T(8,128)(2,1)} %collective-permute-done.23.refs_1_, ...), custom_call_target="tpu_custom_call" | custom-call | tf_op jit(solution)/shard_map/product_far/pallas_call | solution.py:375
  (144 shorter events, 45.5 us)
Async XLA Ops:
  6.5 14.5 %collective-permute-start.3 = (bf16[2,12,9216]{2,0,1:T(2,128)(2,1)}, bf16[2,12,9216]{2,0,1:T(2,128)(2,1)S(1)}, u32[]{:S(2)}, u32[]{:S(2)}) collective-permute-start(bf16[2,12,9216]{2,0,1:T(2,128)(2,1)} %param.14), channel_id=1, source_target_pairs={{0,64},{64,128},{128,192},{192,0},{1,65},{65,129},{129,193},{193,1... | collective-permute-start | bytes 1327112 | tf_op jit(solution)/shard_map/ppermute | solution.py:413
  8.8 14.2 %collective-permute-start.4 = (bf16[2,12,9216]{2,0,1:T(2,128)(2,1)}, bf16[2,12,9216]{2,0,1:T(2,128)(2,1)S(1)}, u32[]{:S(2)}, u32[]{:S(2)}) collective-permute-start(bf16[2,12,9216]{2,0,1:T(2,128)(2,1)} %param.14), channel_id=1, source_target_pairs={{0,192},{64,0},{128,64},{192,128},{1,193},{65,1},{129,65},{193,129... | collective-permute-start | bytes 1327112 | tf_op jit(solution)/shard_map/ppermute | solution.py:413
  8.8 12.3 %collective-permute-start = (bf16[1,12,9216]{2,1,0:T(8,128)(2,1)}, bf16[1,12,9216]{2,1,0:T(8,128)(2,1)S(1)}, u32[]{:S(2)}, u32[]{:S(2)}) collective-permute-start(bf16[1,12,9216]{2,1,0:T(8,128)(2,1)} %refs_0_.1), channel_id=1, source_target_pairs={{0,8},{8,16},{16,24},{24,32},{32,40},{40,48},{48,56},{56,0},{1,9},... | collective-permute-start | bytes 663560 | tf_op jit(solution)/shard_map/ppermute | solution.py:413
  10.5 14.2 %collective-permute-start.1 = (bf16[1,12,9216]{2,1,0:T(8,128)(2,1)}, bf16[1,12,9216]{2,1,0:T(8,128)(2,1)S(1)}, u32[]{:S(2)}, u32[]{:S(2)}) collective-permute-start(bf16[1,12,9216]{2,1,0:T(8,128)(2,1)} %refs_0_.1), channel_id=1, source_target_pairs={{0,56},{8,0},{16,8},{24,16},{32,24},{40,32},{48,40},{56,48},{1,57}... | collective-permute-start | bytes 663560 | tf_op jit(solution)/shard_map/ppermute | solution.py:413
  21.1 8.8 %collective-permute-start.2 = (bf16[1,12,9216]{2,1,0:T(8,128)(2,1)S(1)}, bf16[1,12,9216]{2,1,0:T(8,128)(2,1)S(1)}, u32[]{:S(2)}, u32[]{:S(2)}) collective-permute-start(bf16[1,12,9216]{2,1,0:T(8,128)(2,1)S(1)} %collective-permute-done.refs_1_), channel_id=1, source_target_pairs={{0,8},{8,16},{16,24},{24,32},{32,40},{40,48},{48,56},{56,0},{1,9},... | collective-permute-start | bytes 663560 | tf_op jit(solution)/shard_map/ppermute | solution.py:413
  21.2 8.6 %collective-permute-start.5 = (bf16[1,12,9216]{2,1,0:T(8,128)(2,1)S(1)}, bf16[1,12,9216]{2,1,0:T(8,128)(2,1)S(1)}, u32[]{:S(2)}, u32[]{:S(2)}) collective-permute-start(bf16[1,12,9216]{2,1,0:T(8,128)(2,1)S(1)} %slice.32), channel_id=1, source_target_pairs={{0,64},{64,128},{128,192},{192,0},{1,65},{65,129},{129,193},{193,1... | collective-permute-start | bytes 663560 | tf_op jit(solution)/shard_map/ppermute | solution.py:413
  42.6 42.7 %all-to-all-start = ((bf16[8,48,1408]{2,1,0:T(8,128)(2,1)}), bf16[8,48,1408]{2,1,0:T(8,128)(2,1)S(1)}, u32[]{:S(2)}, u32[]{:S(2)}) async-start(bf16[8,48,1408]{2,1,0:T(8,128)(2,1)} %spectra.2), calls=%async_computation | async-start | bytes 2162688 | tf_op jit(solution)/shard_map/all_to_all | solution.py:456
  48.5 10.7 %collective-permute-start.7 = (bf16[1,12,9216]{2,1,0:T(8,128)(2,1)S(1)}, bf16[1,12,9216]{2,1,0:T(8,128)(2,1)S(1)}, u32[]{:S(2)}, u32[]{:S(2)}) collective-permute-start(bf16[1,12,9216]{2,1,0:T(8,128)(2,1)S(1)} %copy-done.15), channel_id=1, source_target_pairs={{0,56},{8,0},{16,8},{24,16},{32,24},{40,32},{48,40},{56,48},{1,57}... | collective-permute-start | bytes 663560 | tf_op jit(solution)/shard_map/ppermute | solution.py:413
  52.6 17.9 %collective-permute-start.10 = (bf16[1,12,9216]{2,1,0:T(8,128)(2,1)S(1)}, bf16[1,12,9216]{2,1,0:T(8,128)(2,1)S(1)}, u32[]{:S(2)}, u32[]{:S(2)}) collective-permute-start(bf16[1,12,9216]{2,1,0:T(8,128)(2,1)S(1)} %copy-done.13), channel_id=1, source_target_pairs={{0,16},{8,24},{16,32},{24,40},{32,48},{40,56},{48,0},{56,8},{1,17}... | collective-permute-start | bytes 663560 | tf_op jit(solution)/shard_map/ppermute | solution.py:413
  52.7 21.1 %collective-permute-start.8 = (bf16[1,12,9216]{2,1,0:T(8,128)(2,1)S(1)}, bf16[1,12,9216]{2,1,0:T(8,128)(2,1)S(1)}, u32[]{:S(2)}, u32[]{:S(2)}) collective-permute-start(bf16[1,12,9216]{2,1,0:T(8,128)(2,1)S(1)} %copy-done.13), channel_id=1, source_target_pairs={{0,8},{8,16},{16,24},{24,32},{32,40},{40,48},{48,56},{56,0},{1,9},... | collective-permute-start | bytes 663560 | tf_op jit(solution)/shard_map/ppermute | solution.py:413
  59.3 14.6 %collective-permute-start.9 = (bf16[1,12,9216]{2,1,0:T(8,128)(2,1)S(1)}, bf16[1,12,9216]{2,1,0:T(8,128)(2,1)S(1)}, u32[]{:S(2)}, u32[]{:S(2)}) collective-permute-start(bf16[1,12,9216]{2,1,0:T(8,128)(2,1)S(1)} %collective-permute-done.7.refs_0_), channel_id=1, source_target_pairs={{0,56},{8,0},{16,8},{24,16},{32,24},{40,32},{48,40},{56,48},{1,57}... | collective-permute-start | bytes 663560 | tf_op jit(solution)/shard_map/ppermute | solution.py:413
  85.3 20.9 %all-to-all-start.1 = ((bf16[8,48,1408]{2,1,0:T(8,128)(2,1)}), bf16[8,48,1408]{2,1,0:T(8,128)(2,1)S(1)}, u32[]{:S(2)}, u32[]{:S(2)}) async-start(bf16[8,48,1408]{2,1,0:T(8,128)(2,1)} %spectra.3), calls=%async_computation.1 | async-start | bytes 2162688 | tf_op jit(solution)/shard_map/all_to_all | solution.py:458
  89.9 74.6 %all-gather.4.cloned.1.call-start = ((), (), s32[]{:S(2)}) async-start(), calls=%async_computation.4 | async-start | bytes 1179648 | tf_op jit(solution)/shard_map/all_gather | solution.py:463
  125.9 80.3 %all-gather.6.cloned.1.call-start = ((), (), s32[]{:S(2)}) async-start(), calls=%async_computation.5 | async-start | bytes 1769472 | tf_op jit(solution)/shard_map/all_gather | solution.py:472
  151.8 9.6 %collective-permute-start.14 = (bf16[256,512]{1,0:T(8,128)(2,1)S(1)}, bf16[256,512]{1,0:T(8,128)(2,1)S(1)}, u32[]{:S(2)}, u32[]{:S(2)}) collective-permute-start(bf16[256,512]{1,0:T(8,128)(2,1)S(1)} %pad_maximum_fusion.refs_1_), channel_id=1, source_target_pairs={{0,8},{8,16},{16,24},{24,32},{32,40},{40,48},{48,56},{56,0},{1,9},... | collective-permute-start | bytes 786440 | tf_op jit(solution)/shard_map/ppermute | solution.py:413
  164.5 22.3 %collective-permute-start.20 = (bf16[512,1024]{1,0:T(8,128)(2,1)}, bf16[512,1024]{1,0:T(8,128)(2,1)S(1)}, u32[]{:S(2)}, u32[]{:S(2)}) collective-permute-start(bf16[512,1024]{1,0:T(8,128)(2,1)} %all-gather.4.cloned.1.call-done.refs_8_), channel_id=1, source_target_pairs={{0,64},{64,128},{128,192},{192,0},{1,65},{65,129},{129,193},{193,1... | collective-permute-start | bytes 3145736 | tf_op jit(solution)/shard_map/ppermute | solution.py:413
  164.8 24.2 %collective-permute-start.21 = (bf16[512,1024]{1,0:T(8,128)(2,1)}, bf16[512,1024]{1,0:T(8,128)(2,1)S(1)}, u32[]{:S(2)}, u32[]{:S(2)}) collective-permute-start(bf16[512,1024]{1,0:T(8,128)(2,1)} %all-gather.4.cloned.1.call-done.refs_8_), channel_id=1, source_target_pairs={{0,192},{64,0},{128,64},{192,128},{1,193},{65,1},{129,65},{193,129... | collective-permute-start | bytes 3145736 | tf_op jit(solution)/shard_map/ppermute | solution.py:413
  166.5 24.1 %collective-permute-start.16 = (bf16[256,512]{1,0:T(8,128)(2,1)S(1)}, bf16[256,512]{1,0:T(8,128)(2,1)S(1)}, u32[]{:S(2)}, u32[]{:S(2)}) collective-permute-start(bf16[256,512]{1,0:T(8,128)(2,1)S(1)} %collective-permute-done.14.refs_2_), channel_id=1, source_target_pairs={{0,8},{8,16},{16,24},{24,32},{32,40},{40,48},{48,56},{56,0},{1,9},... | collective-permute-start | bytes 786440 | tf_op jit(solution)/shard_map/ppermute | solution.py:413
  168.3 24.3 %collective-permute-start.18 = (bf16[256,512]{1,0:T(8,128)(2,1)S(1)}, bf16[256,512]{1,0:T(8,128)(2,1)S(1)}, u32[]{:S(2)}, u32[]{:S(2)}) collective-permute-start(bf16[256,512]{1,0:T(8,128)(2,1)S(1)} %collective-permute-done.15.refs_5_), channel_id=1, source_target_pairs={{0,56},{8,0},{16,8},{24,16},{32,24},{40,32},{48,40},{56,48},{1,57}... | collective-permute-start | bytes 786440 | tf_op jit(solution)/shard_map/ppermute | solution.py:413
  187.7 26.1 %collective-permute-start.24 = (bf16[256,1024]{1,0:T(8,128)(2,1)}, bf16[256,1024]{1,0:T(8,128)(2,1)S(1)}, u32[]{:S(2)}, u32[]{:S(2)}) collective-permute-start(bf16[256,1024]{1,0:T(8,128)(2,1)} %slice.38), channel_id=1, source_target_pairs={{0,64},{64,128},{128,192},{192,0},{1,65},{65,129},{129,193},{193,1... | collective-permute-start | bytes 1572872 | tf_op jit(solution)/shard_map/ppermute | solution.py:413
  189.8 23.9 %collective-permute-start.25 = (bf16[256,1024]{1,0:T(8,128)(2,1)}, bf16[256,1024]{1,0:T(8,128)(2,1)}, u32[]{:S(2)}, u32[]{:S(2)}) collective-permute-start(bf16[256,1024]{1,0:T(8,128)(2,1)} %slice.39), channel_id=1, source_target_pairs={{0,192},{64,0},{128,64},{192,128},{1,193},{65,1},{129,65},{193,129... | collective-permute-start | bytes 1572872 | tf_op jit(solution)/shard_map/ppermute | solution.py:413
  190.6 9.0 %collective-permute-start.17 = (bf16[256,512]{1,0:T(8,128)(2,1)S(1)}, bf16[256,512]{1,0:T(8,128)(2,1)S(1)}, u32[]{:S(2)}, u32[]{:S(2)}) collective-permute-start(bf16[256,512]{1,0:T(8,128)(2,1)S(1)} %collective-permute-done.16.refs_3_), channel_id=1, source_target_pairs={{0,8},{8,16},{16,24},{24,32},{32,40},{40,48},{48,56},{56,0},{1,9},... | collective-permute-start | bytes 786440 | tf_op jit(solution)/shard_map/ppermute | solution.py:413
  200.3 13.4 %collective-permute-start.22 = (bf16[128,512]{1,0:T(8,128)(2,1)}, bf16[128,512]{1,0:T(8,128)(2,1)S(1)}, u32[]{:S(2)}, u32[]{:S(2)}) collective-permute-start(bf16[128,512]{1,0:T(8,128)(2,1)} %slice.36), channel_id=1, source_target_pairs={{0,8},{8,16},{16,24},{24,32},{32,40},{40,48},{48,56},{56,0},{1,9},... | collective-permute-start | bytes 393224 | tf_op jit(solution)/shard_map/ppermute | solution.py:413
  201.5 12.2 %collective-permute-start.23 = (bf16[128,512]{1,0:T(8,128)(2,1)}, bf16[128,512]{1,0:T(8,128)(2,1)}, u32[]{:S(2)}, u32[]{:S(2)}) collective-permute-start(bf16[128,512]{1,0:T(8,128)(2,1)} %slice.37), channel_id=1, source_target_pairs={{0,56},{8,0},{16,8},{24,16},{32,24},{40,32},{48,40},{56,48},{1,57}... | collective-permute-start | bytes 393224 | tf_op jit(solution)/shard_map/ppermute | solution.py:413
  (40 other events, 377.9 us)
Sparse Core Ops, SparseCore 0:
  126.1 38.3 all-gather.3
  166.3 26.0 all-gather.5
